TPU v7x, 256 devices: a whole 4x4x8 slice. The times are simulated.
256 devices in a mesh: tm: 8 (over z), traj: 32 (over y, x, core).
Axes of the slice: x: 4, y: 4, z: 8, core: 2. Of those that a mesh axis runs over, the one named last changes fastest.
Arguments:
- states: bfloat16 [32, 2048, 1024], P('traj', 'tm'), may hold values from -6 to 6
- episode_end: int32 [32, 2048], P('traj', 'tm'), may hold values 0 or 1
- feature_head: bfloat16 [1024, 128], replicated, may hold values from -0.1875 to 0.1875
- successor_head: bfloat16 [1024, 2048], replicated, may hold values from -0.1875 to 0.1875
- horizon_gap: float32 [16], replicated, may hold values from 1e-05 to 0.01
- trace_gap: float32 [16], replicated, may hold values from 1e-05 to 0.03
Outputs:
- returns: bfloat16 [32, 2048, 2048], P('traj', 'tm')
- head_grad: float32 [1024, 2048], P('traj', 'tm')
All inputs are finite; a program needn't handle non-finite values. No bound on the sum of `episode_end` on one device may be relied on, other than what follows from the above.
Results may differ from a plain program's by a relative error of at most 0.0095.
Values may be sent and summed in bfloat16 or wider, within the bound.
No kernel may reach another device: no remote copies, remote signals or barrier semaphores. Data moves between devices by JAX's collectives and lax.ppermute only.
A program may use at most 64 MiB of HBM per device.

v0:
```python
import jax
import jax.numpy as jnp
from jax import lax
from jax.sharding import PartitionSpec as P

BLOCK = 128


def passed_along(block, axis, distance):
    devices = range(lax.axis_size(axis))
    route = [(i - distance, i) for i in devices if i - distance in devices]
    return lax.ppermute(block, axis, route)


def prefix(array, axis, combine, identity):
    length, here = (lax.axis_size(axis), lax.axis_index(axis))
    everything = jax.tree.map(lambda part: lax.all_gather(part, axis), array)
    start = jax.tree.map(
        lambda part, zero: jnp.broadcast_to(jnp.asarray(zero, part.dtype), part.shape),
        array,
        identity,
    )

    def step(k, before):
        at = length - 1 - k
        reached = at > here
        new = combine(before, jax.tree.map(lambda part: part[at], everything))
        return jax.tree.map(lambda a, b: jnp.where(reached, a, b), new, before)

    return lax.fori_loop(0, length, step, start)


def combine_pair(earlier, later):
    decay_e, value_e = earlier
    decay_l, value_l = later
    return (decay_l * decay_e, value_l + decay_l[:, None] * value_e)


def body(states, episode_end, feature_head, successor_head, horizon_gap, trace_gap):
    steps_dev = states.shape[1]
    num_k = horizon_gap.shape[0]
    width_kf = successor_head.shape[1]
    width_f = width_kf // num_k
    state_rows = states[0]
    keep = 1.0 - episode_end[0].astype(jnp.float32)
    ended = episode_end[0].astype(jnp.float32)
    features = jnp.dot(state_rows, feature_head, preferred_element_type=jnp.float32)
    pred = jnp.dot(state_rows, successor_head, preferred_element_type=jnp.float32).astype(
        jnp.bfloat16
    )
    incoming = passed_along(pred[:1], "tm", -1)
    pred_next = jnp.concatenate([pred[1:], incoming], axis=0).astype(jnp.float32)
    discount = 1.0 - horizon_gap
    rate = discount * (1.0 - trace_gap)
    scale_k = jnp.sqrt(1.0 - rate * rate)
    boot = discount * trace_gap
    log_rate = jnp.log(rate)
    source = scale_k[None, :, None] * features[:, None, :] + boot[None, :, None] * keep[
        :, None, None
    ] * pred_next.reshape(steps_dev, num_k, width_f)
    blk = min(BLOCK, steps_dev)
    nblocks = steps_dev // blk
    source_b = source.reshape(nblocks, blk, num_k, width_f)
    ended_b = ended.reshape(nblocks, blk)
    counts = jnp.cumsum(ended_b, axis=1) - ended_b
    totals = jnp.sum(ended_b, axis=1)
    offsets = jnp.arange(blk)
    spans = offsets[None, :] - offsets[:, None]
    toeplitz = jnp.where(
        spans[None] >= 0,
        jnp.exp(jnp.maximum(spans, 0)[None].astype(jnp.float32) * log_rate[:, None, None]),
        0.0,
    )
    same_seg = (counts[:, None, :] == counts[:, :, None]).astype(jnp.float32)
    matrices = toeplitz[None] * same_seg[:, None]
    local_vals = jnp.einsum("bkts,bskf->btkf", matrices, source_b, precision=lax.Precision.HIGHEST)
    to_end = jnp.exp((blk - offsets).astype(jnp.float32)[None, :, None] * log_rate[None, None, :])
    to_end = to_end * (counts == totals[:, None]).astype(jnp.float32)[:, :, None]
    carry_value = jnp.zeros((num_k, width_f), jnp.float32)
    carry_decay = jnp.ones((num_k,), jnp.float32)
    value_list = []
    decay_list = []
    for block_id in range(nblocks - 1, -1, -1):
        block_val = local_vals[block_id] + to_end[block_id][:, :, None] * carry_value[None]
        block_dec = to_end[block_id] * carry_decay[None]
        value_list.insert(0, block_val)
        decay_list.insert(0, block_dec)
        carry_value = block_val[0]
        carry_decay = block_dec[0]
    local_all = jnp.concatenate(value_list, axis=0)
    decay_all = jnp.concatenate(decay_list, axis=0)
    ident = (jnp.ones((num_k,), jnp.float32), jnp.zeros((num_k, width_f), jnp.float32))
    outside = prefix((carry_decay, carry_value), "tm", combine_pair, ident)[1]
    values = local_all + decay_all[:, :, None] * outside[None]
    values = values.reshape(steps_dev, width_kf)
    returns = values.astype(jnp.bfloat16)[None]
    resid = (pred.astype(jnp.float32) - values).astype(jnp.bfloat16)
    norm_scale = 1.0 / jnp.sqrt(
        jnp.float32(steps_dev * lax.axis_size("tm") * lax.axis_size("traj"))
    )
    full_grad = lax.dot_general(
        state_rows, resid, (((0,), (0,)), ((), ())), preferred_element_type=jnp.float32
    )
    reduced = lax.psum_scatter(
        full_grad.astype(jnp.bfloat16), "tm", scatter_dimension=1, tiled=True
    )
    head_grad = lax.psum_scatter(reduced, "traj", scatter_dimension=0, tiled=True).astype(
        jnp.float32
    )
    return (returns, head_grad * norm_scale)


def solution(mesh):
    return jax.shard_map(
        body,
        mesh=mesh,
        in_specs=(P("traj", "tm", None), P("traj", "tm"), P(), P(), P(), P()),
        out_specs=(P("traj", "tm", None), P("traj", "tm")),
        check_vma=False,
    )
```

profile of v0, /device:TPU:1, one launch (start us, length us, event | category | flops | bytes accessed | tf_op | source)
XLA Modules:
  0.0 238.9 jit_solution(16312482318387090956)
XLA Ops:
  7.3 0.9 copy-done
  8.2 3.4 %convolution_convert_fusion = bf16[256,2048]{1,0:T(8,128)(2,1)S(1)} fusion(bf16[1024,2048]{1,0:T(8,128)(2,1)} %param.11, bf16[1,256,1024]{2,1,0:T(8,128)(2,1)S(1)} %copy-done), kind=kOutput, calls=%fused_computation.4 | convolution fusion | flops 1074266112 | bytes 5767168 | tf_op jit(solution)/shard_map/dot_general | solution.py:48
  11.7 1.3 collective-permute-start
  13.1 0.1 fusion.26
  13.2 0.3 reduce_window_sum.11
  13.7 0.1 slice_reduce_fusion.1
  13.9 0.1 compare_convert_fusion
  14.0 0.1 broadcast_multiply_fusion
  14.1 0.3 fusion.21
  14.4 1.2 exponential_select_fusion
  15.6 0.1 slice_reduce_fusion
  15.7 0.3 slice.44
  16.0 0.2 copy.47
  16.2 1.2 slice.56
  17.4 0.3 copy.42
  17.8 1.1 mul.264
  18.9 1.6 copy.44
  20.4 0.1 copy.38
  20.5 17.4 %all-gather = f32[8,1,16]{2,1,0:T(1,128)S(1)} all-gather(f32[1,1,16]{2,1,0:T(1,128)S(1)} %bitcast.88), channel_id=1, replica_groups=mesh['tm'=8,'traj'=32] {'tm'}, dimensions={0}, use_global_device_ids=true | all-gather | bytes 576 | tf_op jit(solution)/shard_map/all_gather | solution.py:17
  38.0 1.3 pad_maximum_fusion
  39.3 0.7 fusion.5
  40.1 0.5 copy-done.6
  40.6 4.0 %fusion.9 = f32[2,128,16,128]{1,3,2,0:T(8,128)S(1)} fusion(f32[2,128,16,128]{3,2,1,0:T(8,128)S(1)} %fusion.5, f32[2,128,128]{2,1,0:T(8,128)S(1)} %compare_convert_fusion, f32[16,128,128]{2,1,0:T(8,128)S(1)} %copy-done.6), kind=kOutput, calls=%fused_computation.16 | convolution fusion | flops 805830656 | bytes 5373952 | tf_op jit(solution)/shard_map/bkts,bskf->btkf/dot_general | solution.py:76
  44.5 1.6 slice_bitcast_fusion.3
  46.1 0.3 fusion.15
  46.5 1.3 slice_add_fusion
  47.8 1.6 copy.39
  49.3 18.4 %all_gather.6 = f32[8,16,128]{2,1,0:T(8,128)S(1)} all-gather(f32[1,16,128]{2,1,0:T(8,128)S(1)} %copy.39), channel_id=1, replica_groups=mesh['tm'=8,'traj'=32] {'tm'}, dimensions={0}, use_global_device_ids=true | all-gather | bytes 73728 | tf_op jit(solution)/shard_map/all_gather | solution.py:17
  67.7 0.7 while.16
  67.7 0.1 fusion.30
  67.8 0.1 fusion.30
  67.9 0.1 fusion.30
  68.5 2.5 %copy.41 = f32[128,2048]{1,0:T(8,128)} copy(f32[128,2048]{0,1:T(8,128)} %bitcast.76) | data formatting | bytes 2097152 | tf_op jit(solution)/shard_map/squeeze | solution.py:84
  71.0 2.6 %copy.43 = f32[128,2048]{1,0:T(8,128)} copy(f32[128,2048]{0,1:T(8,128)} %bitcast.75) | data formatting | bytes 2097152 | tf_op jit(solution)/shard_map/squeeze | solution.py:84
  73.6 1.4 add.89
  75.0 0.1 copy-done.5
  75.1 0.2 multiply_add_fusion
  75.3 0.6 mul.272
  76.0 0.4 copy-done.2
  76.3 0.7 copy-done.4
  77.0 4.4 %convert_bitcast_fusion = bf16[1024,2048]{0,1:T(8,128)(2,1)} fusion(f32[32,8,16,128]{3,2,1,0:T(8,128)S(1)} %bitcast.68, f32[128,2048]{1,0:T(8,128)S(1)} %add.89, f32[128,2048]{1,0:T(8,128)S(1)} %multiply_add_fusion, bf16[256,2048]{1,0:T(8,128)(2,1)S(1)} %copy-done.4, f32[2048]{0:T(1024)S(1)} %bitcast.78, bf16[1,256,1024]{2,1,0:T(8,128)(2,1)S(1)} %copy-done), kind=kOutput, calls=%fused_computation.3 | convolution fusion | flops 1078984704 | bytes 9969664 | tf_op jit(solution)/shard_map/dot_general | solution.py:101
  81.5 64.0 %reduce-scatter.5.cloned.1.call-done = bf16[1024,256]{0,1:T(8,128)(2,1)} async-done(((bf16[1024,2048]{0,1:T(8,128)(2,1)}), bf16[1024,256]{0,1:T(8,128)(2,1)}) %reduce-scatter.5.cloned.1.call-update) | async-done | bytes 524304 | tf_op jit(solution)/shard_map/reduce_scatter | solution.py:104
  145.5 2.0 copy.45
  147.6 1.5 mul.273
  149.1 3.6 %fusion.4 = bf16[1,256,2048]{2,1,0:T(8,128)(2,1)} fusion(f32[1,128,2048]{2,1,0:T(8,128)} %bitcast.69, f32[1,128,2048]{2,1,0:T(8,128)} %bitcast.70, f32[1,256,2048]{2,1,0:T(8,128)} %mul.273, f32[2048]{0:T(1024)S(1)} %bitcast.79), kind=kLoop, calls=%fused_computation.10 | loop fusion | flops 2097152 | bytes 5251072 | tf_op jit(solution)/shard_map/convert_element_type | solution.py:96
  152.7 77.9 %reduce-scatter.7.cloned.1.call-done = bf16[32,256]{1,0:T(8,128)(2,1)} async-done(((bf16[1024,256]{1,0:T(8,128)(2,1)}), bf16[32,256]{1,0:T(8,128)(2,1)}) %reduce-scatter.7.cloned.1.call-update) | async-done | bytes 16400
  230.5 0.8 copy.46
  231.4 0.7 copy.40
  (51 shorter events, 1.1 us)
Async XLA Ops:
  7.2 1.0 copy-start
  7.2 5.9 %copy-start.8 = (s32[1,256]{1,0:T(1,128)S(1)}, s32[1,256]{1,0:T(1,128)}, u32[]{:S(2)}) copy-start(s32[1,256]{1,0:T(1,128)} %param.9) | copy-start | bytes 3076
  7.2 6.4 %copy-start.10 = (f32[16]{0:T(128)S(1)}, f32[16]{0:T(128)}, u32[]{:S(2)}) copy-start(f32[16]{0:T(128)} %param.12) | copy-start | bytes 196
  7.2 6.4 %copy-start.9 = (f32[16]{0:T(128)S(1)}, f32[16]{0:T(128)}, u32[]{:S(2)}) copy-start(f32[16]{0:T(128)} %param.13) | copy-start | bytes 196
  7.2 6.9 %copy-start.7 = (bf16[1024,128]{1,0:T(8,128)(2,1)S(1)}, bf16[1024,128]{1,0:T(8,128)(2,1)}, u32[]{:S(2)}) copy-start(bf16[1024,128]{1,0:T(8,128)(2,1)} %param.10) | copy-start | bytes 786436
  7.2 138.3 %reduce-scatter.5.cloned.1.call-start = ((), (), s32[]{:S(2)}) async-start(), calls=%async_computation.2 | async-start | bytes 4718592 | tf_op jit(solution)/shard_map/reduce_scatter | solution.py:104
  11.7 4.3 %copy-start.3 = (bf16[256,2048]{1,0:T(8,128)(2,1)}, bf16[256,2048]{1,0:T(8,128)(2,1)S(1)}, u32[]{:S(2)}) copy-start(bf16[256,2048]{1,0:T(8,128)(2,1)S(1)} %convolution_convert_fusion) | copy-start | bytes 3145732
  11.7 26.3 %collective-permute-start = (bf16[1,2048]{1,0:T(2,128)(2,1)S(1)}, bf16[1,2048]{1,0:T(2,128)(2,1)S(1)}, u32[]{:S(2)}, u32[]{:S(2)}) collective-permute-start(bf16[1,2048]{1,0:T(2,128)(2,1)S(1)} %slice.45), channel_id=1, source_target_pairs={{32,0},{64,32},{96,64},{128,96},{160,128},{192,160},{224,192},{33,... | collective-permute-start | bytes 12296 | tf_op jit(solution)/shard_map/ppermute | solution.py:12
  39.3 1.2 copy-start.6
  73.6 1.5 copy-start.5
  75.0 1.0 copy-start.1
  75.1 1.9 copy-start.4
  75.3 1.0 copy-start.2
  81.4 149.1 %reduce-scatter.7.cloned.1.call-start = ((), (), s32[]{:S(2)}) async-start(), calls=%async_computation.3 | async-start | bytes 540672
Sparse Core Ops, SparseCore 0:
  81.6 63.8 reduce-scatter.4
  149.2 81.2 reduce-scatter.6
where the time goes:
time: 240 us; the launch traced here: 239 us
  waiting for transfers between devices  142 us (59%)
  blocking collectives  35.8 us (15%)
  local copies, waits for them, and re-layouts  21.7 us (9%)
  between operations  14.3 us (6%)
  matrix products  12.1 us (5%)
  other arithmetic  11.7 us (5%)
    unnamed x3, waiting for transfers between devices  77.9 us
    reduce_scatter x1, waiting for transfers between devices, body(): lax.psum_scatter(full_grad.astype(jnp.bfloat16), 'tm', scatter_dimension=...  64 us
    all_gather x2, blocking collectives, prefix(): everything = jax.tree.map(lambda part: lax.all_gather(part, axis), array)  35.8 us
    squeeze x3, local copies, waits for them, and re-layouts, body(): local_vals[block_id] + to_end[block_id][:, :, None] * carry_value[None]  6.73 us
    unnamed x26, local copies, waits for them, and re-layouts  6.45 us
  transfers between devices with their start and end apart: 3, of which 2 were waited for; matrix products, arithmetic and copies ran while one was open for 5% of the time, Pallas kernels for 0%

commit v1 on v0

v1 whole, which is shorter than its diff:
```python
import functools
import jax
import jax.numpy as jnp
from jax import lax
from jax.experimental import pallas as pl
from jax.experimental.pallas import tpu as pltpu
from jax.sharding import Mesh, PartitionSpec as P

F = 128
MIB = 1 << 20
f32, bf16 = jnp.float32, jnp.bfloat16
SMEM = pl.BlockSpec(memory_space=pltpu.SMEM)


def coefficients(hg_ref, tg_ref, k):
    hg = jnp.full((1, F), hg_ref[k], f32)
    tg = jnp.full((1, F), tg_ref[k], f32)
    discount = 1.0 - hg
    rate = discount * (1.0 - tg)
    return jnp.log(rate), jnp.sqrt(1.0 - rate * rate), discount * tg / rate


def iota(shape, dim):
    return lax.broadcasted_iota(jnp.int32, shape, dim)


def local_kernel(hg_ref, tg_ref, end_ref, s_ref, wf_ref, w_ref, p_ref, g_ref, msg_ref, open_ref, f_ref, mask_ref):
    i = pl.program_id(0)
    steps = s_ref.shape[0]
    per = w_ref.shape[1] // F
    num_k = hg_ref.shape[0]

    @pl.when(i == 0)
    def _():
        f_ref[...] = jnp.dot(s_ref[...], wf_ref[...], preferred_element_type=f32)
        rows, cols = iota((steps, steps), 0), iota((steps, steps), 1)
        ended = jnp.broadcast_to(end_ref[...].astype(f32), (steps, steps)).astype(bf16)
        below = (cols < rows).astype(f32).astype(bf16)
        above = (rows < cols).astype(f32).astype(bf16)
        at_row = lax.dot_general(below, ended, (((1,), (1,)), ((), ())), preferred_element_type=f32)
        at_col = jnp.dot(ended, above, preferred_element_type=f32)
        mask_ref[...] = jnp.where((at_row == at_col) & (cols >= rows), 1.0, 0.0).astype(bf16)
        total = jnp.sum(end_ref[...].astype(f32), axis=1, keepdims=True)
        open_ref[...] = jnp.where(at_row[:, :F] == total, 1.0, 0.0)
        for z in range(msg_ref.shape[0]):
            msg_ref[z, num_k:, :] = jnp.broadcast_to(jnp.where(total == 0.0, 1.0, 0.0), (msg_ref.shape[1] - num_k, F))

    pred = jnp.dot(s_ref[...], w_ref[...], preferred_element_type=f32).astype(bf16)
    p_ref[...] = pred
    t = iota((steps, F), 0).astype(f32)
    scaled, backs, betas = [], [], []
    for j in range(per):
        log_rate, scale, beta = coefficients(hg_ref, tg_ref, i * per + j)
        q = scale * f_ref[...] + beta * pred[:, j * F : (j + 1) * F].astype(f32)
        scaled.append(jnp.exp(t * log_rate) * q)
        backs.append(jnp.exp(-t * log_rate))
        betas.append(beta)
    scaled = jnp.concatenate(scaled, axis=1)
    high = scaled.astype(bf16)
    low = (scaled - high.astype(f32)).astype(bf16)
    sums = jnp.dot(mask_ref[...], high, preferred_element_type=f32)
    sums = sums + jnp.dot(mask_ref[...], low, preferred_element_type=f32)
    for j in range(per):
        cols = slice(j * F, (j + 1) * F)
        h = backs[j] * sums[:, cols]
        g_ref[:, cols] = h - betas[j] * pred[:, cols].astype(f32)
        for z in range(msg_ref.shape[0]):
            msg_ref[z, pl.ds(i * per + j, 1), :] = h[:1]


def finish_kernel(axis, hg_ref, tg_ref, msg_ref, open_ref, p_ref, g_ref, ret_ref, res_ref):
    i = pl.program_id(0)
    here = lax.axis_index(axis)
    steps = p_ref.shape[0]
    per = p_ref.shape[1] // F
    num_k = hg_ref.shape[0]
    t = iota((steps, F), 0).astype(f32)
    for j in range(per):
        k = i * per + j
        log_rate, _, _ = coefficients(hg_ref, tg_ref, k)
        through = jnp.exp(steps * log_rate)
        later = jnp.zeros((1, F), f32)
        for z in range(msg_ref.shape[0] - 1, 0, -1):
            block = msg_ref[z, pl.ds(k, 1), :] + through * msg_ref[z, num_k : num_k + 1, :] * later
            later = jnp.where(z > here, block, later)
        cols = slice(j * F, (j + 1) * F)
        g = g_ref[:, cols] + open_ref[...] * jnp.exp((steps - t) * log_rate) * later
        ret_ref[:, cols] = g.astype(bf16)
        res_ref[:, cols] = (p_ref[:, cols].astype(f32) - g).astype(bf16)


def grad_kernel(axis, s_ref, so_ref, r_ref, ro_ref, g_ref, st_ref, sto_ref):
    parts, rows, _ = g_ref.shape
    width = s_ref.shape[1]

    @pl.when(pl.program_id(0) == 0)
    def _():
        c = lax.axis_index(axis)
        r = iota((parts * rows, width), 0)
        want = (r // rows) * (2 * rows) + c * rows + r % rows
        pick = (want == iota((parts * rows, width), 1)).astype(f32).astype(bf16)
        contract = (((1,), (1,)), ((), ()))
        st_ref[...] = lax.dot_general(pick, s_ref[...], contract, preferred_element_type=f32).astype(bf16)
        sto_ref[...] = lax.dot_general(pick, so_ref[...], contract, preferred_element_type=f32).astype(bf16)

    g = jnp.dot(st_ref[...], r_ref[...], preferred_element_type=f32)
    g = g + jnp.dot(sto_ref[...], ro_ref[...], preferred_element_type=f32)
    g_ref[...] = g.astype(bf16).reshape(g_ref.shape)


def sum_kernel(x_ref, y_ref):
    y_ref[0] = jnp.sum(x_ref[...].astype(f32), axis=0).astype(y_ref.dtype)


def final_kernel(norm, x_ref, y_ref):
    y_ref[...] = jnp.sum(x_ref[...].astype(f32), axis=0) * norm


def params(mib=40):
    return pltpu.CompilerParams(vmem_limit_bytes=mib * MIB)


def whole(shape):
    return pl.BlockSpec(shape, lambda i: (0,) * len(shape))


def columns(rows, width):
    return pl.BlockSpec((rows, width), lambda i: (0, i))


def body(states, episode_end, feature_head, successor_head, horizon_gap, trace_gap):
    steps, width = states.shape[1:]
    num_k = horizon_gap.shape[0]
    kf = successor_head.shape[1]
    nz, ny, nx, nc = (lax.axis_size(a) for a in ("z", "y", "x", "c"))
    s = states[0]
    swap = [(a, nc - 1 - a) for a in range(nc)]
    s_other = lax.ppermute(s, "c", swap)
    blk = 2 * F
    n = kf // blk
    msg_rows = num_k + 8
    pred, g_local, msg, still_open = pl.pallas_call(
        local_kernel,
        grid=(n,),
        in_specs=[SMEM, SMEM, whole((1, steps)), whole((steps, width)), whole((width, F)), columns(width, blk)],
        out_specs=[columns(steps, blk), columns(steps, blk), whole((nz, msg_rows, F)), whole((steps, F))],
        out_shape=[
            jax.ShapeDtypeStruct((steps, kf), bf16),
            jax.ShapeDtypeStruct((steps, kf), f32),
            jax.ShapeDtypeStruct((nz, msg_rows, F), f32),
            jax.ShapeDtypeStruct((steps, F), f32),
        ],
        scratch_shapes=[pltpu.VMEM((steps, F), f32), pltpu.VMEM((steps, steps), bf16)],
        compiler_params=params(),
        name="local",
    )(horizon_gap, trace_gap, episode_end, s, feature_head, successor_head)
    msg = lax.all_to_all(msg, "z", 0, 0, tiled=True)
    returns, resid = pl.pallas_call(
        functools.partial(finish_kernel, "z"),
        grid=(n,),
        in_specs=[SMEM, SMEM, whole((nz, msg_rows, F)), whole((steps, F)), columns(steps, blk), columns(steps, blk)],
        out_specs=[columns(steps, blk), columns(steps, blk)],
        out_shape=[jax.ShapeDtypeStruct((steps, kf), bf16)] * 2,
        compiler_params=params(),
        name="finish",
    )(horizon_gap, trace_gap, msg, still_open, pred, g_local)
    resid_other = lax.ppermute(resid, "c", swap)
    parts, rows = ny * nx, width // (ny * nx * nc)
    gblk = 4 * F
    grad = pl.pallas_call(
        functools.partial(grad_kernel, "c"),
        grid=(kf // gblk,),
        in_specs=[whole((steps, width)), whole((steps, width)), columns(steps, gblk), columns(steps, gblk)],
        out_specs=pl.BlockSpec((parts, rows, gblk), lambda i: (0, 0, i)),
        out_shape=jax.ShapeDtypeStruct((parts, rows, kf), bf16),
        scratch_shapes=[pltpu.VMEM((parts * rows, steps), bf16)] * 2,
        compiler_params=params(),
        name="grad",
    )(s, s_other, resid, resid_other)
    grad = lax.all_to_all(grad, ("y", "x"), 0, 0, tiled=True)
    cols = kf // nz
    grad = pl.pallas_call(
        sum_kernel,
        grid=(nz,),
        in_specs=[pl.BlockSpec((parts, rows, cols), lambda i: (0, 0, i))],
        out_specs=pl.BlockSpec((1, rows, cols), lambda i: (i, 0, 0)),
        out_shape=jax.ShapeDtypeStruct((nz, rows, cols), bf16),
        compiler_params=params(),
        name="sum_plane",
    )(grad)
    grad = lax.all_to_all(grad, "z", 0, 0, tiled=True)
    norm = float(steps * nz * ny * nx * nc) ** -0.5
    head_grad = pl.pallas_call(
        functools.partial(final_kernel, norm),
        out_shape=jax.ShapeDtypeStruct((rows, cols), f32),
        name="sum_line",
    )(grad)
    return returns[None], head_grad


def solution(mesh):
    grid = Mesh(mesh.devices.reshape(8, 4, 4, 2), ("z", "y", "x", "c"))
    traj = ("y", "x", "c")
    return jax.shard_map(
        body,
        mesh=grid,
        in_specs=(P(traj, "z", None), P(traj, "z"), P(), P(), P(), P()),
        out_specs=(P(traj, "z", None), P(traj, "z")),
        check_vma=False,
    )
```

time: 240 us -> 90.5 us (0.38)
  waiting for transfers between devices: 142 us -> 2.99 us
  blocking collectives: 35.8 us -> 61.7 us
  Pallas kernels: 0 us -> 16 us
  local copies, waits for them, and re-layouts: 21.7 us -> 6.17 us
  between operations: 14.3 us -> 0.68 us
  matrix products: 12.1 us -> 0 us
  other arithmetic: 11.7 us -> 0 us
    unnamed x3 -> x0, waiting for transfers between devices: 77.9 us -> none
    reduce_scatter x1 -> x0, waiting for transfers between devices: 64 us -> none  [body(): lax.psum_scatter(full_grad.astype(jnp.bfloat16), 'tm', scatter_dimension=...]
    all_to_all x0 -> x3, blocking collectives: none -> 61.7 us  [the longest x1 34.1 us: body(): grad = lax.all_to_all(grad, ('y', 'x'), 0, 0, tiled=True)]
    all_gather x2 -> x0, blocking collectives: 35.8 us -> none  [prefix(): everything = jax.tree.map(lambda part: lax.all_gather(part, axis), array)]
    pallas_call x0 -> x5, Pallas kernels: none -> 16 us  [the longest x1 6.93 us: body(): pl.pallas_call(local_kernel, grid=(n,), in_specs=[SMEM, SMEM, whole((1, s...]
    dot_general x4 -> x0, matrix products: 12.1 us -> none  [the longest x1 4.39 us: body(): lax.dot_general(state_rows, resid, (((0,), (0,)), ((), ())), preferred_el...]
    squeeze x3 -> x0, local copies, waits for them, and re-layouts: 6.73 us -> none  [body(): local_vals[block_id] + to_end[block_id][:, :, None] * carry_value[None]]
    mul x15 -> x0, local copies, waits for them, and re-layouts: 5.21 us -> none  [the longest x5 3.05 us: body(): to_end[block_id][:, :, None] * carry_value[None]]
  transfers between devices with their start and end apart: 3 -> 2, of which waited for: 2 -> 1; matrix products, arithmetic and copies ran while one was open for 5% -> 0% of each run, Pallas kernels for 0% -> 0%
where the time goes in v1:
time: 90.5 us; the launch traced here: 89.6 us
  blocking collectives  61.7 us (68%)
  Pallas kernels  16 us (18%)
  local copies, waits for them, and re-layouts  6.17 us (7%)
  waiting for transfers between devices  2.99 us (3%)
  starting transfers between devices  2.11 us (2%)
    all_to_all x1, blocking collectives, body(): grad = lax.all_to_all(grad, ('y', 'x'), 0, 0, tiled=True)  34.1 us
    all_to_all x1, blocking collectives, body(): msg = lax.all_to_all(msg, 'z', 0, 0, tiled=True)  16.6 us
    all_to_all x1, blocking collectives, body(): grad = lax.all_to_all(grad, 'z', 0, 0, tiled=True)  11 us
    pallas_call x1, Pallas kernels, body(): pl.pallas_call(local_kernel, grid=(n,), in_specs=[SMEM, SMEM, whole((1, s...  6.93 us
    unnamed x14, local copies, waits for them, and re-layouts  6.17 us
    pallas_call x1, Pallas kernels, body(): pl.pallas_call(functools.partial(finish_kernel, 'z'), grid=(n,), in_specs...  3.98 us
    ppermute x1, waiting for transfers between devices, body(): s_other = lax.ppermute(s, 'c', swap)  2.99 us
    pallas_call x1, Pallas kernels, body(): pl.pallas_call(functools.partial(grad_kernel, 'c'), grid=(kf // gblk,), i...  2.81 us
  transfers between devices with their start and end apart: 2, of which 1 were waited for; matrix products, arithmetic and copies ran while one was open for 0% of the time, Pallas kernels for 0%

profile of v1, /device:TPU:1, one launch (start us, length us, event | category | flops | bytes accessed | tf_op | source)
XLA Modules:
  0.0 89.6 jit_solution(13302819904119285950)
XLA Ops:
  0.6 0.0 copy-start
  0.6 2.2 %copy-done = bf16[1024,2048]{1,0:T(8,128)(2,1)S(1)} copy-done((bf16[1024,2048]{1,0:T(8,128)(2,1)S(1)}, bf16[1024,2048]{1,0:T(8,128)(2,1)}, u32[]{:S(2)}) %copy-start) | copy-done | bytes 4194328
  2.8 0.0 copy-start.1
  2.8 1.0 %copy-done.1 = bf16[1,256,1024]{2,1,0:T(8,128)(2,1)S(1)} copy-done((bf16[1,256,1024]{2,1,0:T(8,128)(2,1)S(1)}, bf16[1,256,1024]{2,1,0:T(8,128)(2,1)}, u32[]{:S(2)}) %copy-start.1) | copy-done | bytes 524312
  3.9 0.0 copy-start.3
  3.9 0.9 %copy-done.3 = bf16[1024,128]{1,0:T(8,128)(2,1)S(1)} copy-done((bf16[1024,128]{1,0:T(8,128)(2,1)S(1)}, bf16[1024,128]{1,0:T(8,128)(2,1)}, u32[]{:S(2)}) %copy-start.3) | copy-done | bytes 262168
  4.8 0.0 copy-start.4
  4.8 0.7 copy-done.4
  5.5 0.0 copy-start.5
  5.5 0.7 copy-done.5
  6.1 0.0 copy-start.6
  6.1 0.7 copy-done.6
  6.8 6.9 %local.1 = (bf16[256,2048]{1,0:T(8,128)(2,1)S(1)}, f32[256,2048]{1,0:T(8,128)S(1)}, f32[8,24,128]{2,1,0:T(8,128)S(1)}, f32[256,128]{1,0:T(8,128)S(1)}) custom-call(f32[16]{0:T(128)S(1)} %copy-done.4, f32[16]{0:T(128)S(1)} %copy-done.5, s32[1,256]{1,0:T(1,128)S(1)} %copy-done.6, bf16[256,1024]{1,0:T(8,128)(2,1)S(1)} %bitcast.2, ...), custom_call_target="tpu_custom_call" | custom-call | tf_op jit(solution)/shard_map/local/pallas_call | solution.py:142
  13.7 0.0 copy-start.2
  13.7 16.6 %all_to_all.15.msg_ref = f32[8,24,128]{2,1,0:T(8,128)S(1)} all-to-all(f32[8,24,128]{2,1,0:T(8,128)S(1)} %get-tuple-element.8), channel_id=1, replica_groups=mesh['z'=8,'y'=4,'x'=4,'c'=2] {'z'}, dimensions={0} | all-to-all | bytes 196608 | tf_op jit(solution)/shard_map/all_to_all | solution.py:157
  30.3 4.0 %finish.1 = (bf16[256,2048]{1,0:T(8,128)(2,1)}, bf16[256,2048]{1,0:T(8,128)(2,1)S(1)}) custom-call(f32[16]{0:T(128)S(1)} %copy-done.4, f32[16]{0:T(128)S(1)} %copy-done.5, f32[8,24,128]{2,1,0:T(8,128)S(1)} %all_to_all.15.msg_ref, f32[256,128]{1,0:T(8,128)S(1)} %get-tuple-element.9.open_ref, bf16[256,2048]{1,0:T(8,128)(2,1)S(1)} %get-tuple-element.10.p_ref, ...), custom_call_target="tpu_custom_call" | custom-call | tf_op jit(solution)/shard_map/finish/pallas_call | solution.py:158
  34.3 2.1 %collective-permute-start.1 = (bf16[256,2048]{1,0:T(8,128)(2,1)S(1)}, bf16[256,2048]{1,0:T(8,128)(2,1)S(1)}, u32[]{:S(2)}, u32[]{:S(2)}) collective-permute-start(bf16[256,2048]{1,0:T(8,128)(2,1)S(1)} %get-tuple-element.13.r_ref), channel_id=1, source_target_pairs={{0,1},{1,0},{2,3},{3,2},{4,5},{5,4},{6,7},{7,6},{8,9},{9,8},{10,11... | collective-permute-start | bytes 3145736 | tf_op jit(solution)/shard_map/ppermute | solution.py:167
  36.4 0.0 copy-done.2
  36.4 0.0 collective-permute-start
  36.4 3.0 %collective-permute-done.so_ref = bf16[256,1024]{1,0:T(8,128)(2,1)S(1)} collective-permute-done((bf16[256,1024]{1,0:T(8,128)(2,1)S(1)}, bf16[256,1024]{1,0:T(8,128)(2,1)S(1)}, u32[]{:S(2)}, u32[]{:S(2)}) %collective-permute-start) | collective-permute-done | bytes 524320 | tf_op jit(solution)/shard_map/ppermute | solution.py:138
  39.4 0.0 collective-permute-done.1.ro_ref
  39.4 2.8 %grad.1 = bf16[16,32,2048]{2,1,0:T(8,128)(2,1)S(1)} custom-call(bf16[256,1024]{1,0:T(8,128)(2,1)S(1)} %bitcast.4, bf16[256,1024]{1,0:T(8,128)(2,1)S(1)} %collective-permute-done.so_ref, bf16[256,2048]{1,0:T(8,128)(2,1)S(1)} %get-tuple-element.13.r_ref, bf16[256,2048]{1,0:T(8,128)(2,1)S(1)} %collective-permute-done.1.ro_ref), custom_call_target="tpu_custom_call" | custom-call | tf_op jit(solution)/shard_map/grad/pallas_call | solution.py:170
  42.2 34.1 %all_to_all.16.x_ref = bf16[16,32,2048]{2,1,0:T(8,128)(2,1)S(1)} all-to-all(bf16[16,32,2048]{2,1,0:T(8,128)(2,1)S(1)} %grad.1), channel_id=1, replica_groups=mesh['z'=8,'y'=4,'x'=4,'c'=2] {'y','x'}, dimensions={0} | all-to-all | bytes 4194304 | tf_op jit(solution)/shard_map/all_to_all | solution.py:180
  76.3 0.7 sum_plane.1
  77.1 11.0 %all_to_all.17.x_ref = bf16[8,32,256]{2,1,0:T(8,128)(2,1)} all-to-all(bf16[8,32,256]{2,1,0:T(8,128)(2,1)S(1)} %sum_plane.1), channel_id=1, replica_groups=mesh['z'=8,'y'=4,'x'=4,'c'=2] {'z'}, dimensions={0} | all-to-all | bytes 262144 | tf_op jit(solution)/shard_map/all_to_all | solution.py:191
  88.1 1.5 %sum_line.1 = f32[32,256]{1,0:T(8,128)} custom-call(bf16[8,32,256]{2,1,0:T(8,128)(2,1)} %all_to_all.17.x_ref), custom_call_target="tpu_custom_call" | custom-call | tf_op jit(solution)/shard_map/sum_line/pallas_call | solution.py:193
Async XLA Ops:
  0.6 2.2 %copy-start = (bf16[1024,2048]{1,0:T(8,128)(2,1)S(1)}, bf16[1024,2048]{1,0:T(8,128)(2,1)}, u32[]{:S(2)}) copy-start(bf16[1024,2048]{1,0:T(8,128)(2,1)} %w_ref.1) | copy-start | bytes 12582916
  2.8 1.0 %copy-start.1 = (bf16[1,256,1024]{2,1,0:T(8,128)(2,1)S(1)}, bf16[1,256,1024]{2,1,0:T(8,128)(2,1)}, u32[]{:S(2)}) copy-start(bf16[1,256,1024]{2,1,0:T(8,128)(2,1)} %param.6) | copy-start | bytes 1572868
  3.9 0.9 %copy-start.3 = (bf16[1024,128]{1,0:T(8,128)(2,1)S(1)}, bf16[1024,128]{1,0:T(8,128)(2,1)}, u32[]{:S(2)}) copy-start(bf16[1024,128]{1,0:T(8,128)(2,1)} %wf_ref.1) | copy-start | bytes 786436
  4.8 0.7 copy-start.4
  5.5 0.7 copy-start.5
  6.1 0.7 copy-start.6
  13.7 22.6 %copy-start.2 = (bf16[1,256,1024]{2,1,0:T(8,128)(2,1)S(1)}, bf16[1,256,1024]{2,1,0:T(8,128)(2,1)}, u32[]{:S(2)}) copy-start(bf16[1,256,1024]{2,1,0:T(8,128)(2,1)} %param.6) | copy-start | bytes 1572868
  34.3 5.1 %collective-permute-start.1 = (bf16[256,2048]{1,0:T(8,128)(2,1)S(1)}, bf16[256,2048]{1,0:T(8,128)(2,1)S(1)}, u32[]{:S(2)}, u32[]{:S(2)}) collective-permute-start(bf16[256,2048]{1,0:T(8,128)(2,1)S(1)} %get-tuple-element.13.r_ref), channel_id=1, source_target_pairs={{0,1},{1,0},{2,3},{3,2},{4,5},{5,4},{6,7},{7,6},{8,9},{9,8},{10,11... | collective-permute-start | bytes 3145736 | tf_op jit(solution)/shard_map/ppermute | solution.py:167
  36.4 3.0 %collective-permute-start = (bf16[256,1024]{1,0:T(8,128)(2,1)S(1)}, bf16[256,1024]{1,0:T(8,128)(2,1)S(1)}, u32[]{:S(2)}, u32[]{:S(2)}) collective-permute-start(bf16[256,1024]{1,0:T(8,128)(2,1)S(1)} %bitcast.3), channel_id=1, source_target_pairs={{0,1},{1,0},{2,3},{3,2},{4,5},{5,4},{6,7},{7,6},{8,9},{9,8},{10,11... | collective-permute-start | bytes 1572872 | tf_op jit(solution)/shard_map/ppermute | solution.py:138

commit v2 on v1

v2 whole, which is shorter than its diff:
```python
import functools
import itertools
import jax
import jax.numpy as jnp
from jax import lax
from jax.experimental import pallas as pl
from jax.experimental.pallas import tpu as pltpu
from jax.sharding import Mesh, PartitionSpec as P

F = 128
MIB = 1 << 20
TAIL = 16
AXES = ("z", "y", "x", "c")
SIZES = (8, 4, 4, 2)
f32, bf16 = jnp.float32, jnp.bfloat16
SMEM = pl.BlockSpec(memory_space=pltpu.SMEM)
VMEM = pl.BlockSpec(memory_space=pltpu.VMEM)
HBM = pl.BlockSpec(memory_space=pltpu.HBM)
OFFSETS = list(itertools.product((0, 1), repeat=3))


def iota(shape, dim):
    return lax.broadcasted_iota(jnp.int32, shape, dim)


def coefficients(hg_ref, tg_ref, k):
    hg = jnp.full((1, F), hg_ref[k], f32)
    tg = jnp.full((1, F), tg_ref[k], f32)
    discount = 1.0 - hg
    rate = discount * (1.0 - tg)
    return jnp.log(rate), jnp.sqrt(1.0 - rate * rate), discount * tg / rate


def powers(log_rate, steps):
    a = jnp.exp(iota((steps // 8, F), 0).astype(f32) * (8.0 * log_rate))
    b = jnp.exp(iota((8, F), 0).astype(f32) * log_rate)
    return (a[:, None, :] * b[None, :, :]).reshape(steps, F)


def ends_before(ended_row, steps):
    ended = jnp.broadcast_to(ended_row, (F, steps)).astype(bf16)
    below = (iota((steps, steps), 1) < iota((steps, steps), 0)).astype(f32).astype(bf16)
    return lax.dot_general(below, ended, (((1,), (1,)), ((), ())), preferred_element_type=f32)


def open_rows(ended_row, steps):
    total = jnp.sum(ended_row, axis=1, keepdims=True)
    return jnp.where(ends_before(ended_row, steps) == total, 1.0, 0.0)


def local_kernel(hg_hbm, tg_hbm, end_hbm, s_hbm, wf_hbm, w_hbm, r_ref, g_ref, msg_ref, thru_ref, open_ref,
                 hg_ref, tg_ref, end_ref, s_ref, wf_ref, w_ref, sems):
    blocks, _, blk = w_ref.shape
    steps = s_ref.shape[0]
    num_k = hg_ref.shape[0]
    copies = [
        pltpu.make_async_copy(a, b, sems.at[n])
        for n, (a, b) in enumerate(
            [(hg_hbm, hg_ref), (tg_hbm, tg_ref), (end_hbm, end_ref), (s_hbm, s_ref), (wf_hbm, wf_ref)]
            + [(w_hbm.at[:, i * blk : (i + 1) * blk], w_ref.at[i]) for i in range(blocks)]
        )
    ]
    for copy in copies:
        copy.start()
    for copy in copies[:3]:
        copy.wait()
    ended_row = end_ref[...].astype(f32)
    rows, cols = iota((steps, steps), 0), iota((steps, steps), 1)
    at_row = ends_before(ended_row, steps)
    ended = jnp.broadcast_to(ended_row, (steps, steps)).astype(bf16)
    above = (rows < cols).astype(f32).astype(bf16)
    at_col = jnp.dot(ended, above, preferred_element_type=f32)
    at_rows = jnp.concatenate([at_row] * (steps // F), axis=1)
    mask = jnp.where((at_rows == at_col) & (cols >= rows), 1.0, 0.0).astype(bf16)
    total = jnp.sum(ended_row, axis=1, keepdims=True)
    open_ref[...] = jnp.where(at_row == total, 1.0, 0.0)
    for z in range(msg_ref.shape[0]):
        msg_ref[z, num_k:, :] = jnp.broadcast_to(jnp.where(total == 0.0, 1.0, 0.0), (msg_ref.shape[1] - num_k, F))
    r_ref[steps:, :] = jnp.zeros((TAIL, r_ref.shape[1]), bf16)
    r_ref[steps:, :steps] = jnp.broadcast_to(ended_row, (TAIL, steps)).astype(bf16)

    for copy in copies[3:5]:
        copy.wait()
    s = s_ref[...]
    f = jnp.dot(s, wf_ref[...], preferred_element_type=f32)
    for i in range(blocks):
        copies[5 + i].wait()
        pred = jnp.dot(s, w_ref[i], preferred_element_type=f32).astype(bf16)
        scaled, backs, biased = [], [], []
        for j in range(blk // F):
            log_rate, scale, beta = coefficients(hg_ref, tg_ref, i * (blk // F) + j)
            thru_ref[i * (blk // F) + j : i * (blk // F) + j + 1, :] = jnp.exp(steps * log_rate)
            p = pred[:, j * F : (j + 1) * F].astype(f32)
            biased.append((p, beta * p))
            scaled.append(powers(log_rate, steps) * (scale * f + biased[j][1]))
            backs.append(powers(-log_rate, steps))
        scaled = jnp.concatenate(scaled, axis=1)
        high = scaled.astype(bf16)
        low = (scaled - high.astype(f32)).astype(bf16)
        sums = jnp.dot(mask, high, preferred_element_type=f32)
        sums = sums + jnp.dot(mask, low, preferred_element_type=f32)
        for j in range(blk // F):
            k = i * (blk // F) + j
            cols = slice(k * F, (k + 1) * F)
            h = backs[j] * sums[:, j * F : (j + 1) * F]
            g = h - biased[j][1]
            g_ref[:, cols] = g
            r_ref[:steps, cols] = (biased[j][0] - g).astype(bf16)
            for z in range(msg_ref.shape[0]):
                msg_ref[z, k : k + 1, :] = h[:1]


def later_kernel(msg_ref, thru_ref, h_ref):
    here = lax.axis_index("z")
    num_k = thru_ref.shape[0]
    later = jnp.zeros((num_k, F), f32)
    for z in range(msg_ref.shape[0] - 1, 0, -1):
        block = msg_ref[z, :num_k, :] + thru_ref[...] * msg_ref[z, num_k : num_k + 1, :] * later
        later = jnp.where(z > here, block, later)
    h_ref[...] = later


def backwards(log_rate, steps):
    return jnp.exp(steps * log_rate) * powers(-log_rate, steps)


def returns_kernel(hg_ref, tg_ref, h_ref, open_ref, g_ref, out_ref):
    steps = g_ref.shape[0]
    still = open_ref[...]
    for k in range(hg_ref.shape[0]):
        cols = slice(k * F, (k + 1) * F)
        decay = still * backwards(coefficients(hg_ref, tg_ref, k)[0], steps)
        out_ref[:, cols] = (g_ref[:, cols] + decay * h_ref[k : k + 1, :]).astype(bf16)


def grad_kernel(dz, hg_ref, tg_ref, s_ref, so_ref, r_ref, ro_ref, h_ref, ho_ref, open_ref, *outs):
    steps, width = s_ref.shape
    halves, quads, rows, cols = outs[0].shape
    num_k = h_ref.shape[0]
    per = cols // F
    z, y, x, c = (lax.axis_index(a) for a in AXES)
    py, px, pz = y % 2, x % 2, (z + dz) % 2
    tall = len(outs) * quads * rows
    r = iota((tall, 1), 0)
    part, quad = r // (quads * rows), (r // rows) % quads
    row_y = 2 * (quad // 2) + (part // 2 + py) % 2
    row_x = 2 * (quad % 2) + (part % 2 + px) % 2
    want = ((row_y * SIZES[2] + row_x) * SIZES[3] + c) * rows + r % rows
    pick = (want == iota((tall, width), 1)).astype(f32).astype(bf16)
    contract = (((1,), (1,)), ((), ()))
    st = lax.dot_general(pick, s_ref[...], contract, preferred_element_type=f32).astype(bf16)
    sto = lax.dot_general(pick, so_ref[...], contract, preferred_element_type=f32).astype(bf16)
    still = open_ref[...]
    still_o = open_rows(ro_ref[steps : steps + 1, :steps].astype(f32), steps)
    for half in range(halves):
        first = (2 * half + pz) * per
        mine, other = [], []
        for j in range(per):
            k = first + j
            at = pl.ds(pl.multiple_of(k * F, F), F)
            back = backwards(coefficients(hg_ref, tg_ref, k)[0], steps)
            mine.append((r_ref[:steps, at].astype(f32) - still * back * h_ref[pl.ds(k, 1), :]).astype(bf16))
            other.append((ro_ref[:steps, at].astype(f32) - still_o * back * ho_ref[pl.ds(k, 1), :]).astype(bf16))
        g = jnp.dot(st, jnp.concatenate(mine, axis=1), preferred_element_type=f32)
        g = g + jnp.dot(sto, jnp.concatenate(other, axis=1), preferred_element_type=f32)
        g = g.astype(bf16).reshape(len(outs), quads, rows, cols)
        for n, out in enumerate(outs):
            out[half] = g[n]


def cube_kernel(*refs):
    *ins, out_ref = refs
    for half in range(out_ref.shape[0]):
        total = ins[0][half].astype(f32)
        for ref in ins[1:]:
            total = total + ref[half].astype(f32)
        out_ref[half] = total.astype(out_ref.dtype)


def final_kernel(norm, x_ref, y_ref):
    y_ref[...] = jnp.sum(x_ref[...].astype(f32), axis=0) * norm


def params(mib=48):
    return pltpu.CompilerParams(vmem_limit_bytes=mib * MIB)


def flat(place):
    n = 0
    for i, size in zip(place, SIZES):
        n = n * size + i
    return n


def across(offset):
    pairs = []
    for place in itertools.product(*(range(n) for n in SIZES)):
        core = place[3]
        to = [
            i if not d else (i ^ 1 if core == 0 else ((i + 1) % n if i % 2 else (i - 1) % n))
            for i, d, n in zip(place, offset, SIZES)
        ]
        pairs.append((flat(place), flat(to + [core])))
    return pairs


def alike():
    return [
        [flat((2 * z + pz, 2 * y + py, 2 * x + px, c)) for z in range(4) for y in range(2) for x in range(2)]
        for c in range(2)
        for pz, py, px in OFFSETS
    ]


def body(states, episode_end, feature_head, successor_head, horizon_gap, trace_gap):
    steps, width = states.shape[1:]
    num_k = horizon_gap.shape[0]
    kf = successor_head.shape[1]
    nz, ny, nx, nc = SIZES
    s = states[0]
    swap = [(0, 1), (1, 0)]
    s_other = lax.ppermute(s, "c", swap)
    blk = 4 * F
    n = kf // blk
    shape = jax.ShapeDtypeStruct
    resid, g_local, msg, thru, still_open = pl.pallas_call(
        local_kernel,
        in_specs=[HBM] * 6,
        out_specs=[VMEM] * 5,
        out_shape=[
            shape((steps + TAIL, kf), bf16),
            shape((steps, kf), f32),
            shape((nz, num_k + 8, F), f32),
            shape((num_k, F), f32),
            shape((steps, F), f32),
        ],
        scratch_shapes=[
            pltpu.SMEM((num_k,), f32),
            pltpu.SMEM((num_k,), f32),
            pltpu.VMEM((1, steps), jnp.int32),
            pltpu.VMEM((steps, width), bf16),
            pltpu.VMEM((width, F), bf16),
            pltpu.VMEM((n, width, blk), bf16),
            pltpu.SemaphoreType.DMA((5 + n,)),
        ],
        compiler_params=params(),
        name="local",
    )(horizon_gap, trace_gap, episode_end, s, feature_head, successor_head)
    resid_other = lax.ppermute(resid, "c", swap)
    msg = lax.all_to_all(msg, "z", 0, 0, tiled=True)
    later = pl.pallas_call(
        later_kernel,
        in_specs=[VMEM] * 2,
        out_specs=VMEM,
        out_shape=shape((num_k, F), f32),
        name="later",
    )(msg, thru)
    later_other = lax.ppermute(later, "c", swap)
    rows, cols = width // (ny * nx * nc), kf // nz
    chunk = (nz // 2, ny * nx // 4, rows, cols)

    def grads(dz):
        return pl.pallas_call(
            functools.partial(grad_kernel, dz),
            in_specs=[SMEM] * 2 + [VMEM] * 7,
            out_specs=[VMEM] * 4,
            out_shape=[shape(chunk, bf16)] * 4,
            compiler_params=params(),
            name="grad",
        )(horizon_gap, trace_gap, s, s_other, resid, resid_other, later, later_other, still_open)

    chunks = dict(zip([o for o in OFFSETS if o[0] == 1], grads(1)))
    chunks |= dict(zip([o for o in OFFSETS if o[0] == 0], grads(0)))
    sums = [chunks[0, 0, 0]] + [lax.ppermute(chunks[o], AXES, across(o)) for o in reversed(OFFSETS[1:])]
    returns = pl.pallas_call(
        returns_kernel,
        in_specs=[SMEM] * 2 + [VMEM] * 3,
        out_specs=VMEM,
        out_shape=shape((steps, kf), bf16),
        compiler_params=params(),
        name="returns",
    )(horizon_gap, trace_gap, later, still_open, g_local)
    grad = pl.pallas_call(
        cube_kernel,
        in_specs=[VMEM] * 8,
        out_specs=VMEM,
        out_shape=shape(chunk, bf16),
        compiler_params=params(),
        name="sum_cube",
    )(*sums)
    grad = lax.all_to_all(grad.reshape(-1, rows, cols), AXES, 0, 0, axis_index_groups=alike())
    norm = float(steps * nz * ny * nx * nc) ** -0.5
    head_grad = pl.pallas_call(
        functools.partial(final_kernel, norm),
        in_specs=[VMEM],
        out_specs=VMEM,
        out_shape=shape((rows, cols), f32),
        name="sum_rest",
    )(grad)
    return returns[None], head_grad


def solution(mesh):
    grid = Mesh(mesh.devices.reshape(SIZES), AXES)
    traj = ("y", "x", "c")
    return jax.shard_map(
        body,
        mesh=grid,
        in_specs=(P(traj, "z", None), P(traj, "z"), P(), P(), P(), P()),
        out_specs=(P(traj, "z", None), P(traj, "z")),
        check_vma=False,
    )
```

time: 90.5 us -> 82.2 us (0.908)
  blocking collectives: 61.7 us -> 13.8 us
  starting transfers between devices: 2.11 us -> 24 us
  waiting for transfers between devices: 2.99 us -> 19.9 us
  Pallas kernels: 16 us -> 17 us
    all_to_all x2 -> x0, blocking collectives: 45.1 us -> none  [the longest x1 34.1 us: body(): grad = lax.all_to_all(grad, ('y', 'x'), 0, 0, tiled=True)]
    ppermute x0 -> x8, starting transfers between devices: none -> 17.2 us  [the longest x7 15.2 us: body(): lax.ppermute(chunks[o], AXES, across(o))]
    all_to_all x0 -> x1, waiting for transfers between devices: none -> 12.6 us  [body(): lax.all_to_all(grad.reshape(-1, rows, cols), AXES, 0, 0, axis_index_group...]
    ppermute x0 -> x8, waiting for transfers between devices: none -> 7.29 us  [the longest x7 6.25 us: body(): lax.ppermute(chunks[o], AXES, across(o))]
    all_to_all x0 -> x1, starting transfers between devices: none -> 3.53 us  [body(): lax.all_to_all(grad.reshape(-1, rows, cols), AXES, 0, 0, axis_index_group...]
    ppermute x1, waiting for transfers between devices: 2.99 us -> 0.01 us  [body(): s_other = lax.ppermute(s, 'c', swap)]
    all_to_all x1, blocking collectives: 16.6 us -> 13.8 us  [body(): msg = lax.all_to_all(msg, 'z', 0, 0, tiled=True)]
    ppermute x1, starting transfers between devices: 2.07 us -> 3.24 us  [body(): resid_other = lax.ppermute(resid, 'c', swap)]
  transfers between devices with their start and end apart: 2 -> 11, of which waited for: 1 -> 6; matrix products, arithmetic and copies ran while one was open for 0% -> 0% of each run, Pallas kernels for 0% -> 8%
where the time goes in v2:
time: 82.2 us; the launch traced here: 81.7 us
  starting transfers between devices  24 us (29%)
  waiting for transfers between devices  19.9 us (24%)
  Pallas kernels  17 us (21%)
  blocking collectives  13.8 us (17%)
  local copies, waits for them, and re-layouts  6.26 us (8%)
    ppermute x7, starting transfers between devices, body(): lax.ppermute(chunks[o], AXES, across(o))  15.2 us
    all_to_all x1, blocking collectives, body(): msg = lax.all_to_all(msg, 'z', 0, 0, tiled=True)  13.8 us
    all_to_all x1, waiting for transfers between devices, body(): lax.all_to_all(grad.reshape(-1, rows, cols), AXES, 0, 0, axis_index_group...  12.6 us
    unnamed x24, local copies, waits for them, and re-layouts  6.26 us
    ppermute x7, waiting for transfers between devices, body(): lax.ppermute(chunks[o], AXES, across(o))  6.25 us
    pallas_call x2, Pallas kernels, grads(): pl.pallas_call(functools.partial(grad_kernel, dz), in_specs=[SMEM] * 2 +...  5.89 us
    pallas_call x1, Pallas kernels, body(): pl.pallas_call(local_kernel, in_specs=[HBM] * 6, out_specs=[VMEM] * 5, ou...  4.83 us
    all_to_all x1, starting transfers between devices, body(): lax.all_to_all(grad.reshape(-1, rows, cols), AXES, 0, 0, axis_index_group...  3.53 us
  transfers between devices with their start and end apart: 11, of which 6 were waited for; matrix products, arithmetic and copies ran while one was open for 0% of the time, Pallas kernels for 8%

profile of v2, /device:TPU:1, one launch (start us, length us, event | category | flops | bytes accessed | tf_op | source)
XLA Modules:
  0.0 81.7 jit_solution(10106386395939319385)
XLA Ops:
  0.6 0.0 copy-start.2
  0.6 0.9 %copy-done.2 = bf16[1024,128]{1,0:T(8,128)(2,1)S(1)} copy-done((bf16[1024,128]{1,0:T(8,128)(2,1)S(1)}, bf16[1024,128]{1,0:T(8,128)(2,1)}, u32[]{:S(2)}) %copy-start.2) | copy-done | bytes 262168
  1.6 0.0 copy-start.5
  1.6 0.7 copy-done.5
  2.2 0.7 copy-done.7
  2.9 0.7 copy-done.10
  3.6 4.8 %local.1 = (bf16[272,2048]{1,0:T(8,128)(2,1)S(1)}, f32[256,2048]{1,0:T(8,128)S(1)}, f32[8,24,128]{2,1,0:T(8,128)S(1)}, f32[16,128]{1,0:T(8,128)S(1)}, f32[256,128]{1,0:T(8,128)S(1)}) custom-call(f32[16]{0:T(128)S(1)} %copy-done.5, f32[16]{0:T(128)S(1)} %copy-done.7, s32[1,256]{1,0:T(1,128)S(1)} %copy-done.10, bf16[256,1024]{1,0:T(8,128)(2,1)} %bitcast.s_hbm.s_ref, ...), custom_call_target="tpu_custom_call" | custom-call | tf_op jit(solution)/shard_map/local/pallas_call | solution.py:226
  8.4 0.0 copy-start
  8.4 1.3 %copy-done = f32[256,2048]{1,0:T(8,128)} copy-done((f32[256,2048]{1,0:T(8,128)}, f32[256,2048]{1,0:T(8,128)S(1)}, u32[]{:S(2)}) %copy-start) | copy-done | bytes 2097176
  9.7 0.6 copy-done.9
  10.3 3.2 %collective-permute-start.1 = (bf16[272,2048]{1,0:T(8,128)(2,1)S(1)}, bf16[272,2048]{1,0:T(8,128)(2,1)S(1)}, u32[]{:S(2)}, u32[]{:S(2)}) collective-permute-start(bf16[272,2048]{1,0:T(8,128)(2,1)S(1)} %get-tuple-element.19.r_ref), channel_id=1, source_target_pairs={{0,1},{1,0},{2,3},{3,2},{4,5},{5,4},{6,7},{7,6},{8,9},{9,8},{10,11... | collective-permute-start | bytes 3342344 | tf_op jit(solution)/shard_map/ppermute | solution.py:249
  13.6 0.0 collective-permute-start
  13.6 13.8 %all_to_all.10.msg_ref = f32[8,24,128]{2,1,0:T(8,128)} all-to-all(f32[8,24,128]{2,1,0:T(8,128)S(1)} %get-tuple-element.15), channel_id=1, replica_groups=mesh['z'=8,'y'=4,'x'=4,'c'=2] {'z'}, dimensions={0} | all-to-all | bytes 196608 | tf_op jit(solution)/shard_map/all_to_all | solution.py:250
  27.4 1.5 %later.1.h_ref = f32[16,128]{1,0:T(8,128)} custom-call(f32[8,24,128]{2,1,0:T(8,128)} %all_to_all.10.msg_ref, f32[16,128]{1,0:T(8,128)} %copy-done.9), custom_call_target="tpu_custom_call" | custom-call | tf_op jit(solution)/shard_map/later/pallas_call | solution.py:251
  28.9 2.1 %collective-permute-start.2 = (f32[16,128]{1,0:T(8,128)}, f32[16,128]{1,0:T(8,128)S(1)}, u32[]{:S(2)}, u32[]{:S(2)}) collective-permute-start(f32[16,128]{1,0:T(8,128)} %later.1.h_ref), channel_id=1, source_target_pairs={{0,1},{1,0},{2,3},{3,2},{4,5},{5,4},{6,7},{7,6},{8,9},{9,8},{10,11... | collective-permute-start | bytes 24584 | tf_op jit(solution)/shard_map/ppermute | solution.py:258
  31.0 1.0 %collective-permute-done.2.ho_ref = f32[16,128]{1,0:T(8,128)S(1)} collective-permute-done((f32[16,128]{1,0:T(8,128)}, f32[16,128]{1,0:T(8,128)S(1)}, u32[]{:S(2)}, u32[]{:S(2)}) %collective-permute-start.2) | collective-permute-done | bytes 8224 | tf_op jit(solution)/shard_map/ppermute | solution.py:258
  32.0 0.0 collective-permute-done.so_ref
  32.0 0.0 collective-permute-done.1.ro_ref
  32.0 0.0 copy-done.6
  32.0 0.0 copy-done.8
  32.0 0.0 copy-start.3
  32.0 0.7 copy-done.3
  32.7 3.0 %grad.3 = (bf16[4,4,32,256]{3,2,1,0:T(8,128)(2,1)S(1)}, bf16[4,4,32,256]{3,2,1,0:T(8,128)(2,1)S(1)}, bf16[4,4,32,256]{3,2,1,0:T(8,128)(2,1)S(1)}, bf16[4,4,32,256]{3,2,1,0:T(8,128)(2,1)S(1)}) custom-call(f32[16]{0:T(128)S(1)} %copy-done.6, f32[16]{0:T(128)S(1)} %copy-done.8, bf16[256,1024]{1,0:T(8,128)(2,1)} %bitcast.s_hbm.s_ref, ...), custom_call_target="tpu_custom_call" | custom-call | tf_op jit(solution)/shard_map/grad/pallas_call | solution.py:263
  35.7 4.5 %collective-permute-start.3 = (bf16[4,4,32,256]{3,2,1,0:T(8,128)(2,1)S(1)}, bf16[4,4,32,256]{3,2,1,0:T(8,128)(2,1)S(1)}, u32[]{:S(2)}, u32[]{:S(2)}) collective-permute-start(bf16[4,4,32,256]{3,2,1,0:T(8,128)(2,1)S(1)} %get-tuple-element.21), channel_id=1, source_target_pairs={{0,42},{1,255},{2,40},{3,253},{4,46},{5,251},{6,44},{7,249},{8,34}... | collective-permute-start | bytes 786440 | tf_op jit(solution)/shard_map/ppermute | solution.py:274
  40.2 2.6 %collective-permute-start.4 = (bf16[4,4,32,256]{3,2,1,0:T(8,128)(2,1)S(1)}, bf16[4,4,32,256]{3,2,1,0:T(8,128)(2,1)S(1)}, u32[]{:S(2)}, u32[]{:S(2)}) collective-permute-start(bf16[4,4,32,256]{3,2,1,0:T(8,128)(2,1)S(1)} %get-tuple-element.22), channel_id=1, source_target_pairs={{0,40},{1,249},{2,42},{3,251},{4,44},{5,253},{6,46},{7,255},{8,32}... | collective-permute-start | bytes 786440 | tf_op jit(solution)/shard_map/ppermute | solution.py:274
  42.7 0.4 collective-permute-start.5
  43.2 2.1 %collective-permute-start.6 = (bf16[4,4,32,256]{3,2,1,0:T(8,128)(2,1)S(1)}, bf16[4,4,32,256]{3,2,1,0:T(8,128)(2,1)S(1)}, u32[]{:S(2)}, u32[]{:S(2)}) collective-permute-start(bf16[4,4,32,256]{3,2,1,0:T(8,128)(2,1)S(1)} %get-tuple-element.24), channel_id=1, source_target_pairs={{0,32},{1,225},{2,34},{3,227},{4,36},{5,229},{6,38},{7,231},{8,40}... | collective-permute-start | bytes 786440 | tf_op jit(solution)/shard_map/ppermute | solution.py:274
  45.3 2.9 %grad.2 = (bf16[4,4,32,256]{3,2,1,0:T(8,128)(2,1)S(1)}, bf16[4,4,32,256]{3,2,1,0:T(8,128)(2,1)S(1)}, bf16[4,4,32,256]{3,2,1,0:T(8,128)(2,1)S(1)}, bf16[4,4,32,256]{3,2,1,0:T(8,128)(2,1)S(1)}) custom-call(f32[16]{0:T(128)S(1)} %copy-done.6, f32[16]{0:T(128)S(1)} %copy-done.8, bf16[256,1024]{1,0:T(8,128)(2,1)} %bitcast.s_hbm.s_ref, ...), custom_call_target="tpu_custom_call" | custom-call | tf_op jit(solution)/shard_map/grad/pallas_call | solution.py:263
  48.3 0.0 copy-start.1
  48.3 0.0 copy-start.4
  48.3 5.0 %collective-permute-start.7 = (bf16[4,4,32,256]{3,2,1,0:T(8,128)(2,1)S(1)}, bf16[4,4,32,256]{3,2,1,0:T(8,128)(2,1)S(1)}, u32[]{:S(2)}, u32[]{:S(2)}) collective-permute-start(bf16[4,4,32,256]{3,2,1,0:T(8,128)(2,1)S(1)} %get-tuple-element.25), channel_id=1, source_target_pairs={{0,10},{1,31},{2,8},{3,29},{4,14},{5,27},{6,12},{7,25},{8,2},{9,23... | collective-permute-start | bytes 786440 | tf_op jit(solution)/shard_map/ppermute | solution.py:274
  53.3 0.0 collective-permute-done.3.refs_1_
  53.3 0.0 collective-permute-start.8
  53.3 0.0 collective-permute-done.4.refs_2_
  53.3 0.5 collective-permute-start.9
  53.8 0.0 collective-permute-done.5.refs_3_
  53.8 1.4 %collective-permute-done.6.refs_4_ = bf16[4,4,32,256]{3,2,1,0:T(8,128)(2,1)S(1)} collective-permute-done((bf16[4,4,32,256]{3,2,1,0:T(8,128)(2,1)S(1)}, bf16[4,4,32,256]{3,2,1,0:T(8,128)(2,1)S(1)}, u32[]{:S(2)}, u32[]{:S(2)}) %collective-permute-start.6) | collective-permute-done | bytes 262176 | tf_op jit(solution)/shard_map/ppermute | solution.py:274
  55.3 1.8 %collective-permute-done.7.refs_5_ = bf16[4,4,32,256]{3,2,1,0:T(8,128)(2,1)S(1)} collective-permute-done((bf16[4,4,32,256]{3,2,1,0:T(8,128)(2,1)S(1)}, bf16[4,4,32,256]{3,2,1,0:T(8,128)(2,1)S(1)}, u32[]{:S(2)}, u32[]{:S(2)}) %collective-permute-start.7) | collective-permute-done | bytes 262176 | tf_op jit(solution)/shard_map/ppermute | solution.py:274
  57.1 2.8 %collective-permute-done.8.refs_6_ = bf16[4,4,32,256]{3,2,1,0:T(8,128)(2,1)S(1)} collective-permute-done((bf16[4,4,32,256]{3,2,1,0:T(8,128)(2,1)S(1)}, bf16[4,4,32,256]{3,2,1,0:T(8,128)(2,1)S(1)}, u32[]{:S(2)}, u32[]{:S(2)}) %collective-permute-start.8) | collective-permute-done | bytes 262176 | tf_op jit(solution)/shard_map/ppermute | solution.py:274
  59.9 0.2 collective-permute-done.9.refs_7_
  60.1 1.0 %sum_cube.1 = bf16[4,4,32,256]{3,2,1,0:T(8,128)(2,1)} custom-call(bf16[4,4,32,256]{3,2,1,0:T(8,128)(2,1)S(1)} %get-tuple-element.20.refs_0_, bf16[4,4,32,256]{3,2,1,0:T(8,128)(2,1)S(1)} %collective-permute-done.3.refs_1_, bf16[4,4,32,256]{3,2,1,0:T(8,128)(2,1)S(1)} %collective-permute-done.4.refs_2_, ...), custom_call_target="tpu_custom_call" | custom-call | tf_op jit(solution)/shard_map/sum_cube/pallas_call | solution.py:283
  61.1 3.5 %all-to-all-start.1 = ((bf16[16,32,256]{2,1,0:T(8,128)(2,1)}), bf16[16,32,256]{2,1,0:T(8,128)(2,1)S(1)}, u32[]{:S(2)}, u32[]{:S(2)}) async-start(bf16[16,32,256]{2,1,0:T(8,128)(2,1)} %bitcast.2), calls=%async_computation.1 | async-start | bytes 524288 | tf_op jit(solution)/shard_map/all_to_all | solution.py:291
  64.6 0.0 copy-done.1
  64.6 0.0 copy-done.4
  64.6 2.1 %returns.1 = bf16[256,2048]{1,0:T(8,128)(2,1)} custom-call(f32[16]{0:T(128)S(1)} %copy-done.6, f32[16]{0:T(128)S(1)} %copy-done.8, f32[16,128]{1,0:T(8,128)S(1)} %copy-done.4, f32[256,128]{1,0:T(8,128)S(1)} %get-tuple-element.17.open_ref, f32[256,2048]{1,0:T(8,128)S(1)} %copy-done.1), custom_call_target="tpu_custom_call" | custom-call | tf_op jit(solution)/shard_map/returns/pallas_call | solution.py:275
  66.8 12.6 %all-to-all-done.1.x_ref = bf16[16,32,256]{2,1,0:T(8,128)(2,1)S(1)} async-done(((bf16[16,32,256]{2,1,0:T(8,128)(2,1)}), bf16[16,32,256]{2,1,0:T(8,128)(2,1)S(1)}, u32[]{:S(2)}, u32[]{:S(2)}) %all-to-all-start.1) | async-done | bytes 262176 | tf_op jit(solution)/shard_map/all_to_all | solution.py:291
  79.4 0.7 copy-done.11
  80.1 1.6 %sum_rest.1 = f32[32,256]{1,0:T(8,128)} custom-call(bf16[16,32,256]{2,1,0:T(8,128)(2,1)} %copy-done.11), custom_call_target="tpu_custom_call" | custom-call | tf_op jit(solution)/shard_map/sum_rest/pallas_call | solution.py:293
  (6 shorter events, 0.0 us)
Async XLA Ops:
  0.6 1.0 %copy-start.2 = (bf16[1024,128]{1,0:T(8,128)(2,1)S(1)}, bf16[1024,128]{1,0:T(8,128)(2,1)}, u32[]{:S(2)}) copy-start(bf16[1024,128]{1,0:T(8,128)(2,1)} %wf_hbm.1) | copy-start | bytes 786436
  1.6 0.7 copy-start.5
  2.2 0.7 copy-start.7
  2.9 0.7 copy-start.10
  3.6 28.4 %copy-start.6 = (f32[16]{0:T(128)S(1)}, f32[16]{0:T(128)}, u32[]{:S(2)}) copy-start(f32[16]{0:T(128)} %hg_ref.5) | copy-start | bytes 196
  3.6 28.4 %copy-start.8 = (f32[16]{0:T(128)S(1)}, f32[16]{0:T(128)}, u32[]{:S(2)}) copy-start(f32[16]{0:T(128)} %tg_ref.5) | copy-start | bytes 196
  8.4 1.3 %copy-start = (f32[256,2048]{1,0:T(8,128)}, f32[256,2048]{1,0:T(8,128)S(1)}, u32[]{:S(2)}) copy-start(f32[256,2048]{1,0:T(8,128)S(1)} %get-tuple-element.18.g_ref) | copy-start | bytes 6291460
  9.7 0.6 copy-start.9
  10.3 21.7 %collective-permute-start.1 = (bf16[272,2048]{1,0:T(8,128)(2,1)S(1)}, bf16[272,2048]{1,0:T(8,128)(2,1)S(1)}, u32[]{:S(2)}, u32[]{:S(2)}) collective-permute-start(bf16[272,2048]{1,0:T(8,128)(2,1)S(1)} %get-tuple-element.19.r_ref), channel_id=1, source_target_pairs={{0,1},{1,0},{2,3},{3,2},{4,5},{5,4},{6,7},{7,6},{8,9},{9,8},{10,11... | collective-permute-start | bytes 3342344 | tf_op jit(solution)/shard_map/ppermute | solution.py:249
  13.6 18.4 %collective-permute-start = (bf16[256,1024]{1,0:T(8,128)(2,1)}, bf16[256,1024]{1,0:T(8,128)(2,1)S(1)}, u32[]{:S(2)}, u32[]{:S(2)}) collective-permute-start(bf16[256,1024]{1,0:T(8,128)(2,1)} %bitcast.s_hbm.s_ref), channel_id=1, source_target_pairs={{0,1},{1,0},{2,3},{3,2},{4,5},{5,4},{6,7},{7,6},{8,9},{9,8},{10,11... | collective-permute-start | bytes 1572872 | tf_op jit(solution)/shard_map/ppermute | solution.py:222
  28.9 3.1 %collective-permute-start.2 = (f32[16,128]{1,0:T(8,128)}, f32[16,128]{1,0:T(8,128)S(1)}, u32[]{:S(2)}, u32[]{:S(2)}) collective-permute-start(f32[16,128]{1,0:T(8,128)} %later.1.h_ref), channel_id=1, source_target_pairs={{0,1},{1,0},{2,3},{3,2},{4,5},{5,4},{6,7},{7,6},{8,9},{9,8},{10,11... | collective-permute-start | bytes 24584 | tf_op jit(solution)/shard_map/ppermute | solution.py:258
  32.0 0.7 copy-start.3
  35.7 17.6 %collective-permute-start.3 = (bf16[4,4,32,256]{3,2,1,0:T(8,128)(2,1)S(1)}, bf16[4,4,32,256]{3,2,1,0:T(8,128)(2,1)S(1)}, u32[]{:S(2)}, u32[]{:S(2)}) collective-permute-start(bf16[4,4,32,256]{3,2,1,0:T(8,128)(2,1)S(1)} %get-tuple-element.21), channel_id=1, source_target_pairs={{0,42},{1,255},{2,40},{3,253},{4,46},{5,251},{6,44},{7,249},{8,34}... | collective-permute-start | bytes 786440 | tf_op jit(solution)/shard_map/ppermute | solution.py:274
  40.2 13.2 %collective-permute-start.4 = (bf16[4,4,32,256]{3,2,1,0:T(8,128)(2,1)S(1)}, bf16[4,4,32,256]{3,2,1,0:T(8,128)(2,1)S(1)}, u32[]{:S(2)}, u32[]{:S(2)}) collective-permute-start(bf16[4,4,32,256]{3,2,1,0:T(8,128)(2,1)S(1)} %get-tuple-element.22), channel_id=1, source_target_pairs={{0,40},{1,249},{2,42},{3,251},{4,44},{5,253},{6,46},{7,255},{8,32}... | collective-permute-start | bytes 786440 | tf_op jit(solution)/shard_map/ppermute | solution.py:274
  42.7 11.1 %collective-permute-start.5 = (bf16[4,4,32,256]{3,2,1,0:T(8,128)(2,1)S(1)}, bf16[4,4,32,256]{3,2,1,0:T(8,128)(2,1)S(1)}, u32[]{:S(2)}, u32[]{:S(2)}) collective-permute-start(bf16[4,4,32,256]{3,2,1,0:T(8,128)(2,1)S(1)} %get-tuple-element.23), channel_id=1, source_target_pairs={{0,34},{1,231},{2,32},{3,229},{4,38},{5,227},{6,36},{7,225},{8,42}... | collective-permute-start | bytes 786440 | tf_op jit(solution)/shard_map/ppermute | solution.py:274
  43.2 12.1 %collective-permute-start.6 = (bf16[4,4,32,256]{3,2,1,0:T(8,128)(2,1)S(1)}, bf16[4,4,32,256]{3,2,1,0:T(8,128)(2,1)S(1)}, u32[]{:S(2)}, u32[]{:S(2)}) collective-permute-start(bf16[4,4,32,256]{3,2,1,0:T(8,128)(2,1)S(1)} %get-tuple-element.24), channel_id=1, source_target_pairs={{0,32},{1,225},{2,34},{3,227},{4,36},{5,229},{6,38},{7,231},{8,40}... | collective-permute-start | bytes 786440 | tf_op jit(solution)/shard_map/ppermute | solution.py:274
  48.3 16.3 %copy-start.1 = (f32[256,2048]{1,0:T(8,128)S(1)}, f32[256,2048]{1,0:T(8,128)}, u32[]{:S(2)}) copy-start(f32[256,2048]{1,0:T(8,128)} %copy-done) | copy-start | bytes 6291460
  48.3 16.3 %copy-start.4 = (f32[16,128]{1,0:T(8,128)S(1)}, f32[16,128]{1,0:T(8,128)}, u32[]{:S(2)}) copy-start(f32[16,128]{1,0:T(8,128)} %later.1.h_ref) | copy-start | bytes 24580
  48.3 8.8 %collective-permute-start.7 = (bf16[4,4,32,256]{3,2,1,0:T(8,128)(2,1)S(1)}, bf16[4,4,32,256]{3,2,1,0:T(8,128)(2,1)S(1)}, u32[]{:S(2)}, u32[]{:S(2)}) collective-permute-start(bf16[4,4,32,256]{3,2,1,0:T(8,128)(2,1)S(1)} %get-tuple-element.25), channel_id=1, source_target_pairs={{0,10},{1,31},{2,8},{3,29},{4,14},{5,27},{6,12},{7,25},{8,2},{9,23... | collective-permute-start | bytes 786440 | tf_op jit(solution)/shard_map/ppermute | solution.py:274
  53.3 6.6 %collective-permute-start.8 = (bf16[4,4,32,256]{3,2,1,0:T(8,128)(2,1)S(1)}, bf16[4,4,32,256]{3,2,1,0:T(8,128)(2,1)S(1)}, u32[]{:S(2)}, u32[]{:S(2)}) collective-permute-start(bf16[4,4,32,256]{3,2,1,0:T(8,128)(2,1)S(1)} %get-tuple-element.26), channel_id=1, source_target_pairs={{0,8},{1,25},{2,10},{3,27},{4,12},{5,29},{6,14},{7,31},{8,0},{9,17... | collective-permute-start | bytes 786440 | tf_op jit(solution)/shard_map/ppermute | solution.py:274
  53.3 6.8 %collective-permute-start.9 = (bf16[4,4,32,256]{3,2,1,0:T(8,128)(2,1)S(1)}, bf16[4,4,32,256]{3,2,1,0:T(8,128)(2,1)S(1)}, u32[]{:S(2)}, u32[]{:S(2)}) collective-permute-start(bf16[4,4,32,256]{3,2,1,0:T(8,128)(2,1)S(1)} %get-tuple-element.27), channel_id=1, source_target_pairs={{0,2},{1,7},{2,0},{3,5},{4,6},{5,3},{6,4},{7,1},{8,10},{9,15},{10,... | collective-permute-start | bytes 786440 | tf_op jit(solution)/shard_map/ppermute | solution.py:274
  61.1 18.3 %all-to-all-start.1 = ((bf16[16,32,256]{2,1,0:T(8,128)(2,1)}), bf16[16,32,256]{2,1,0:T(8,128)(2,1)S(1)}, u32[]{:S(2)}, u32[]{:S(2)}) async-start(bf16[16,32,256]{2,1,0:T(8,128)(2,1)} %bitcast.2), calls=%async_computation.1 | async-start | bytes 524288 | tf_op jit(solution)/shard_map/all_to_all | solution.py:291
  79.4 0.7 copy-start.11

commit v3 on v2

v3 whole, which is shorter than its diff:
```python
import functools
import itertools
import jax
import jax.numpy as jnp
from jax import lax
from jax.experimental import pallas as pl
from jax.experimental.pallas import tpu as pltpu
from jax.sharding import Mesh, PartitionSpec as P

F = 128
MIB = 1 << 20
AXES = ("z", "y", "x", "c")
SIZES = (8, 4, 4, 2)
f32, bf16 = jnp.float32, jnp.bfloat16
SMEM = pl.BlockSpec(memory_space=pltpu.SMEM)
VMEM = pl.BlockSpec(memory_space=pltpu.VMEM)
HBM = pl.BlockSpec(memory_space=pltpu.HBM)
OFFSETS = list(itertools.product((0, 1), repeat=3))
ORDER = [(1, 0, 0), (0, 1, 0), (0, 0, 1), (1, 1, 1), (1, 1, 0), (1, 0, 1), (0, 1, 1)]


def iota(shape, dim):
    return lax.broadcasted_iota(jnp.int32, shape, dim)


def coefficients(hg_ref, tg_ref, k):
    hg = jnp.full((1, F), hg_ref[k], f32)
    tg = jnp.full((1, F), tg_ref[k], f32)
    discount = 1.0 - hg
    rate = discount * (1.0 - tg)
    return jnp.log(rate), jnp.sqrt(1.0 - rate * rate), discount * tg / rate


def powers(log_rate, steps):
    a = jnp.exp(iota((steps // 8, F), 0).astype(f32) * (8.0 * log_rate))
    b = jnp.exp(iota((8, F), 0).astype(f32) * log_rate)
    return (a[:, None, :] * b[None, :, :]).reshape(steps, F)


def ends_before(ended_row, steps):
    ended = jnp.broadcast_to(ended_row, (F, steps)).astype(bf16)
    below = (iota((steps, steps), 1) < iota((steps, steps), 0)).astype(f32).astype(bf16)
    return lax.dot_general(below, ended, (((1,), (1,)), ((), ())), preferred_element_type=f32)


def place_in_cube(i, core):
    gray, half = (i ^ (i >> 1)) & 1, i >> 1
    return (gray, half) if core == 0 else (half, gray)


def local_kernel(hg_hbm, tg_hbm, end_hbm, s_hbm, wf_hbm, w_hbm, r_ref, st_ref, g_ref, msg_ref, rate_ref, open_ref,
                 hg_ref, tg_ref, end_ref, s_ref, wf_ref, w_ref, sems):
    blocks, _, blk = w_ref.shape
    steps, width = s_ref.shape
    num_k = hg_ref.shape[0]
    kf = blocks * blk
    copies = [
        pltpu.make_async_copy(a, b, sems.at[n])
        for n, (a, b) in enumerate(
            [(hg_hbm, hg_ref), (tg_hbm, tg_ref), (end_hbm, end_ref), (s_hbm, s_ref), (wf_hbm, wf_ref)]
            + [(w_hbm.at[:, i * blk : (i + 1) * blk], w_ref.at[i]) for i in range(blocks)]
        )
    ]
    for copy in copies:
        copy.start()
    for copy in copies[:3]:
        copy.wait()
    ended_row = end_ref[...].astype(f32)
    rows, cols = iota((steps, steps), 0), iota((steps, steps), 1)
    at_row = ends_before(ended_row, steps)
    ended = jnp.broadcast_to(ended_row, (steps, steps)).astype(bf16)
    above = (rows < cols).astype(f32).astype(bf16)
    at_col = jnp.dot(ended, above, preferred_element_type=f32)
    at_rows = jnp.concatenate([at_row] * (steps // F), axis=1)
    mask = jnp.where((at_rows == at_col) & (cols >= rows), 1.0, 0.0).astype(bf16)
    total = jnp.sum(ended_row, axis=1, keepdims=True)
    still = jnp.where(at_row == total, 1.0, 0.0)
    open_ref[...] = still
    for z in range(msg_ref.shape[0]):
        msg_ref[z, num_k:, :] = jnp.broadcast_to(jnp.where(total == 0.0, 1.0, 0.0), (msg_ref.shape[1] - num_k, F))
    lane = iota((1, F), 1)
    by_lane = jnp.zeros((1, F), f32)
    for k in range(num_k):
        log_rate = coefficients(hg_ref, tg_ref, k)[0]
        rate_ref[k : k + 1, :] = log_rate
        by_lane = jnp.where(lane % num_k == k, log_rate, by_lane)
    rate_ref[num_k:, :] = jnp.broadcast_to(by_lane, (8, F))
    r_ref[:, kf : kf + F] = (still * backwards(by_lane, steps)).astype(bf16)

    for copy in copies[3:5]:
        copy.wait()
    s = s_ref[...]
    f = jnp.dot(s, wf_ref[...], preferred_element_type=f32)
    per = blk // F

    def predict(i):
        copies[5 + i].wait()
        return jnp.dot(s, w_ref[i], preferred_element_type=f32).astype(bf16)

    def turn():
        st = s.T
        here = lax.axis_index("c")
        label = {(a, core): place_in_cube(lax.axis_index(a), core)[0] for a in ("y", "x") for core in range(2)}
        tall = st_ref.shape[0] // (SIZES[1] * SIZES[2])
        for n in range(st.shape[0] // tall):
            y, x, core = n // (SIZES[2] * SIZES[3]), n // SIZES[3] % SIZES[2], n % SIZES[3]
            (ly, iy), (lx, ix) = place_in_cube(y, core), place_in_cube(x, core)
            at = ((ly ^ label["y", core]) * 2 + (lx ^ label["x", core])) * 4 + iy * 2 + ix
            part = st[n * tall : (n + 1) * tall, :]

            @pl.when(here == core)
            def _():
                st_ref[pl.ds(pl.multiple_of(at * tall, tall), tall), :] = part

            @pl.when(here != core)
            def _():
                left = kf + F + at // (steps // tall) * steps
                r_ref[pl.ds(pl.multiple_of(at % (steps // tall) * tall, tall), tall), pl.ds(pl.multiple_of(left, F), steps)] = part

    turn()
    following = predict(0)
    for i in range(blocks):
        pred = following
        if i + 1 < blocks:
            following = predict(i + 1)
        scaled, backs, biased = [], [], []
        for j in range(per):
            log_rate, scale, beta = coefficients(hg_ref, tg_ref, i * per + j)
            p = pred[:, j * F : (j + 1) * F].astype(f32)
            biased.append((p, beta * p))
            scaled.append(powers(log_rate, steps) * (scale * f + biased[j][1]))
            backs.append(powers(-log_rate, steps))
        scaled = jnp.concatenate(scaled, axis=1)
        high = scaled.astype(bf16)
        low = (scaled - high.astype(f32)).astype(bf16)
        sums = jnp.dot(mask, high, preferred_element_type=f32)
        sums = sums + jnp.dot(mask, low, preferred_element_type=f32)
        for j in range(per):
            k = i * per + j
            cols = slice(k * F, (k + 1) * F)
            h = backs[j] * sums[:, j * F : (j + 1) * F]
            g = h - biased[j][1]
            g_ref[:, cols] = g
            r_ref[:, cols] = (biased[j][0] - g).astype(bf16)
            for z in range(msg_ref.shape[0]):
                msg_ref[z, k : k + 1, :] = h[:1]


def carry_in(msg_ref, rate_ref, steps):
    here = lax.axis_index("z")
    num_k = rate_ref.shape[0] - 8
    through = jnp.exp(steps * rate_ref[:num_k, :])
    later = jnp.zeros((num_k, F), f32)
    for z in range(msg_ref.shape[0] - 1, 0, -1):
        block = msg_ref[z, :num_k, :] + through * msg_ref[z, num_k : num_k + 1, :] * later
        later = jnp.where(z > here, block, later)
    return later


def backwards(log_rate, steps):
    return jnp.exp(steps * log_rate) * powers(-log_rate, steps)


def returns_kernel(msg_ref, rate_ref, open_ref, g_ref, out_ref, h_ref):
    steps = g_ref.shape[0]
    per = g_ref.shape[1] // F
    i = pl.program_id(0)

    @pl.when(i == 0)
    def _():
        h_ref[...] = carry_in(msg_ref, rate_ref, steps)

    still = open_ref[...]
    for j in range(per):
        k = pl.ds(i * per + j, 1)
        cols = slice(j * F, (j + 1) * F)
        decay = still * backwards(rate_ref[k, :], steps)
        out_ref[:, cols] = (g_ref[:, cols] + decay * h_ref[k, :]).astype(bf16)


def grad_kernel(dz, st_ref, r_ref, ro_ref, msg_ref, msgo_ref, rate_ref, *outs):
    tall, steps = st_ref.shape
    halves, quads, rows, cols = outs[0].shape
    num_k = rate_ref.shape[0] - 8
    kf = num_k * F
    st = st_ref[...]
    sto = jnp.concatenate([ro_ref[:, at : at + steps] for at in range(kf + F, ro_ref.shape[1], steps)], axis=0)
    lane = iota((tall, F), 1)
    a = jnp.dot(st, r_ref[:, kf : kf + F], preferred_element_type=f32)
    a = jnp.where(lane < num_k, a, jnp.dot(sto, ro_ref[:, kf : kf + F], preferred_element_type=f32)).astype(bf16)
    h = [carry_in(ref, rate_ref, steps) for ref in (msg_ref, msgo_ref)]
    h = jnp.concatenate(h + [jnp.zeros((F - 2 * num_k, F), f32)], axis=0)
    row = iota((F, F), 0)
    pz = (lax.axis_index("z") + dz) % 2
    for half in range(halves):
        z = 2 * half + pz
        at = pl.ds(pl.multiple_of(z * cols, cols), cols)
        of_k = [z * (cols // F) + j for j in range(cols // F)]
        h_k = [jnp.where((row == k) | (row == k + num_k), h, 0.0) for k in of_k]
        g = jnp.dot(st, r_ref[:, at], preferred_element_type=f32)
        g = g + jnp.dot(sto, ro_ref[:, at], preferred_element_type=f32)
        g = g - jnp.dot(a, jnp.concatenate(h_k, axis=1).astype(bf16), preferred_element_type=f32)
        g = g.astype(bf16).reshape(len(outs), quads, rows, cols)
        for n, out in enumerate(outs):
            out[half] = g[n]


def cube_kernel(*refs):
    *ins, out_ref = refs
    for half in range(out_ref.shape[0]):
        total = ins[0][half].astype(f32)
        for ref in ins[1:]:
            total = total + ref[half].astype(f32)
        out_ref[half] = total.astype(out_ref.dtype)


def final_kernel(norm, x_ref, y_ref):
    y_ref[...] = jnp.sum(x_ref[...].astype(f32), axis=0) * norm


def whole(shape):
    return pl.BlockSpec(shape, lambda i: (0,) * len(shape))


def params(mib):
    return pltpu.CompilerParams(vmem_limit_bytes=mib * MIB)


def flat(place):
    n = 0
    for i, size in zip(place, SIZES):
        n = n * size + i
    return n


def across(offset):
    pairs = []
    for place in itertools.product(*(range(n) for n in SIZES)):
        core = place[3]
        to = [
            i if not d else (i ^ 1 if core == 0 else ((i + 1) % n if i % 2 else (i - 1) % n))
            for i, d, n in zip(place, offset, SIZES)
        ]
        pairs.append((flat(place), flat(to + [core])))
    return pairs


def alike():
    def place(core, label, index):
        if core == 0:
            return 3 - label if index else label
        return 3 - index if label else index

    return [
        [flat((2 * z + pz, place(c, py, y), place(c, px, x), c)) for z in range(4) for y in range(2) for x in range(2)]
        for c in range(2)
        for pz, py, px in OFFSETS
    ]


def body(states, episode_end, feature_head, successor_head, horizon_gap, trace_gap):
    steps, width = states.shape[1:]
    num_k = horizon_gap.shape[0]
    kf = successor_head.shape[1]
    nz, ny, nx, nc = SIZES
    swap = [(0, 1), (1, 0)]
    blk = 4 * F
    n = kf // blk
    rows, cols = width // (ny * nx * nc), kf // nz
    half, parts, quads = nz // 2, 4, ny * nx // 4
    tall = parts * quads * rows
    shape = jax.ShapeDtypeStruct
    resid, st, g_local, msg, rates, still_open = pl.pallas_call(
        local_kernel,
        in_specs=[HBM] * 6,
        out_specs=[VMEM] * 6,
        out_shape=[
            shape((steps, kf + F + tall), bf16),
            shape((tall, steps), bf16),
            shape((steps, kf), f32),
            shape((nz, num_k + 8, F), f32),
            shape((num_k + 8, F), f32),
            shape((steps, F), f32),
        ],
        scratch_shapes=[
            pltpu.SMEM((num_k,), f32),
            pltpu.SMEM((num_k,), f32),
            pltpu.VMEM((1, steps), jnp.int32),
            pltpu.VMEM((steps, width), bf16),
            pltpu.VMEM((width, F), bf16),
            pltpu.VMEM((n, width, blk), bf16),
            pltpu.SemaphoreType.DMA((5 + n,)),
        ],
        compiler_params=params(48),
        name="local",
    )(*[
        pltpu.with_memory_space_constraint(array, pltpu.HBM)
        for array in (horizon_gap, trace_gap, episode_end, states[0], feature_head, successor_head)
    ])
    resid_other = lax.ppermute(resid, "c", swap)
    msg = lax.all_to_all(msg, "z", 0, 0, tiled=True)
    msg_other = lax.ppermute(msg, "c", swap)
    chunk = (half, quads, rows, cols)

    def grads(dz):
        return pl.pallas_call(
            functools.partial(grad_kernel, dz),
            in_specs=[VMEM] * 6,
            out_specs=[VMEM] * 4,
            out_shape=[shape(chunk, bf16)] * 4,
            compiler_params=params(12),
            name="grad",
        )(st, resid, resid_other, msg, msg_other, rates)

    far, near = grads(1), grads(0)
    chunks = near + far
    chunks = dict(zip(OFFSETS, chunks))
    sums = [chunks[0, 0, 0]] + [lax.ppermute(chunks[o], AXES, across(o)) for o in ORDER]
    returns = pl.pallas_call(
        returns_kernel,
        grid=(n,),
        in_specs=[VMEM] * 3 + [pl.BlockSpec((steps, blk), lambda i: (0, i))],
        out_specs=pl.BlockSpec((steps, blk), lambda i: (0, i)),
        out_shape=shape((steps, kf), bf16),
        scratch_shapes=[pltpu.VMEM((num_k, F), f32)],
        compiler_params=params(12),
        name="returns",
    )(msg, rates, still_open, g_local)
    returns, *sums = lax.optimization_barrier((returns, *sums))
    grad = pl.pallas_call(
        cube_kernel,
        in_specs=[VMEM] * 8,
        out_specs=VMEM,
        out_shape=shape(chunk, bf16),
        compiler_params=params(12),
        name="sum_cube",
    )(*sums)
    grad = lax.all_to_all(grad.reshape(-1, rows, cols), AXES, 0, 0, axis_index_groups=alike())
    norm = float(steps * nz * ny * nx * nc) ** -0.5
    head_grad = pl.pallas_call(
        functools.partial(final_kernel, norm),
        in_specs=[VMEM],
        out_specs=VMEM,
        out_shape=shape((rows, cols), f32),
        compiler_params=params(4),
        name="sum_rest",
    )(grad)
    return returns[None], head_grad


def solution(mesh):
    grid = Mesh(mesh.devices.reshape(SIZES), AXES)
    traj = ("y", "x", "c")
    return jax.shard_map(
        body,
        mesh=grid,
        in_specs=(P(traj, "z", None), P(traj, "z"), P(), P(), P(), P()),
        out_specs=(P(traj, "z", None), P(traj, "z")),
        check_vma=False,
    )
```

time: 82.2 us -> 67.4 us (0.82)
  the two profiles are of different devices: /device:TPU:1 before, /device:TPU:32 now
where the time goes in v3:
time: 67.4 us; the launch traced here: 67.2 us
  blocking collectives  37.8 us (56%)
  Pallas kernels  9.98 us (15%)
  starting transfers between devices  9.77 us (14%)
  waiting for transfers between devices  8.97 us (13%)
    all_to_all x1, blocking collectives, body(): lax.all_to_all(grad.reshape(-1, rows, cols), AXES, 0, 0, axis_index_group...  21.9 us
    all_to_all x1, blocking collectives, body(): msg = lax.all_to_all(msg, 'z', 0, 0, tiled=True)  15.9 us
    ppermute x7, starting transfers between devices, body(): lax.ppermute(chunks[o], AXES, across(o))  9.68 us
    ppermute x7, waiting for transfers between devices, body(): lax.ppermute(chunks[o], AXES, across(o))  7.67 us
    pallas_call x1, Pallas kernels, body(): pl.pallas_call(local_kernel, in_specs=[HBM] * 6, out_specs=[VMEM] * 6, ou...  4.65 us
    pallas_call x2, Pallas kernels, grads(): pl.pallas_call(functools.partial(grad_kernel, dz), in_specs=[VMEM] * 6, o...  2.28 us
    pallas_call x1, Pallas kernels, body(): pl.pallas_call(returns_kernel, grid=(n,), in_specs=[VMEM] * 3 + [pl.Block...  2.13 us
  transfers between devices with their start and end apart: 9, of which 6 were waited for; matrix products, arithmetic and copies ran while one was open for 0% of the time, Pallas kernels for 5%

profile of v3, /device:TPU:32, one launch (start us, length us, event | category | flops | bytes accessed | tf_op | source)
XLA Modules:
  0.0 67.2 jit_solution(9914414606870913300)
XLA Ops:
  0.6 4.6 %local.1 = (bf16[256,2688]{1,0:T(8,128)(2,1)S(1)}, bf16[512,256]{1,0:T(8,128)(2,1)S(1)}, f32[256,2048]{1,0:T(8,128)S(1)}, f32[8,24,128]{2,1,0:T(8,128)S(1)}, f32...) custom-call(f32[16]{0:T(128)} %hg_hbm.1, f32[16]{0:T(128)} %tg_hbm.1, s32[1,256]{1,0:T(1,128)} %end_hbm.1, ...), custom_call_target="tpu_custom_call" | custom-call | tf_op jit(solution)/shard_map/local/pallas_call | solution.py:273
  5.3 0.1 collective-permute-start
  5.4 15.9 %all_to_all.10.msg_ref = f32[8,24,128]{2,1,0:T(8,128)S(1)} all-to-all(f32[8,24,128]{2,1,0:T(8,128)S(1)} %get-tuple-element.25), channel_id=1, replica_groups=mesh['z'=8,'y'=4,'x'=4,'c'=2] {'z'}, dimensions={0} | all-to-all | bytes 196608 | tf_op jit(solution)/shard_map/all_to_all | solution.py:301
  21.3 0.0 collective-permute-start.1
  21.3 1.3 %collective-permute-done.1.msgo_ref = f32[8,24,128]{2,1,0:T(8,128)S(1)} collective-permute-done((f32[8,24,128]{2,1,0:T(8,128)S(1)}, f32[8,24,128]{2,1,0:T(8,128)S(1)}, u32[]{:S(2)}, u32[]{:S(2)}) %collective-permute-start.1) | collective-permute-done | bytes 98336 | tf_op jit(solution)/shard_map/ppermute | solution.py:302
  22.6 0.0 collective-permute-done.ro_ref
  22.6 1.1 %grad.3 = (bf16[4,4,32,256]{3,2,1,0:T(8,128)(2,1)S(1)}, bf16[4,4,32,256]{3,2,1,0:T(8,128)(2,1)S(1)}, bf16[4,4,32,256]{3,2,1,0:T(8,128)(2,1)S(1)}, bf16[4,4,32,256]{3,2,1,0:T(8,128)(2,1)S(1)}) custom-call(bf16[512,256]{1,0:T(8,128)(2,1)S(1)} %get-tuple-element.29.st_ref, bf16[256,2688]{1,0:T(8,128)(2,1)S(1)} %get-tuple-element.30.r_ref, ...), custom_call_target="tpu_custom_call" | custom-call | tf_op jit(solution)/shard_map/grad/pallas_call | solution.py:306
  23.8 1.6 %collective-permute-start.2 = (bf16[4,4,32,256]{3,2,1,0:T(8,128)(2,1)S(1)}, bf16[4,4,32,256]{3,2,1,0:T(8,128)(2,1)S(1)}, u32[]{:S(2)}, u32[]{:S(2)}) collective-permute-start(bf16[4,4,32,256]{3,2,1,0:T(8,128)(2,1)S(1)} %get-tuple-element.32), channel_id=1, source_target_pairs={{0,32},{1,225},{2,34},{3,227},{4,36},{5,229},{6,38},{7,231},{8,40}... | collective-permute-start | bytes 786440 | tf_op jit(solution)/shard_map/ppermute | solution.py:318
  25.3 2.5 %collective-permute-start.5 = (bf16[4,4,32,256]{3,2,1,0:T(8,128)(2,1)S(1)}, bf16[4,4,32,256]{3,2,1,0:T(8,128)(2,1)S(1)}, u32[]{:S(2)}, u32[]{:S(2)}) collective-permute-start(bf16[4,4,32,256]{3,2,1,0:T(8,128)(2,1)S(1)} %get-tuple-element.35), channel_id=1, source_target_pairs={{0,42},{1,255},{2,40},{3,253},{4,46},{5,251},{6,44},{7,249},{8,34}... | collective-permute-start | bytes 786440 | tf_op jit(solution)/shard_map/ppermute | solution.py:318
  27.8 1.4 %collective-permute-start.6 = (bf16[4,4,32,256]{3,2,1,0:T(8,128)(2,1)S(1)}, bf16[4,4,32,256]{3,2,1,0:T(8,128)(2,1)S(1)}, u32[]{:S(2)}, u32[]{:S(2)}) collective-permute-start(bf16[4,4,32,256]{3,2,1,0:T(8,128)(2,1)S(1)} %get-tuple-element.36), channel_id=1, source_target_pairs={{0,40},{1,249},{2,42},{3,251},{4,44},{5,253},{6,46},{7,255},{8,32}... | collective-permute-start | bytes 786440 | tf_op jit(solution)/shard_map/ppermute | solution.py:318
  29.2 0.5 collective-permute-start.7
  29.7 1.1 %grad.2 = (bf16[4,4,32,256]{3,2,1,0:T(8,128)(2,1)S(1)}, bf16[4,4,32,256]{3,2,1,0:T(8,128)(2,1)S(1)}, bf16[4,4,32,256]{3,2,1,0:T(8,128)(2,1)S(1)}, bf16[4,4,32,256]{3,2,1,0:T(8,128)(2,1)S(1)}) custom-call(bf16[512,256]{1,0:T(8,128)(2,1)S(1)} %get-tuple-element.29.st_ref, bf16[256,2688]{1,0:T(8,128)(2,1)S(1)} %get-tuple-element.30.r_ref, ...), custom_call_target="tpu_custom_call" | custom-call | tf_op jit(solution)/shard_map/grad/pallas_call | solution.py:306
  30.8 1.7 %collective-permute-start.3 = (bf16[4,4,32,256]{3,2,1,0:T(8,128)(2,1)S(1)}, bf16[4,4,32,256]{3,2,1,0:T(8,128)(2,1)S(1)}, u32[]{:S(2)}, u32[]{:S(2)}) collective-permute-start(bf16[4,4,32,256]{3,2,1,0:T(8,128)(2,1)S(1)} %get-tuple-element.33), channel_id=1, source_target_pairs={{0,8},{1,25},{2,10},{3,27},{4,12},{5,29},{6,14},{7,31},{8,0},{9,17... | collective-permute-start | bytes 786440 | tf_op jit(solution)/shard_map/ppermute | solution.py:318
  32.5 0.0 collective-permute-done.2.refs_1_
  32.5 1.5 %collective-permute-start.4 = (bf16[4,4,32,256]{3,2,1,0:T(8,128)(2,1)S(1)}, bf16[4,4,32,256]{3,2,1,0:T(8,128)(2,1)S(1)}, u32[]{:S(2)}, u32[]{:S(2)}) collective-permute-start(bf16[4,4,32,256]{3,2,1,0:T(8,128)(2,1)S(1)} %get-tuple-element.34), channel_id=1, source_target_pairs={{0,2},{1,7},{2,0},{3,5},{4,6},{5,3},{6,4},{7,1},{8,10},{9,15},{10,... | collective-permute-start | bytes 786440 | tf_op jit(solution)/shard_map/ppermute | solution.py:318
  34.0 2.0 %collective-permute-done.5.refs_4_ = bf16[4,4,32,256]{3,2,1,0:T(8,128)(2,1)S(1)} collective-permute-done((bf16[4,4,32,256]{3,2,1,0:T(8,128)(2,1)S(1)}, bf16[4,4,32,256]{3,2,1,0:T(8,128)(2,1)S(1)}, u32[]{:S(2)}, u32[]{:S(2)}) %collective-permute-start.5) | collective-permute-done | bytes 262176 | tf_op jit(solution)/shard_map/ppermute | solution.py:318
  36.0 0.6 collective-permute-start.8
  36.6 2.1 %returns.1 = bf16[256,2048]{1,0:T(8,128)(2,1)} custom-call(f32[8,24,128]{2,1,0:T(8,128)S(1)} %all_to_all.10.msg_ref, f32[24,128]{1,0:T(8,128)S(1)} %get-tuple-element.26.rate_ref, f32[256,128]{1,0:T(8,128)S(1)} %get-tuple-element.27.open_ref, f32[256,2048]{1,0:T(8,128)S(1)} %get-tuple-element.28.g_ref), custom_call_target="tpu_custom_call" | custom-call | tf_op jit(solution)/shard_map/returns/pallas_call | solution.py:319
  38.7 0.0 collective-permute-done.6.refs_5_
  38.7 1.6 %collective-permute-done.7.refs_6_ = bf16[4,4,32,256]{3,2,1,0:T(8,128)(2,1)S(1)} collective-permute-done((bf16[4,4,32,256]{3,2,1,0:T(8,128)(2,1)S(1)}, bf16[4,4,32,256]{3,2,1,0:T(8,128)(2,1)S(1)}, u32[]{:S(2)}, u32[]{:S(2)}) %collective-permute-start.7) | collective-permute-done | bytes 262176 | tf_op jit(solution)/shard_map/ppermute | solution.py:318
  40.3 0.3 collective-permute-done.3.refs_2_
  40.6 1.1 %collective-permute-done.4.refs_3_ = bf16[4,4,32,256]{3,2,1,0:T(8,128)(2,1)S(1)} collective-permute-done((bf16[4,4,32,256]{3,2,1,0:T(8,128)(2,1)S(1)}, bf16[4,4,32,256]{3,2,1,0:T(8,128)(2,1)S(1)}, u32[]{:S(2)}, u32[]{:S(2)}) %collective-permute-start.4) | collective-permute-done | bytes 262176 | tf_op jit(solution)/shard_map/ppermute | solution.py:318
  41.7 2.7 %collective-permute-done.8.refs_7_ = bf16[4,4,32,256]{3,2,1,0:T(8,128)(2,1)S(1)} collective-permute-done((bf16[4,4,32,256]{3,2,1,0:T(8,128)(2,1)S(1)}, bf16[4,4,32,256]{3,2,1,0:T(8,128)(2,1)S(1)}, u32[]{:S(2)}, u32[]{:S(2)}) %collective-permute-start.8) | collective-permute-done | bytes 262176 | tf_op jit(solution)/shard_map/ppermute | solution.py:318
  44.4 0.3 sum_cube.1
  44.7 21.9 %all_to_all.11.x_ref = bf16[16,32,256]{2,1,0:T(8,128)(2,1)S(1)} all-to-all(bf16[16,32,256]{2,1,0:T(8,128)(2,1)S(1)} %bitcast.3), channel_id=1, replica_groups={{0,6,24,30,64,70,88,94,128,134,152,158,192,198,216,222},{2,4,26,28,66,6..., dimensions={0} | all-to-all | bytes 524288 | tf_op jit(solution)/shard_map/all_to_all | solution.py:338
  66.6 0.7 sum_rest.1
Async XLA Ops:
  5.3 17.3 %collective-permute-start = (bf16[256,2688]{1,0:T(8,128)(2,1)S(1)}, bf16[256,2688]{1,0:T(8,128)(2,1)S(1)}, u32[]{:S(2)}, u32[]{:S(2)}) collective-permute-start(bf16[256,2688]{1,0:T(8,128)(2,1)S(1)} %get-tuple-element.30.r_ref), channel_id=1, source_target_pairs={{0,1},{1,0},{2,3},{3,2},{4,5},{5,4},{6,7},{7,6},{8,9},{9,8},{10,11... | collective-permute-start | bytes 4128776 | tf_op jit(solution)/shard_map/ppermute | solution.py:300
  21.3 1.3 %collective-permute-start.1 = (f32[8,24,128]{2,1,0:T(8,128)S(1)}, f32[8,24,128]{2,1,0:T(8,128)S(1)}, u32[]{:S(2)}, u32[]{:S(2)}) collective-permute-start(f32[8,24,128]{2,1,0:T(8,128)S(1)} %all_to_all.10.msg_ref), channel_id=1, source_target_pairs={{0,1},{1,0},{2,3},{3,2},{4,5},{5,4},{6,7},{7,6},{8,9},{9,8},{10,11... | collective-permute-start | bytes 294920 | tf_op jit(solution)/shard_map/ppermute | solution.py:302
  23.8 8.8 %collective-permute-start.2 = (bf16[4,4,32,256]{3,2,1,0:T(8,128)(2,1)S(1)}, bf16[4,4,32,256]{3,2,1,0:T(8,128)(2,1)S(1)}, u32[]{:S(2)}, u32[]{:S(2)}) collective-permute-start(bf16[4,4,32,256]{3,2,1,0:T(8,128)(2,1)S(1)} %get-tuple-element.32), channel_id=1, source_target_pairs={{0,32},{1,225},{2,34},{3,227},{4,36},{5,229},{6,38},{7,231},{8,40}... | collective-permute-start | bytes 786440 | tf_op jit(solution)/shard_map/ppermute | solution.py:318
  25.3 10.7 %collective-permute-start.5 = (bf16[4,4,32,256]{3,2,1,0:T(8,128)(2,1)S(1)}, bf16[4,4,32,256]{3,2,1,0:T(8,128)(2,1)S(1)}, u32[]{:S(2)}, u32[]{:S(2)}) collective-permute-start(bf16[4,4,32,256]{3,2,1,0:T(8,128)(2,1)S(1)} %get-tuple-element.35), channel_id=1, source_target_pairs={{0,42},{1,255},{2,40},{3,253},{4,46},{5,251},{6,44},{7,249},{8,34}... | collective-permute-start | bytes 786440 | tf_op jit(solution)/shard_map/ppermute | solution.py:318
  27.8 10.9 %collective-permute-start.6 = (bf16[4,4,32,256]{3,2,1,0:T(8,128)(2,1)S(1)}, bf16[4,4,32,256]{3,2,1,0:T(8,128)(2,1)S(1)}, u32[]{:S(2)}, u32[]{:S(2)}) collective-permute-start(bf16[4,4,32,256]{3,2,1,0:T(8,128)(2,1)S(1)} %get-tuple-element.36), channel_id=1, source_target_pairs={{0,40},{1,249},{2,42},{3,251},{4,44},{5,253},{6,46},{7,255},{8,32}... | collective-permute-start | bytes 786440 | tf_op jit(solution)/shard_map/ppermute | solution.py:318
  29.2 11.1 %collective-permute-start.7 = (bf16[4,4,32,256]{3,2,1,0:T(8,128)(2,1)S(1)}, bf16[4,4,32,256]{3,2,1,0:T(8,128)(2,1)S(1)}, u32[]{:S(2)}, u32[]{:S(2)}) collective-permute-start(bf16[4,4,32,256]{3,2,1,0:T(8,128)(2,1)S(1)} %get-tuple-element.37), channel_id=1, source_target_pairs={{0,34},{1,231},{2,32},{3,229},{4,38},{5,227},{6,36},{7,225},{8,42}... | collective-permute-start | bytes 786440 | tf_op jit(solution)/shard_map/ppermute | solution.py:318
  30.8 9.7 %collective-permute-start.3 = (bf16[4,4,32,256]{3,2,1,0:T(8,128)(2,1)S(1)}, bf16[4,4,32,256]{3,2,1,0:T(8,128)(2,1)S(1)}, u32[]{:S(2)}, u32[]{:S(2)}) collective-permute-start(bf16[4,4,32,256]{3,2,1,0:T(8,128)(2,1)S(1)} %get-tuple-element.33), channel_id=1, source_target_pairs={{0,8},{1,25},{2,10},{3,27},{4,12},{5,29},{6,14},{7,31},{8,0},{9,17... | collective-permute-start | bytes 786440 | tf_op jit(solution)/shard_map/ppermute | solution.py:318
  32.5 9.2 %collective-permute-start.4 = (bf16[4,4,32,256]{3,2,1,0:T(8,128)(2,1)S(1)}, bf16[4,4,32,256]{3,2,1,0:T(8,128)(2,1)S(1)}, u32[]{:S(2)}, u32[]{:S(2)}) collective-permute-start(bf16[4,4,32,256]{3,2,1,0:T(8,128)(2,1)S(1)} %get-tuple-element.34), channel_id=1, source_target_pairs={{0,2},{1,7},{2,0},{3,5},{4,6},{5,3},{6,4},{7,1},{8,10},{9,15},{10,... | collective-permute-start | bytes 786440 | tf_op jit(solution)/shard_map/ppermute | solution.py:318
  36.0 8.4 %collective-permute-start.8 = (bf16[4,4,32,256]{3,2,1,0:T(8,128)(2,1)S(1)}, bf16[4,4,32,256]{3,2,1,0:T(8,128)(2,1)S(1)}, u32[]{:S(2)}, u32[]{:S(2)}) collective-permute-start(bf16[4,4,32,256]{3,2,1,0:T(8,128)(2,1)S(1)} %get-tuple-element.38), channel_id=1, source_target_pairs={{0,10},{1,31},{2,8},{3,29},{4,14},{5,27},{6,12},{7,25},{8,2},{9,23... | collective-permute-start | bytes 786440 | tf_op jit(solution)/shard_map/ppermute | solution.py:318

commit v4 on v3

--- a/solution.py
+++ b/solution.py
@@ -8,6 +8,7 @@
 from jax.sharding import Mesh, PartitionSpec as P
 
 F = 128
+EARLY = 5
 MIB = 1 << 20
 AXES = ("z", "y", "x", "c")
 SIZES = (8, 4, 4, 2)
@@ -16,7 +17,6 @@
 VMEM = pl.BlockSpec(memory_space=pltpu.VMEM)
 HBM = pl.BlockSpec(memory_space=pltpu.HBM)
 OFFSETS = list(itertools.product((0, 1), repeat=3))
-ORDER = [(1, 0, 0), (0, 1, 0), (0, 0, 1), (1, 1, 1), (1, 1, 0), (1, 0, 1), (0, 1, 1)]
 
 
 def iota(shape, dim):
@@ -100,22 +100,21 @@
     def turn():
         st = s.T
         here = lax.axis_index("c")
-        label = {(a, core): place_in_cube(lax.axis_index(a), core)[0] for a in ("y", "x") for core in range(2)}
         tall = st_ref.shape[0] // (SIZES[1] * SIZES[2])
         for n in range(st.shape[0] // tall):
             y, x, core = n // (SIZES[2] * SIZES[3]), n // SIZES[3] % SIZES[2], n % SIZES[3]
             (ly, iy), (lx, ix) = place_in_cube(y, core), place_in_cube(x, core)
-            at = ((ly ^ label["y", core]) * 2 + (lx ^ label["x", core])) * 4 + iy * 2 + ix
+            at = (ly * 2 + lx) * 4 + iy * 2 + ix
             part = st[n * tall : (n + 1) * tall, :]
 
             @pl.when(here == core)
             def _():
-                st_ref[pl.ds(pl.multiple_of(at * tall, tall), tall), :] = part
+                st_ref[at * tall : (at + 1) * tall, :] = part
 
             @pl.when(here != core)
             def _():
-                left = kf + F + at // (steps // tall) * steps
-                r_ref[pl.ds(pl.multiple_of(at % (steps // tall) * tall, tall), tall), pl.ds(pl.multiple_of(left, F), steps)] = part
+                left, top = kf + F + at // (steps // tall) * steps, at % (steps // tall) * tall
+                r_ref[top : top + tall, left : left + steps] = part
 
     turn()
     following = predict(0)
@@ -178,40 +177,48 @@
         out_ref[:, cols] = (g_ref[:, cols] + decay * h_ref[k, :]).astype(bf16)
 
 
-def grad_kernel(dz, st_ref, r_ref, ro_ref, msg_ref, msgo_ref, rate_ref, *outs):
-    tall, steps = st_ref.shape
-    halves, quads, rows, cols = outs[0].shape
+def product(st, r_ref, ro_ref, at):
+    kf, steps = ro_ref.shape[1] - st.shape[0] - F, st.shape[1]
+    sto = jnp.concatenate([ro_ref[:, n : n + steps] for n in range(kf + F, ro_ref.shape[1], steps)], axis=0)
+    g = jnp.dot(st, r_ref[:, at], preferred_element_type=f32)
+    return g + jnp.dot(sto, ro_ref[:, at], preferred_element_type=f32)
+
+
+def early_kernel(num_k, st_ref, r_ref, ro_ref, g_ref, a_ref):
+    st = st_ref[...]
+    kf = num_k * F
+    steps = st.shape[1]
+    sto = jnp.concatenate([ro_ref[:, n : n + steps] for n in range(kf + F, ro_ref.shape[1], steps)], axis=0)
+    lane = iota((st.shape[0], F), 1)
+    a = jnp.dot(st, r_ref[:, kf : kf + F], preferred_element_type=f32)
+    a_ref[...] = jnp.where(lane < num_k, a, jnp.dot(sto, ro_ref[:, kf : kf + F], preferred_element_type=f32)).astype(bf16)
+    cols = g_ref.shape[-1]
+    for z in range(g_ref.shape[0]):
+        g_ref[z] = product(st, r_ref, ro_ref, slice(z * cols, (z + 1) * cols))
+
+
+def grad_kernel(st_ref, r_ref, ro_ref, msg_ref, msgo_ref, rate_ref, g_ref, a_ref, out_ref):
+    parts, halves, quads, rows, cols = out_ref.shape
+    parts //= 2
     num_k = rate_ref.shape[0] - 8
-    kf = num_k * F
+    steps = st_ref.shape[1]
     st = st_ref[...]
-    sto = jnp.concatenate([ro_ref[:, at : at + steps] for at in range(kf + F, ro_ref.shape[1], steps)], axis=0)
-    lane = iota((tall, F), 1)
-    a = jnp.dot(st, r_ref[:, kf : kf + F], preferred_element_type=f32)
-    a = jnp.where(lane < num_k, a, jnp.dot(sto, ro_ref[:, kf : kf + F], preferred_element_type=f32)).astype(bf16)
     h = [carry_in(ref, rate_ref, steps) for ref in (msg_ref, msgo_ref)]
     h = jnp.concatenate(h + [jnp.zeros((F - 2 * num_k, F), f32)], axis=0)
     row = iota((F, F), 0)
-    pz = (lax.axis_index("z") + dz) % 2
-    for half in range(halves):
-        z = 2 * half + pz
-        at = pl.ds(pl.multiple_of(z * cols, cols), cols)
+    for z in range(2 * halves):
         of_k = [z * (cols // F) + j for j in range(cols // F)]
         h_k = [jnp.where((row == k) | (row == k + num_k), h, 0.0) for k in of_k]
-        g = jnp.dot(st, r_ref[:, at], preferred_element_type=f32)
-        g = g + jnp.dot(sto, ro_ref[:, at], preferred_element_type=f32)
-        g = g - jnp.dot(a, jnp.concatenate(h_k, axis=1).astype(bf16), preferred_element_type=f32)
-        g = g.astype(bf16).reshape(len(outs), quads, rows, cols)
-        for n, out in enumerate(outs):
-            out[half] = g[n]
-
-
-def cube_kernel(*refs):
-    *ins, out_ref = refs
+        g = g_ref[z] if z < g_ref.shape[0] else product(st, r_ref, ro_ref, slice(z * cols, (z + 1) * cols))
+        g = g - jnp.dot(a_ref[...], jnp.concatenate(h_k, axis=1).astype(bf16), preferred_element_type=f32)
+        g = g.astype(bf16).reshape(parts, quads, rows, cols)
+        for n in range(parts):
+            out_ref[z % 2 * parts + n, z // 2] = g[n]
+
+
+def cube_kernel(in_ref, out_ref):
     for half in range(out_ref.shape[0]):
-        total = ins[0][half].astype(f32)
-        for ref in ins[1:]:
-            total = total + ref[half].astype(f32)
-        out_ref[half] = total.astype(out_ref.dtype)
+        out_ref[half] = jnp.sum(in_ref[:, half].astype(f32), axis=0).astype(out_ref.dtype)
 
 
 def final_kernel(norm, x_ref, y_ref):
@@ -233,28 +240,30 @@
     return n
 
 
-def across(offset):
-    pairs = []
-    for place in itertools.product(*(range(n) for n in SIZES)):
-        core = place[3]
-        to = [
-            i if not d else (i ^ 1 if core == 0 else ((i + 1) % n if i % 2 else (i - 1) % n))
-            for i, d, n in zip(place, offset, SIZES)
-        ]
-        pairs.append((flat(place), flat(to + [core])))
-    return pairs
+def place(core, label, index):
+    if core == 0:
+        return 3 - label if index else label
+    return 3 - index if label else index
 
 
 def alike():
-    def place(core, label, index):
-        if core == 0:
-            return 3 - label if index else label
-        return 3 - index if label else index
-
     return [
         [flat((2 * z + pz, place(c, py, y), place(c, px, x), c)) for z in range(4) for y in range(2) for x in range(2)]
         for c in range(2)
         for pz, py, px in OFFSETS
+    ]
+
+
+def cubes():
+    def along(core, label, cube):
+        return 2 * cube + label if core == 0 else (2 * cube + 2 - label) % SIZES[0]
+
+    return [
+        [flat((along(c, pz, z), place(c, py, y), place(c, px, x), c)) for pz, py, px in OFFSETS]
+        for c in range(2)
+        for z in range(SIZES[0] // 2)
+        for y in range(2)
+        for x in range(2)
     ]
 
 
@@ -299,23 +308,37 @@
     ])
     resid_other = lax.ppermute(resid, "c", swap)
     msg = lax.all_to_all(msg, "z", 0, 0, tiled=True)
+    msg, resid_other = lax.optimization_barrier((msg, resid_other))
     msg_other = lax.ppermute(msg, "c", swap)
     chunk = (half, quads, rows, cols)
 
-    def grads(dz):
-        return pl.pallas_call(
-            functools.partial(grad_kernel, dz),
-            in_specs=[VMEM] * 6,
-            out_specs=[VMEM] * 4,
-            out_shape=[shape(chunk, bf16)] * 4,
-            compiler_params=params(12),
-            name="grad",
-        )(st, resid, resid_other, msg, msg_other, rates)
-
-    far, near = grads(1), grads(0)
-    chunks = near + far
-    chunks = dict(zip(OFFSETS, chunks))
-    sums = [chunks[0, 0, 0]] + [lax.ppermute(chunks[o], AXES, across(o)) for o in ORDER]
+    early, factor = pl.pallas_call(
+        functools.partial(early_kernel, num_k),
+        in_specs=[VMEM] * 3,
+        out_specs=[VMEM] * 2,
+        out_shape=[shape((EARLY, tall, cols), f32), shape((tall, F), bf16)],
+        compiler_params=params(12),
+        cost_estimate=pl.CostEstimate(flops=2 * EARLY * tall * steps * cols * 2, bytes_accessed=4 * MIB, transcendentals=0),
+        name="early",
+    )(st, resid, resid_other)
+    grad = pl.pallas_call(
+        grad_kernel,
+        in_specs=[VMEM] * 8,
+        out_specs=VMEM,
+        out_shape=shape((2 * parts, *chunk), bf16),
+        compiler_params=params(12),
+        name="grad",
+    )(st, resid, resid_other, msg, msg_other, rates, early, factor)
+    grad = lax.all_to_all(grad.reshape(2 * parts, -1, cols), AXES, 0, 0, axis_index_groups=cubes())
+    grad = pl.pallas_call(
+        cube_kernel,
+        in_specs=[VMEM],
+        out_specs=VMEM,
+        out_shape=shape(chunk, bf16),
+        compiler_params=params(12),
+        name="sum_cube",
+    )(grad.reshape(2 * parts, *chunk))
+    grad, msg = lax.optimization_barrier((grad, msg))
     returns = pl.pallas_call(
         returns_kernel,
         grid=(n,),
@@ -326,15 +349,6 @@
         compiler_params=params(12),
         name="returns",
     )(msg, rates, still_open, g_local)
-    returns, *sums = lax.optimization_barrier((returns, *sums))
-    grad = pl.pallas_call(
-        cube_kernel,
-        in_specs=[VMEM] * 8,
-        out_specs=VMEM,
-        out_shape=shape(chunk, bf16),
-        compiler_params=params(12),
-        name="sum_cube",
-    )(*sums)
     grad = lax.all_to_all(grad.reshape(-1, rows, cols), AXES, 0, 0, axis_index_groups=alike())
     norm = float(steps * nz * ny * nx * nc) ** -0.5
     head_grad = pl.pallas_call(

time: 67.4 us -> 66.3 us (0.984)
  the two profiles are of different devices: /device:TPU:32 before, /device:TPU:1 now
where the time goes in v4:
time: 66.3 us; the launch traced here: 66 us
  blocking collectives  39 us (59%)
  Pallas kernels  10.4 us (16%)
  starting transfers between devices  8.48 us (13%)
  waiting for transfers between devices  7.52 us (11%)
  between operations  0.67 us (1%)
    all_to_all x1, blocking collectives, body(): lax.all_to_all(grad.reshape(2 * parts, -1, cols), AXES, 0, 0, axis_index_...  24.9 us
    all_to_all x1, blocking collectives, body(): msg = lax.all_to_all(msg, 'z', 0, 0, tiled=True)  14 us
    all_to_all x1, waiting for transfers between devices, body(): lax.all_to_all(grad.reshape(-1, rows, cols), AXES, 0, 0, axis_index_group...  7.52 us
    pallas_call x1, Pallas kernels, body(): pl.pallas_call(local_kernel, in_specs=[HBM] * 6, out_specs=[VMEM] * 6, ou...  4.49 us
    all_to_all x1, starting transfers between devices, body(): lax.all_to_all(grad.reshape(-1, rows, cols), AXES, 0, 0, axis_index_group...  3.64 us
    ppermute x1, starting transfers between devices, body(): resid_other = lax.ppermute(resid, 'c', swap)  3.33 us
    pallas_call x1, Pallas kernels, body(): pl.pallas_call(returns_kernel, grid=(n,), in_specs=[VMEM] * 3 + [pl.Block...  2.13 us
    ppermute x1, starting transfers between devices, body(): msg_other = lax.ppermute(msg, 'c', swap)  1.51 us
  transfers between devices with their start and end apart: 3, of which 1 were waited for; matrix products, arithmetic and copies ran while one was open for 0% of the time, Pallas kernels for 5%

profile of v4, /device:TPU:1, one launch (start us, length us, event | category | flops | bytes accessed | tf_op | source)
XLA Modules:
  0.0 66.0 jit_solution(1015576237429961015)
XLA Ops:
  0.6 4.5 %local.1 = (bf16[256,2688]{1,0:T(8,128)(2,1)S(1)}, bf16[512,256]{1,0:T(8,128)(2,1)S(1)}, f32[256,2048]{1,0:T(8,128)S(1)}, f32[8,24,128]{2,1,0:T(8,128)S(1)}, f32...) custom-call(f32[16]{0:T(128)} %hg_hbm.1, f32[16]{0:T(128)} %tg_hbm.1, s32[1,256]{1,0:T(1,128)} %end_hbm.1, ...), custom_call_target="tpu_custom_call" | custom-call | tf_op jit(solution)/shard_map/local/pallas_call | solution.py:282
  5.1 3.3 %collective-permute-start = (bf16[256,2688]{1,0:T(8,128)(2,1)S(1)}, bf16[256,2688]{1,0:T(8,128)(2,1)S(1)}, u32[]{:S(2)}, u32[]{:S(2)}) collective-permute-start(bf16[256,2688]{1,0:T(8,128)(2,1)S(1)} %get-tuple-element.15.r_ref), channel_id=1, source_target_pairs={{0,1},{1,0},{2,3},{3,2},{4,5},{5,4},{6,7},{7,6},{8,9},{9,8},{10,11... | collective-permute-start | bytes 4128776 | tf_op jit(solution)/shard_map/ppermute | solution.py:309
  8.5 14.0 %all_to_all.15.msg_ref = f32[8,24,128]{2,1,0:T(8,128)S(1)} all-to-all(f32[8,24,128]{2,1,0:T(8,128)S(1)} %get-tuple-element.16), channel_id=1, replica_groups=mesh['z'=8,'y'=4,'x'=4,'c'=2] {'z'}, dimensions={0} | all-to-all | bytes 196608 | tf_op jit(solution)/shard_map/all_to_all | solution.py:310
  22.5 0.0 collective-permute-done.ro_ref
  22.5 1.5 %collective-permute-start.1 = (f32[8,24,128]{2,1,0:T(8,128)S(1)}, f32[8,24,128]{2,1,0:T(8,128)S(1)}, u32[]{:S(2)}, u32[]{:S(2)}) collective-permute-start(f32[8,24,128]{2,1,0:T(8,128)S(1)} %all_to_all.15.msg_ref), channel_id=1, source_target_pairs={{0,1},{1,0},{2,3},{3,2},{4,5},{5,4},{6,7},{7,6},{8,9},{9,8},{10,11... | collective-permute-start | bytes 294920 | tf_op jit(solution)/shard_map/ppermute | solution.py:312
  24.0 1.0 %early.1 = (f32[5,512,256]{2,1,0:T(8,128)S(1)}, bf16[512,128]{1,0:T(8,128)(2,1)S(1)}) custom-call(bf16[512,256]{1,0:T(8,128)(2,1)S(1)} %get-tuple-element.14.st_ref, bf16[256,2688]{1,0:T(8,128)(2,1)S(1)} %get-tuple-element.15.r_ref, bf16[256,2688]{1,0:T(8,128)(2,1)S(1)} %collective-permute-done.ro_ref), custom_call_target="tpu_custom_call" | custom-call | flops 671088640 | bytes 4194304 | tf_op jit(solution)/shard_map/early/pallas_call | solution.py:315
  25.0 0.0 collective-permute-done.1.msgo_ref
  25.0 1.1 %grad.1 = bf16[8,4,4,32,256]{4,3,2,1,0:T(8,128)(2,1)S(1)} custom-call(bf16[512,256]{1,0:T(8,128)(2,1)S(1)} %get-tuple-element.14.st_ref, bf16[256,2688]{1,0:T(8,128)(2,1)S(1)} %get-tuple-element.15.r_ref, bf16[256,2688]{1,0:T(8,128)(2,1)S(1)} %collective-permute-done.ro_ref, f32[8,24,128]{2,1,0:T(8,128)S(1)} %all_to_all.15.msg_ref, ...), custom_call_target="tpu_custom_call" | custom-call | tf_op jit(solution)/shard_map/grad/pallas_call | solution.py:324
  26.2 24.9 %all_to_all.16 = bf16[8,512,256]{2,1,0:T(8,128)(2,1)S(1)} all-to-all(bf16[8,512,256]{2,1,0:T(8,128)(2,1)S(1)} %bitcast.6), channel_id=1, replica_groups={{0,2,8,10,32,34,40,42},{6,4,14,12,38,36,46,44},{24,26,16,18,56,58,48,50..., dimensions={0} | all-to-all | bytes 4194304 | tf_op jit(solution)/shard_map/all_to_all | solution.py:332
  51.1 1.0 %sum_cube.1 = bf16[4,4,32,256]{3,2,1,0:T(8,128)(2,1)} custom-call(bf16[8,4,4,32,256]{4,3,2,1,0:T(8,128)(2,1)S(1)} %bitcast.5), custom_call_target="tpu_custom_call" | custom-call | tf_op jit(solution)/shard_map/sum_cube/pallas_call | solution.py:333
  52.1 3.6 %all-to-all-start.2 = ((bf16[16,32,256]{2,1,0:T(8,128)(2,1)}), bf16[16,32,256]{2,1,0:T(8,128)(2,1)S(1)}, u32[]{:S(2)}, u32[]{:S(2)}) async-start(bf16[16,32,256]{2,1,0:T(8,128)(2,1)} %bitcast.4), calls=%async_computation.2 | async-start | bytes 524288 | tf_op jit(solution)/shard_map/all_to_all | solution.py:352
  55.7 2.1 %returns.1 = bf16[256,2048]{1,0:T(8,128)(2,1)} custom-call(f32[8,24,128]{2,1,0:T(8,128)S(1)} %all_to_all.15.msg_ref, f32[24,128]{1,0:T(8,128)S(1)} %get-tuple-element.19.rate_ref, f32[256,128]{1,0:T(8,128)S(1)} %get-tuple-element.23.open_ref, f32[256,2048]{1,0:T(8,128)S(1)} %get-tuple-element.24.g_ref), custom_call_target="tpu_custom_call" | custom-call | tf_op jit(solution)/shard_map/returns/pallas_call | solution.py:342
  57.8 7.5 %all-to-all-done.2.x_ref = bf16[16,32,256]{2,1,0:T(8,128)(2,1)S(1)} async-done(((bf16[16,32,256]{2,1,0:T(8,128)(2,1)}), bf16[16,32,256]{2,1,0:T(8,128)(2,1)S(1)}, u32[]{:S(2)}, u32[]{:S(2)}) %all-to-all-start.2) | async-done | bytes 262176 | tf_op jit(solution)/shard_map/all_to_all | solution.py:352
  65.3 0.7 %sum_rest.1 = f32[32,256]{1,0:T(8,128)} custom-call(bf16[16,32,256]{2,1,0:T(8,128)(2,1)S(1)} %all-to-all-done.2.x_ref), custom_call_target="tpu_custom_call" | custom-call | tf_op jit(solution)/shard_map/sum_rest/pallas_call | solution.py:354
Async XLA Ops:
  5.1 17.4 %collective-permute-start = (bf16[256,2688]{1,0:T(8,128)(2,1)S(1)}, bf16[256,2688]{1,0:T(8,128)(2,1)S(1)}, u32[]{:S(2)}, u32[]{:S(2)}) collective-permute-start(bf16[256,2688]{1,0:T(8,128)(2,1)S(1)} %get-tuple-element.15.r_ref), channel_id=1, source_target_pairs={{0,1},{1,0},{2,3},{3,2},{4,5},{5,4},{6,7},{7,6},{8,9},{9,8},{10,11... | collective-permute-start | bytes 4128776 | tf_op jit(solution)/shard_map/ppermute | solution.py:309
  22.5 2.5 %collective-permute-start.1 = (f32[8,24,128]{2,1,0:T(8,128)S(1)}, f32[8,24,128]{2,1,0:T(8,128)S(1)}, u32[]{:S(2)}, u32[]{:S(2)}) collective-permute-start(f32[8,24,128]{2,1,0:T(8,128)S(1)} %all_to_all.15.msg_ref), channel_id=1, source_target_pairs={{0,1},{1,0},{2,3},{3,2},{4,5},{5,4},{6,7},{7,6},{8,9},{9,8},{10,11... | collective-permute-start | bytes 294920 | tf_op jit(solution)/shard_map/ppermute | solution.py:312
  52.1 13.3 %all-to-all-start.2 = ((bf16[16,32,256]{2,1,0:T(8,128)(2,1)}), bf16[16,32,256]{2,1,0:T(8,128)(2,1)S(1)}, u32[]{:S(2)}, u32[]{:S(2)}) async-start(bf16[16,32,256]{2,1,0:T(8,128)(2,1)} %bitcast.4), calls=%async_computation.2 | async-start | bytes 524288 | tf_op jit(solution)/shard_map/all_to_all | solution.py:352

commit v5 on v4

--- a/solution.py
+++ b/solution.py
@@ -8,7 +8,6 @@
 from jax.sharding import Mesh, PartitionSpec as P
 
 F = 128
-EARLY = 5
 MIB = 1 << 20
 AXES = ("z", "y", "x", "c")
 SIZES = (8, 4, 4, 2)
@@ -48,7 +47,7 @@
     return (gray, half) if core == 0 else (half, gray)
 
 
-def local_kernel(hg_hbm, tg_hbm, end_hbm, s_hbm, wf_hbm, w_hbm, r_ref, st_ref, g_ref, msg_ref, rate_ref, open_ref,
+def local_kernel(hg_hbm, tg_hbm, end_hbm, s_hbm, wf_hbm, w_hbm, r_ref, st_ref, g_ref, rate_ref, open_ref,
                  hg_ref, tg_ref, end_ref, s_ref, wf_ref, w_ref, sems):
     blocks, _, blk = w_ref.shape
     steps, width = s_ref.shape
@@ -76,8 +75,7 @@
     total = jnp.sum(ended_row, axis=1, keepdims=True)
     still = jnp.where(at_row == total, 1.0, 0.0)
     open_ref[...] = still
-    for z in range(msg_ref.shape[0]):
-        msg_ref[z, num_k:, :] = jnp.broadcast_to(jnp.where(total == 0.0, 1.0, 0.0), (msg_ref.shape[1] - num_k, F))
+    free = jnp.where(total == 0.0, 1.0, 0.0)
     lane = iota((1, F), 1)
     by_lane = jnp.zeros((1, F), f32)
     for k in range(num_k):
@@ -118,6 +116,7 @@
 
     turn()
     following = predict(0)
+    carries = []
     for i in range(blocks):
         pred = following
         if i + 1 < blocks:
@@ -141,33 +140,39 @@
             g = h - biased[j][1]
             g_ref[:, cols] = g
             r_ref[:, cols] = (biased[j][0] - g).astype(bf16)
-            for z in range(msg_ref.shape[0]):
-                msg_ref[z, k : k + 1, :] = h[:1]
-
-
-def carry_in(msg_ref, rate_ref, steps):
-    here = lax.axis_index("z")
-    num_k = rate_ref.shape[0] - 8
-    through = jnp.exp(steps * rate_ref[:num_k, :])
-    later = jnp.zeros((num_k, F), f32)
-    for z in range(msg_ref.shape[0] - 1, 0, -1):
-        block = msg_ref[z, :num_k, :] + through * msg_ref[z, num_k : num_k + 1, :] * later
-        later = jnp.where(z > here, block, later)
-    return later
+            carries.append(h[:1])
+    last = r_ref.shape[1] - F
+    r_ref[:num_k, last:] = jnp.concatenate(carries, axis=0).astype(bf16)
+    r_ref[num_k:, last:] = jnp.broadcast_to(free, (steps - num_k, F)).astype(bf16)
 
 
 def backwards(log_rate, steps):
     return jnp.exp(steps * log_rate) * powers(-log_rate, steps)
 
 
-def returns_kernel(msg_ref, rate_ref, open_ref, g_ref, out_ref, h_ref):
+def returns_kernel(rows, rate_ref, open_ref, g_ref, partner_ref, x_ref, out_ref, h_ref):
     steps = g_ref.shape[0]
     per = g_ref.shape[1] // F
     i = pl.program_id(0)
 
     @pl.when(i == 0)
     def _():
-        h_ref[...] = carry_in(msg_ref, rate_ref, steps)
+        num_k = h_ref.shape[0]
+        z, core = lax.axis_index("z"), lax.axis_index("c")
+        (_, iy), (_, ix) = own_place("y"), own_place("x")
+        through = jnp.exp(steps * rate_ref[:num_k, :])
+        places = x_ref.shape[0] // (SIZES[0] // 2)
+
+        def pair(n):
+            block = x_ref[n * places + iy * 2 + ix, rows + 16 :, :].astype(f32)
+            return block[:, F:], block[:, F - 32 : F - 31]
+
+        later = jnp.where((core == 1) & (z % 2 == 0), pair(0)[0], 0.0)
+        for n in range(SIZES[0] // 2 - 1, 0, -1):
+            carry, free = pair(n)
+            later = jnp.where(n > z // 2, carry + through * through * free * later, later)
+        after = partner_ref[:num_k, :] + through * partner_ref[num_k : num_k + 1, :] * later
+        h_ref[...] = jnp.where((z % 2 == core) & (z < SIZES[0] - 1), after, later)
 
     still = open_ref[...]
     for j in range(per):
@@ -177,52 +182,132 @@
         out_ref[:, cols] = (g_ref[:, cols] + decay * h_ref[k, :]).astype(bf16)
 
 
-def product(st, r_ref, ro_ref, at):
-    kf, steps = ro_ref.shape[1] - st.shape[0] - F, st.shape[1]
-    sto = jnp.concatenate([ro_ref[:, n : n + steps] for n in range(kf + F, ro_ref.shape[1], steps)], axis=0)
-    g = jnp.dot(st, r_ref[:, at], preferred_element_type=f32)
-    return g + jnp.dot(sto, ro_ref[:, at], preferred_element_type=f32)
-
-
-def early_kernel(num_k, st_ref, r_ref, ro_ref, g_ref, a_ref):
+def own_place(axis):
+    here = lax.axis_index(axis)
+    return tuple(
+        jnp.where(lax.axis_index("c") == 0, a, b) for a, b in zip(place_in_cube(here, 0), place_in_cube(here, 1))
+    )
+
+
+def grad_kernel(num_k, st_ref, r_ref, ro_ref, out_ref):
+    tall, steps = st_ref.shape
+    labels, deep, cols = out_ref.shape
+    parts, per = labels // 2, cols // F
+    part = tall // parts
+    kf = num_k * F
+    halves = kf // cols // 2
+    last = r_ref.shape[1] - F
     st = st_ref[...]
-    kf = num_k * F
-    steps = st.shape[1]
-    sto = jnp.concatenate([ro_ref[:, n : n + steps] for n in range(kf + F, ro_ref.shape[1], steps)], axis=0)
-    lane = iota((st.shape[0], F), 1)
+    sto = jnp.concatenate([ro_ref[:, n : n + steps] for n in range(kf + F, last, steps)], axis=0)
+    lane = iota((tall, F), 1)
     a = jnp.dot(st, r_ref[:, kf : kf + F], preferred_element_type=f32)
-    a_ref[...] = jnp.where(lane < num_k, a, jnp.dot(sto, ro_ref[:, kf : kf + F], preferred_element_type=f32)).astype(bf16)
-    cols = g_ref.shape[-1]
-    for z in range(g_ref.shape[0]):
-        g_ref[z] = product(st, r_ref, ro_ref, slice(z * cols, (z + 1) * cols))
-
-
-def grad_kernel(st_ref, r_ref, ro_ref, msg_ref, msgo_ref, rate_ref, g_ref, a_ref, out_ref):
-    parts, halves, quads, rows, cols = out_ref.shape
-    parts //= 2
+    a = jnp.where(lane < num_k, a, jnp.dot(sto, ro_ref[:, kf : kf + F], preferred_element_type=f32))
+    at = a.T
+    carries = [ref[: num_k + 1, last:].astype(f32) for ref in (r_ref, ro_ref)]
+    for z in range(2 * halves):
+        columns = slice(z * cols, (z + 1) * cols)
+        g = jnp.dot(st, r_ref[:, columns], preferred_element_type=f32)
+        g = g + jnp.dot(sto, ro_ref[:, columns], preferred_element_type=f32)
+        g = g.astype(bf16)
+        for n in range(parts):
+            out_ref[z % 2 * parts + n, z // 2 * part : (z // 2 + 1) * part, :] = g[n * part : (n + 1) * part]
+
+    def wide(rows):
+        return jnp.concatenate(rows, axis=1)
+
+    for pz in range(2):
+        for n in range(parts):
+            rows = [
+                wide([carries[u][k : k + 1] for k in range((2 * half + pz) * per, (2 * half + pz + 1) * per)])
+                for half in range(halves)
+                for u in range(2)
+            ]
+            rows += [
+                wide([
+                    at[u * num_k + k : u * num_k + k + 1, n * part : (n + 1) * part]
+                    for k in range((2 * half + pz) * per, (2 * half + pz + 1) * per)
+                ])
+                for half in range(halves)
+                for u in range(2)
+            ]
+            rows += [wide([carries[u][num_k : num_k + 1]] * per) for u in range(2)]
+            rows.append(jnp.zeros((24 - len(rows), cols), f32))
+            rows.append(wide([carries[0][m * 8 : (m + 1) * 8] for m in range(num_k // 8)]))
+            out_ref[pz * parts + n, halves * part :, :] = jnp.concatenate(rows, axis=0).astype(bf16)
+
+
+def cube_kernel(halves, quads, rows, steps, rate_ref, in_ref, out_ref, partner_ref):
+    part = quads * rows
     num_k = rate_ref.shape[0] - 8
-    steps = st_ref.shape[1]
-    st = st_ref[...]
-    h = [carry_in(ref, rate_ref, steps) for ref in (msg_ref, msgo_ref)]
-    h = jnp.concatenate(h + [jnp.zeros((F - 2 * num_k, F), f32)], axis=0)
-    row = iota((F, F), 0)
-    for z in range(2 * halves):
-        of_k = [z * (cols // F) + j for j in range(cols // F)]
-        h_k = [jnp.where((row == k) | (row == k + num_k), h, 0.0) for k in of_k]
-        g = g_ref[z] if z < g_ref.shape[0] else product(st, r_ref, ro_ref, slice(z * cols, (z + 1) * cols))
-        g = g - jnp.dot(a_ref[...], jnp.concatenate(h_k, axis=1).astype(bf16), preferred_element_type=f32)
-        g = g.astype(bf16).reshape(parts, quads, rows, cols)
-        for n in range(parts):
-            out_ref[z % 2 * parts + n, z // 2] = g[n]
-
-
-def cube_kernel(in_ref, out_ref):
-    for half in range(out_ref.shape[0]):
-        out_ref[half] = jnp.sum(in_ref[:, half].astype(f32), axis=0).astype(out_ref.dtype)
-
-
-def final_kernel(norm, x_ref, y_ref):
-    y_ref[...] = jnp.sum(x_ref[...].astype(f32), axis=0) * norm
+    extra = in_ref[:, halves * part :, :].astype(f32)
+    sources = range(in_ref.shape[0])
+
+    def all_of(first):
+        return jnp.concatenate([extra[n, first : first + 2] for n in sources], axis=0)
+
+    def own(n):
+        block = in_ref[n, halves * part :, :].astype(f32)
+        return jnp.concatenate([block[24:, m * F : (m + 1) * F] for m in range(num_k // 8)], axis=0), block[16:17, :F]
+
+    z, core = lax.axis_index("z"), lax.axis_index("c")
+    label = z % 2 * 4 + own_place("y")[0] * 2 + own_place("x")[0]
+    (mine, my_free), (other, other_free) = own(label), own(label ^ 4)
+    partner_ref[:num_k, :] = other
+    partner_ref[num_k:, :] = jnp.broadcast_to(other_free, (8, F))
+    first = z % 2 == core
+    through = jnp.exp(steps * rate_ref[:num_k, :])
+    early, late = jnp.where(first, mine, other), jnp.where(first, other, mine)
+    joined = early + through * jnp.where(first, my_free, other_free) * late
+    apart = (core == 1) & ((z == 0) | (z == SIZES[0] - 1))
+    joined = jnp.where(apart, early, joined)
+    both = jnp.broadcast_to(my_free * other_free, (num_k, F))
+
+    free = all_of(4 * halves)
+    for half in range(halves):
+        total = jnp.sum(in_ref[:, half * part : (half + 1) * part, :].astype(f32), axis=0).astype(bf16)
+        carries, at = all_of(2 * half).astype(bf16), all_of(2 * halves + 2 * half)
+        for quad in range(quads):
+            here = slice(quad * rows, (quad + 1) * rows)
+            beside = [at[:, j * F + quad * rows : j * F + (quad + 1) * rows] for j in range(at.shape[1] // F)]
+            beside += [free[:, :rows], both[:, :rows], joined]
+            out_ref[half * quads + quad, :rows, :] = total[here]
+            out_ref[half * quads + quad, rows : rows + 16, :] = carries
+            out_ref[half * quads + quad, rows + 16 :, :] = jnp.concatenate(beside, axis=1).astype(bf16)
+
+
+def final_kernel(norm, steps, rate_ref, x_ref, y_ref):
+    rows, cols = y_ref.shape
+    per = cols // F
+    z_here, core = lax.axis_index("z"), lax.axis_index("c")
+    pz = z_here % 2
+    nz, places = SIZES[0], x_ref.shape[0] // (SIZES[0] // 2)
+
+    def cube_of(z):
+        if z % 2:
+            other = jnp.where(pz == 1, (z - 1) // 2, (z + 1) // 2)
+        else:
+            other = jnp.where(pz == 1, (z // 2 + nz // 2 - 1) % (nz // 2), z // 2)
+        return jnp.where(core == 0, z // 2, other) % (nz // 2)
+
+    def units(z, first):
+        n, top = cube_of(z), first + z % 2 * 8
+        return jnp.concatenate([x_ref[n * places + p, top : top + 8, :].astype(f32) for p in range(places)], axis=0)
+
+    k = [rate_ref[pl.ds(z_here * per + j, 1), :] for j in range(per)]
+    through = jnp.exp(steps * jnp.concatenate(k, axis=1))
+    later = jnp.zeros((8 * places, cols), f32)
+    h, at = [], []
+    for z in range(nz - 1, -1, -1):
+        beside = units(z, rows + 16)
+        h.append(later)
+        at.append(beside[:, :F])
+        later = units(z, rows) + through * beside[:, per * rows : per * rows + 1] * later
+    h = jnp.concatenate(h, axis=0).astype(bf16)
+    at = jnp.concatenate(at, axis=0).astype(bf16)
+    part = lax.dot_general(at, h, (((0,), (0,)), ((), ())), preferred_element_type=f32)
+    part = jnp.concatenate([part[j * rows : (j + 1) * rows, j * F : (j + 1) * F] for j in range(per)], axis=1)
+    total = jnp.sum(x_ref[:, :rows, :].astype(f32), axis=0)
+    y_ref[...] = (total - part) * norm
 
 
 def whole(shape):
@@ -279,15 +364,14 @@
     half, parts, quads = nz // 2, 4, ny * nx // 4
     tall = parts * quads * rows
     shape = jax.ShapeDtypeStruct
-    resid, st, g_local, msg, rates, still_open = pl.pallas_call(
+    resid, st, g_local, rates, still_open = pl.pallas_call(
         local_kernel,
         in_specs=[HBM] * 6,
-        out_specs=[VMEM] * 6,
+        out_specs=[VMEM] * 5,
         out_shape=[
-            shape((steps, kf + F + tall), bf16),
+            shape((steps, kf + F + tall + F), bf16),
             shape((tall, steps), bf16),
             shape((steps, kf), f32),
-            shape((nz, num_k + 8, F), f32),
             shape((num_k + 8, F), f32),
             shape((steps, F), f32),
         ],
@@ -307,58 +391,44 @@
         for array in (horizon_gap, trace_gap, episode_end, states[0], feature_head, successor_head)
     ])
     resid_other = lax.ppermute(resid, "c", swap)
-    msg = lax.all_to_all(msg, "z", 0, 0, tiled=True)
-    msg, resid_other = lax.optimization_barrier((msg, resid_other))
-    msg_other = lax.ppermute(msg, "c", swap)
-    chunk = (half, quads, rows, cols)
-
-    early, factor = pl.pallas_call(
-        functools.partial(early_kernel, num_k),
+    deep = half * quads * rows + 32
+    grad = pl.pallas_call(
+        functools.partial(grad_kernel, num_k),
         in_specs=[VMEM] * 3,
-        out_specs=[VMEM] * 2,
-        out_shape=[shape((EARLY, tall, cols), f32), shape((tall, F), bf16)],
-        compiler_params=params(12),
-        cost_estimate=pl.CostEstimate(flops=2 * EARLY * tall * steps * cols * 2, bytes_accessed=4 * MIB, transcendentals=0),
-        name="early",
-    )(st, resid, resid_other)
-    grad = pl.pallas_call(
-        grad_kernel,
-        in_specs=[VMEM] * 8,
         out_specs=VMEM,
-        out_shape=shape((2 * parts, *chunk), bf16),
+        out_shape=shape((2 * parts, deep, cols), bf16),
         compiler_params=params(12),
         name="grad",
-    )(st, resid, resid_other, msg, msg_other, rates, early, factor)
-    grad = lax.all_to_all(grad.reshape(2 * parts, -1, cols), AXES, 0, 0, axis_index_groups=cubes())
-    grad = pl.pallas_call(
-        cube_kernel,
-        in_specs=[VMEM],
-        out_specs=VMEM,
-        out_shape=shape(chunk, bf16),
+    )(st, resid, resid_other)
+    grad = lax.all_to_all(grad, AXES, 0, 0, axis_index_groups=cubes())
+    grad, partner = pl.pallas_call(
+        functools.partial(cube_kernel, half, quads, rows, steps),
+        in_specs=[VMEM] * 2,
+        out_specs=[VMEM] * 2,
+        out_shape=[shape((half * quads, rows + 32, cols), bf16), shape((num_k + 8, F), f32)],
         compiler_params=params(12),
         name="sum_cube",
-    )(grad.reshape(2 * parts, *chunk))
-    grad, msg = lax.optimization_barrier((grad, msg))
+    )(rates, grad)
+    grad = lax.all_to_all(grad, AXES, 0, 0, axis_index_groups=alike())
     returns = pl.pallas_call(
-        returns_kernel,
+        functools.partial(returns_kernel, rows),
         grid=(n,),
-        in_specs=[VMEM] * 3 + [pl.BlockSpec((steps, blk), lambda i: (0, i))],
+        in_specs=[VMEM] * 2 + [pl.BlockSpec((steps, blk), lambda i: (0, i))] + [VMEM] * 2,
         out_specs=pl.BlockSpec((steps, blk), lambda i: (0, i)),
         out_shape=shape((steps, kf), bf16),
         scratch_shapes=[pltpu.VMEM((num_k, F), f32)],
         compiler_params=params(12),
         name="returns",
-    )(msg, rates, still_open, g_local)
-    grad = lax.all_to_all(grad.reshape(-1, rows, cols), AXES, 0, 0, axis_index_groups=alike())
+    )(rates, still_open, g_local, partner, grad)
     norm = float(steps * nz * ny * nx * nc) ** -0.5
     head_grad = pl.pallas_call(
-        functools.partial(final_kernel, norm),
-        in_specs=[VMEM],
+        functools.partial(final_kernel, norm, steps),
+        in_specs=[VMEM] * 2,
         out_specs=VMEM,
         out_shape=shape((rows, cols), f32),
-        compiler_params=params(4),
+        compiler_params=params(8),
         name="sum_rest",
-    )(grad)
+    )(rates, grad)
     return returns[None], head_grad
 
 

time: 66.3 us -> 63.9 us (0.964)
  blocking collectives: 39 us -> 47.5 us
  starting transfers between devices: 8.48 us -> 3.33 us
  waiting for transfers between devices: 7.52 us -> 2.85 us
  Pallas kernels: 10.4 us -> 9.41 us
    all_to_all x2, blocking collectives: 39 us -> 47.5 us  [the longest x1 29.4 us: body(): grad = lax.all_to_all(grad, AXES, 0, 0, axis_index_groups=cubes())]
    all_to_all x1 -> x0, waiting for transfers between devices: 7.52 us -> none  [body(): lax.all_to_all(grad.reshape(-1, rows, cols), AXES, 0, 0, axis_index_group...]
    all_to_all x1 -> x0, starting transfers between devices: 3.64 us -> none  [body(): lax.all_to_all(grad.reshape(-1, rows, cols), AXES, 0, 0, axis_index_group...]
    ppermute x1, waiting for transfers between devices: 0.01 us -> 2.85 us  [body(): resid_other = lax.ppermute(resid, 'c', swap)]
    ppermute x1 -> x0, starting transfers between devices: 1.51 us -> none  [body(): msg_other = lax.ppermute(msg, 'c', swap)]
    pallas_call x6 -> x5, Pallas kernels: 10.4 us -> 9.41 us  [the longest x1 4.48 us: body(): pl.pallas_call(local_kernel, in_specs=[HBM] * 6, out_specs=[VMEM] * 5, ou...]
  transfers between devices with their start and end apart: 3 -> 1, of which waited for: 1 -> 1; matrix products, arithmetic and copies ran while one was open for 0% -> 0% of each run, Pallas kernels for 5% -> 0%
where the time goes in v5:
time: 63.9 us; the launch traced here: 63.8 us
  blocking collectives  47.5 us (74%)
  Pallas kernels  9.41 us (15%)
  starting transfers between devices  3.33 us (5%)
  waiting for transfers between devices  2.85 us (4%)
  between operations  0.66 us (1%)
    all_to_all x1, blocking collectives, body(): grad = lax.all_to_all(grad, AXES, 0, 0, axis_index_groups=cubes())  29.4 us
    all_to_all x1, blocking collectives, body(): grad = lax.all_to_all(grad, AXES, 0, 0, axis_index_groups=alike())  18.2 us
    pallas_call x1, Pallas kernels, body(): pl.pallas_call(local_kernel, in_specs=[HBM] * 6, out_specs=[VMEM] * 5, ou...  4.48 us
    ppermute x1, starting transfers between devices, body(): resid_other = lax.ppermute(resid, 'c', swap)  3.33 us
    ppermute x1, waiting for transfers between devices, body(): resid_other = lax.ppermute(resid, 'c', swap)  2.85 us
    pallas_call x1, Pallas kernels, body(): pl.pallas_call(functools.partial(returns_kernel, rows), grid=(n,), in_spe...  2.22 us
    pallas_call x1, Pallas kernels, body(): pl.pallas_call(functools.partial(grad_kernel, num_k), in_specs=[VMEM] * 3...  1.39 us
  transfers between devices with their start and end apart: 1, of which 1 were waited for; matrix products, arithmetic and copies ran while one was open for 0% of the time, Pallas kernels for 0%

profile of v5, /device:TPU:1, one launch (start us, length us, event | category | flops | bytes accessed | tf_op | source)
XLA Modules:
  0.0 63.8 jit_solution(2020649028907121957)
XLA Ops:
  0.6 4.5 %local.1 = (bf16[256,2816]{1,0:T(8,128)(2,1)S(1)}, bf16[512,256]{1,0:T(8,128)(2,1)S(1)}, f32[256,2048]{1,0:T(8,128)S(1)}, f32[24,128]{1,0:T(8,128)S(1)}, f32[256,128]{1,0:T(8,128)S(1)}) custom-call(f32[16]{0:T(128)} %hg_hbm.1, f32[16]{0:T(128)} %tg_hbm.1, s32[1,256]{1,0:T(1,128)} %end_hbm.1, bf16[256,1024]{1,0:T(8,128)(2,1)} %bitcast.3, ...), custom_call_target="tpu_custom_call" | custom-call | tf_op jit(solution)/shard_map/local/pallas_call | solution.py:367
  5.1 3.3 %collective-permute-start = (bf16[256,2816]{1,0:T(8,128)(2,1)S(1)}, bf16[256,2816]{1,0:T(8,128)(2,1)S(1)}, u32[]{:S(2)}, u32[]{:S(2)}) collective-permute-start(bf16[256,2816]{1,0:T(8,128)(2,1)S(1)} %get-tuple-element.13.r_ref), channel_id=1, source_target_pairs={{0,1},{1,0},{2,3},{3,2},{4,5},{5,4},{6,7},{7,6},{8,9},{9,8},{10,11... | collective-permute-start | bytes 4325384 | tf_op jit(solution)/shard_map/ppermute | solution.py:393
  8.5 2.8 %collective-permute-done.ro_ref = bf16[256,2816]{1,0:T(8,128)(2,1)S(1)} collective-permute-done((bf16[256,2816]{1,0:T(8,128)(2,1)S(1)}, bf16[256,2816]{1,0:T(8,128)(2,1)S(1)}, u32[]{:S(2)}, u32[]{:S(2)}) %collective-permute-start) | collective-permute-done | bytes 1441824 | tf_op jit(solution)/shard_map/ppermute | solution.py:393
  11.3 1.4 %grad.1 = bf16[8,544,256]{2,1,0:T(8,128)(2,1)S(1)} custom-call(bf16[512,256]{1,0:T(8,128)(2,1)S(1)} %get-tuple-element.12.st_ref, bf16[256,2816]{1,0:T(8,128)(2,1)S(1)} %get-tuple-element.13.r_ref, bf16[256,2816]{1,0:T(8,128)(2,1)S(1)} %collective-permute-done.ro_ref), custom_call_target="tpu_custom_call" | custom-call | tf_op jit(solution)/shard_map/grad/pallas_call | solution.py:395
  12.7 29.4 %all_to_all.10.in_ref = bf16[8,544,256]{2,1,0:T(8,128)(2,1)S(1)} all-to-all(bf16[8,544,256]{2,1,0:T(8,128)(2,1)S(1)} %grad.1), channel_id=1, replica_groups={{0,2,8,10,32,34,40,42},{6,4,14,12,38,36,46,44},{24,26,16,18,56,58,48,50..., dimensions={0} | all-to-all | bytes 4456448 | tf_op jit(solution)/shard_map/all_to_all | solution.py:403
  42.1 0.4 sum_cube.1
  42.5 18.2 %all_to_all.11.x_ref = bf16[16,64,256]{2,1,0:T(8,128)(2,1)S(1)} all-to-all(bf16[16,64,256]{2,1,0:T(8,128)(2,1)S(1)} %get-tuple-element.15), channel_id=1, replica_groups={{0,6,24,30,64,70,88,94,128,134,152,158,192,198,216,222},{2,4,26,28,66,6..., dimensions={0} | all-to-all | bytes 1048576 | tf_op jit(solution)/shard_map/all_to_all | solution.py:412
  60.7 0.9 %sum_rest.1 = f32[32,256]{1,0:T(8,128)} custom-call(f32[24,128]{1,0:T(8,128)S(1)} %get-tuple-element.9.rate_ref, bf16[16,64,256]{2,1,0:T(8,128)(2,1)S(1)} %all_to_all.11.x_ref), custom_call_target="tpu_custom_call" | custom-call | tf_op jit(solution)/shard_map/sum_rest/pallas_call | solution.py:424
  61.5 2.2 %returns.1 = bf16[256,2048]{1,0:T(8,128)(2,1)} custom-call(f32[24,128]{1,0:T(8,128)S(1)} %get-tuple-element.9.rate_ref, f32[256,128]{1,0:T(8,128)S(1)} %get-tuple-element.10.open_ref, f32[256,2048]{1,0:T(8,128)S(1)} %get-tuple-element.11.g_ref, f32[24,128]{1,0:T(8,128)S(1)} %get-tuple-element.14.partner_ref, bf16[16,64,256]{2,1,0:T(8,128)(2,1)S(1)} %all_to_all.11.x_ref), custom_call_target="tpu_custom_call" | custom-call | tf_op jit(solution)/shard_map/returns/pallas_call | solution.py:413
Async XLA Ops:
  5.1 6.2 %collective-permute-start = (bf16[256,2816]{1,0:T(8,128)(2,1)S(1)}, bf16[256,2816]{1,0:T(8,128)(2,1)S(1)}, u32[]{:S(2)}, u32[]{:S(2)}) collective-permute-start(bf16[256,2816]{1,0:T(8,128)(2,1)S(1)} %get-tuple-element.13.r_ref), channel_id=1, source_target_pairs={{0,1},{1,0},{2,3},{3,2},{4,5},{5,4},{6,7},{7,6},{8,9},{9,8},{10,11... | collective-permute-start | bytes 4325384 | tf_op jit(solution)/shard_map/ppermute | solution.py:393

commit v6 on v5

--- a/solution.py
+++ b/solution.py
@@ -47,17 +47,44 @@
     return (gray, half) if core == 0 else (half, gray)
 
 
-def local_kernel(hg_hbm, tg_hbm, end_hbm, s_hbm, wf_hbm, w_hbm, r_ref, st_ref, g_ref, rate_ref, open_ref,
-                 hg_ref, tg_ref, end_ref, s_ref, wf_ref, w_ref, sems):
+def scan_block(first, top, pred, f, mask, rate_ref, coef_ref, r_ref, g_ref):
+    steps = pred.shape[0]
+    per, num_k = pred.shape[1] // F, coef_ref.shape[0] // 2
+    scaled, backs, biased, carries = [], [], [], []
+    for j in range(per):
+        k = first + j
+        log_rate, scale = rate_ref[k : k + 1, :], coef_ref[k : k + 1, :]
+        p = pred[:, j * F : (j + 1) * F].astype(f32)
+        biased.append((p, coef_ref[num_k + k : num_k + k + 1, :] * p))
+        scaled.append(powers(log_rate, steps) * (scale * f + biased[j][1]))
+        backs.append(powers(-log_rate, steps))
+    scaled = jnp.concatenate(scaled, axis=1)
+    high = scaled.astype(bf16)
+    low = (scaled - high.astype(f32)).astype(bf16)
+    sums = jnp.dot(mask, high, preferred_element_type=f32)
+    sums = sums + jnp.dot(mask, low, preferred_element_type=f32)
+    for j in range(per):
+        cols = slice((first - top + j) * F, (first - top + j + 1) * F)
+        h = backs[j] * sums[:, j * F : (j + 1) * F]
+        g = h - biased[j][1]
+        g_ref[:, cols] = g
+        r_ref[:, cols] = (biased[j][0] - g).astype(bf16)
+        carries.append(h[:1])
+    return carries
+
+
+def local_kernel(hg_hbm, tg_hbm, end_hbm, s_hbm, wf_hbm, w_hbm, r_ref, st_ref, g_ref, rate_ref, open_ref, coef_ref,
+                 f_ref, mask_ref, s_ref, wl_ref, hg_ref, tg_ref, end_ref, wf_ref, w_ref, sems):
     blocks, _, blk = w_ref.shape
     steps, width = s_ref.shape
     num_k = hg_ref.shape[0]
-    kf = blocks * blk
+    half = blocks * blk
     copies = [
         pltpu.make_async_copy(a, b, sems.at[n])
         for n, (a, b) in enumerate(
             [(hg_hbm, hg_ref), (tg_hbm, tg_ref), (end_hbm, end_ref), (s_hbm, s_ref), (wf_hbm, wf_ref)]
             + [(w_hbm.at[:, i * blk : (i + 1) * blk], w_ref.at[i]) for i in range(blocks)]
+            + [(w_hbm.at[:, half:], wl_ref)]
         )
     ]
     for copy in copies:
@@ -72,114 +99,79 @@
     at_col = jnp.dot(ended, above, preferred_element_type=f32)
     at_rows = jnp.concatenate([at_row] * (steps // F), axis=1)
     mask = jnp.where((at_rows == at_col) & (cols >= rows), 1.0, 0.0).astype(bf16)
+    mask_ref[...] = mask
     total = jnp.sum(ended_row, axis=1, keepdims=True)
     still = jnp.where(at_row == total, 1.0, 0.0)
     open_ref[...] = still
-    free = jnp.where(total == 0.0, 1.0, 0.0)
     lane = iota((1, F), 1)
     by_lane = jnp.zeros((1, F), f32)
     for k in range(num_k):
-        log_rate = coefficients(hg_ref, tg_ref, k)[0]
+        log_rate, scale, beta = coefficients(hg_ref, tg_ref, k)
         rate_ref[k : k + 1, :] = log_rate
+        coef_ref[k : k + 1, :] = scale
+        coef_ref[num_k + k : num_k + k + 1, :] = beta
         by_lane = jnp.where(lane % num_k == k, log_rate, by_lane)
     rate_ref[num_k:, :] = jnp.broadcast_to(by_lane, (8, F))
-    r_ref[:, kf : kf + F] = (still * backwards(by_lane, steps)).astype(bf16)
+    r_ref[:, half : half + F] = (still * backwards(by_lane, steps)).astype(bf16)
 
     for copy in copies[3:5]:
         copy.wait()
     s = s_ref[...]
     f = jnp.dot(s, wf_ref[...], preferred_element_type=f32)
-    per = blk // F
+    f_ref[...] = f
+    st = s.T
+    here = lax.axis_index("c")
+    tall = st_ref.shape[0] // (SIZES[1] * SIZES[2])
+    for n in range(st.shape[0] // tall):
+        y, x, core = n // (SIZES[2] * SIZES[3]), n // SIZES[3] % SIZES[2], n % SIZES[3]
+        (ly, iy), (lx, ix) = place_in_cube(y, core), place_in_cube(x, core)
+        at = (ly * 2 + lx) * 4 + iy * 2 + ix
+        part = st[n * tall : (n + 1) * tall, :]
+
+        @pl.when(here == core)
+        def _():
+            st_ref[at * tall : (at + 1) * tall, :] = part
+
+        @pl.when(here != core)
+        def _():
+            left, top = half + F + at // (steps // tall) * steps, at % (steps // tall) * tall
+            r_ref[top : top + tall, left : left + steps] = part
 
     def predict(i):
         copies[5 + i].wait()
         return jnp.dot(s, w_ref[i], preferred_element_type=f32).astype(bf16)
 
-    def turn():
-        st = s.T
-        here = lax.axis_index("c")
-        tall = st_ref.shape[0] // (SIZES[1] * SIZES[2])
-        for n in range(st.shape[0] // tall):
-            y, x, core = n // (SIZES[2] * SIZES[3]), n // SIZES[3] % SIZES[2], n % SIZES[3]
-            (ly, iy), (lx, ix) = place_in_cube(y, core), place_in_cube(x, core)
-            at = (ly * 2 + lx) * 4 + iy * 2 + ix
-            part = st[n * tall : (n + 1) * tall, :]
-
-            @pl.when(here == core)
-            def _():
-                st_ref[at * tall : (at + 1) * tall, :] = part
-
-            @pl.when(here != core)
-            def _():
-                left, top = kf + F + at // (steps // tall) * steps, at % (steps // tall) * tall
-                r_ref[top : top + tall, left : left + steps] = part
-
-    turn()
     following = predict(0)
     carries = []
     for i in range(blocks):
         pred = following
         if i + 1 < blocks:
             following = predict(i + 1)
-        scaled, backs, biased = [], [], []
-        for j in range(per):
-            log_rate, scale, beta = coefficients(hg_ref, tg_ref, i * per + j)
-            p = pred[:, j * F : (j + 1) * F].astype(f32)
-            biased.append((p, beta * p))
-            scaled.append(powers(log_rate, steps) * (scale * f + biased[j][1]))
-            backs.append(powers(-log_rate, steps))
-        scaled = jnp.concatenate(scaled, axis=1)
-        high = scaled.astype(bf16)
-        low = (scaled - high.astype(f32)).astype(bf16)
-        sums = jnp.dot(mask, high, preferred_element_type=f32)
-        sums = sums + jnp.dot(mask, low, preferred_element_type=f32)
-        for j in range(per):
-            k = i * per + j
-            cols = slice(k * F, (k + 1) * F)
-            h = backs[j] * sums[:, j * F : (j + 1) * F]
-            g = h - biased[j][1]
-            g_ref[:, cols] = g
-            r_ref[:, cols] = (biased[j][0] - g).astype(bf16)
-            carries.append(h[:1])
+        carries += scan_block(i * blk // F, 0, pred, f, mask, rate_ref, coef_ref, r_ref, g_ref)
     last = r_ref.shape[1] - F
+    free = jnp.where(total == 0.0, 1.0, 0.0)
+    carries += [jnp.zeros((num_k - len(carries), F), f32)]
     r_ref[:num_k, last:] = jnp.concatenate(carries, axis=0).astype(bf16)
     r_ref[num_k:, last:] = jnp.broadcast_to(free, (steps - num_k, F)).astype(bf16)
+    copies[-1].wait()
+
+
+def rest_kernel(s_ref, w_ref, f_ref, mask_ref, rate_ref, coef_ref, r_ref, g_ref):
+    num_k = coef_ref.shape[0] // 2
+    half = w_ref.shape[1]
+    blk = half // 2
+    carries = []
+    for i in range(2):
+        pred = jnp.dot(s_ref[...], w_ref[:, i * blk : (i + 1) * blk], preferred_element_type=f32).astype(bf16)
+        first = num_k - half // F
+        carries += scan_block(first + i * blk // F, first, pred, f_ref[...], mask_ref[...], rate_ref, coef_ref, r_ref, g_ref)
+    carries += [jnp.zeros((num_k - len(carries), F), f32)]
+    r_ref[:num_k, half:] = jnp.concatenate(carries, axis=0).astype(bf16)
+    r_ref[num_k:, half:] = jnp.zeros((r_ref.shape[0] - num_k, F), bf16)
 
 
 def backwards(log_rate, steps):
     return jnp.exp(steps * log_rate) * powers(-log_rate, steps)
-
-
-def returns_kernel(rows, rate_ref, open_ref, g_ref, partner_ref, x_ref, out_ref, h_ref):
-    steps = g_ref.shape[0]
-    per = g_ref.shape[1] // F
-    i = pl.program_id(0)
-
-    @pl.when(i == 0)
-    def _():
-        num_k = h_ref.shape[0]
-        z, core = lax.axis_index("z"), lax.axis_index("c")
-        (_, iy), (_, ix) = own_place("y"), own_place("x")
-        through = jnp.exp(steps * rate_ref[:num_k, :])
-        places = x_ref.shape[0] // (SIZES[0] // 2)
-
-        def pair(n):
-            block = x_ref[n * places + iy * 2 + ix, rows + 16 :, :].astype(f32)
-            return block[:, F:], block[:, F - 32 : F - 31]
-
-        later = jnp.where((core == 1) & (z % 2 == 0), pair(0)[0], 0.0)
-        for n in range(SIZES[0] // 2 - 1, 0, -1):
-            carry, free = pair(n)
-            later = jnp.where(n > z // 2, carry + through * through * free * later, later)
-        after = partner_ref[:num_k, :] + through * partner_ref[num_k : num_k + 1, :] * later
-        h_ref[...] = jnp.where((z % 2 == core) & (z < SIZES[0] - 1), after, later)
-
-    still = open_ref[...]
-    for j in range(per):
-        k = pl.ds(i * per + j, 1)
-        cols = slice(j * F, (j + 1) * F)
-        decay = still * backwards(rate_ref[k, :], steps)
-        out_ref[:, cols] = (g_ref[:, cols] + decay * h_ref[k, :]).astype(bf16)
 
 
 def own_place(axis):
@@ -189,26 +181,42 @@
     )
 
 
-def grad_kernel(num_k, st_ref, r_ref, ro_ref, out_ref):
+def columns_of(st, sto, r_ref, ro_ref, at):
+    g = jnp.dot(st, r_ref[:, at], preferred_element_type=f32)
+    return (g + jnp.dot(sto, ro_ref[:, at], preferred_element_type=f32)).astype(bf16)
+
+
+def early_kernel(num_k, st_ref, r_ref, ro_ref, g_ref, sto_ref, at_ref):
+    tall, steps = st_ref.shape
+    count, _, cols = g_ref.shape
+    half, last = count * cols, r_ref.shape[1] - F
+    st = st_ref[...]
+    sto = jnp.concatenate([ro_ref[:, n : n + steps] for n in range(half + F, last, steps)], axis=0)
+    sto_ref[...] = sto
+    lane = iota((tall, F), 1)
+    a = jnp.dot(st, r_ref[:, half : half + F], preferred_element_type=f32)
+    a = jnp.where(lane < num_k, a, jnp.dot(sto, ro_ref[:, half : half + F], preferred_element_type=f32))
+    at_ref[...] = a.T
+    for z in range(count):
+        g_ref[z] = columns_of(st, sto, r_ref, ro_ref, slice(z * cols, (z + 1) * cols))
+
+
+def grad_kernel(num_k, st_ref, sto_ref, r_ref, ro_ref, rl_ref, rlo_ref, g_ref, at_ref, out_ref):
     tall, steps = st_ref.shape
     labels, deep, cols = out_ref.shape
+    count = g_ref.shape[0]
     parts, per = labels // 2, cols // F
     part = tall // parts
-    kf = num_k * F
-    halves = kf // cols // 2
+    halves = num_k * F // cols // 2
+    st, sto, at = st_ref[...], sto_ref[...], at_ref[...]
     last = r_ref.shape[1] - F
-    st = st_ref[...]
-    sto = jnp.concatenate([ro_ref[:, n : n + steps] for n in range(kf + F, last, steps)], axis=0)
-    lane = iota((tall, F), 1)
-    a = jnp.dot(st, r_ref[:, kf : kf + F], preferred_element_type=f32)
-    a = jnp.where(lane < num_k, a, jnp.dot(sto, ro_ref[:, kf : kf + F], preferred_element_type=f32))
-    at = a.T
-    carries = [ref[: num_k + 1, last:].astype(f32) for ref in (r_ref, ro_ref)]
+    carries = []
+    for first, second in ((r_ref, rl_ref), (ro_ref, rlo_ref)):
+        a, b = first[: num_k + 1, last:].astype(f32), second[: num_k // 2, count * cols :].astype(f32)
+        carries.append(jnp.concatenate([a[: num_k // 2], b, a[num_k:]], axis=0))
     for z in range(2 * halves):
-        columns = slice(z * cols, (z + 1) * cols)
-        g = jnp.dot(st, r_ref[:, columns], preferred_element_type=f32)
-        g = g + jnp.dot(sto, ro_ref[:, columns], preferred_element_type=f32)
-        g = g.astype(bf16)
+        at_z = slice((z - count) * cols, (z - count + 1) * cols)
+        g = g_ref[z] if z < count else columns_of(st, sto, rl_ref, rlo_ref, at_z)
         for n in range(parts):
             out_ref[z % 2 * parts + n, z // 2 * part : (z // 2 + 1) * part, :] = g[n * part : (n + 1) * part]
 
@@ -275,12 +283,38 @@
             out_ref[half * quads + quad, rows + 16 :, :] = jnp.concatenate(beside, axis=1).astype(bf16)
 
 
-def final_kernel(norm, steps, rate_ref, x_ref, y_ref):
+def final_kernel(norm, rate_ref, open_ref, g_ref, gl_ref, partner_ref, x_ref, out_hbm, y_hbm, out_ref, y_ref, sems):
     rows, cols = y_ref.shape
     per = cols // F
+    steps, kf = out_ref.shape
+    num_k = rate_ref.shape[0] - 8
+    nz, places = SIZES[0], x_ref.shape[0] // (SIZES[0] // 2)
     z_here, core = lax.axis_index("z"), lax.axis_index("c")
     pz = z_here % 2
-    nz, places = SIZES[0], x_ref.shape[0] // (SIZES[0] // 2)
+    (_, iy), (_, ix) = own_place("y"), own_place("x")
+
+    def pair(n):
+        block = x_ref[n * places + iy * 2 + ix, rows + 16 :, :].astype(f32)
+        return block[:, F:], block[:, F - 32 : F - 31]
+
+    through = jnp.exp(steps * rate_ref[:num_k, :])
+    later = jnp.where((core == 1) & (pz == 0), pair(0)[0], 0.0)
+    for n in range(nz // 2 - 1, 0, -1):
+        carry, free = pair(n)
+        later = jnp.where(n > z_here // 2, carry + through * through * free * later, later)
+    after = partner_ref[:num_k, :] + through * partner_ref[num_k : num_k + 1, :] * later
+    h = jnp.where((pz == core) & (z_here < nz - 1), after, later)
+    still = open_ref[...]
+    copies = []
+    for k in range(num_k):
+        at = slice(k * F, (k + 1) * F)
+        decay = still * backwards(rate_ref[k : k + 1, :], steps)
+        g = g_ref[:, at] if k < num_k // 2 else gl_ref[:, (k - num_k // 2) * F : (k - num_k // 2 + 1) * F]
+        out_ref[:, at] = (g + decay * h[k : k + 1, :]).astype(bf16)
+        if k % per == per - 1:
+            at = slice((k + 1 - per) * F, (k + 1) * F)
+            copies.append(pltpu.make_async_copy(out_ref.at[:, at], out_hbm.at[:, at], sems.at[len(copies)]))
+            copies[-1].start()
 
     def cube_of(z):
         if z % 2:
@@ -308,6 +342,10 @@
     part = jnp.concatenate([part[j * rows : (j + 1) * rows, j * F : (j + 1) * F] for j in range(per)], axis=1)
     total = jnp.sum(x_ref[:, :rows, :].astype(f32), axis=0)
     y_ref[...] = (total - part) * norm
+    copies.append(pltpu.make_async_copy(y_ref, y_hbm, sems.at[len(copies)]))
+    copies[-1].start()
+    for copy in copies:
+        copy.wait()
 
 
 def whole(shape):
@@ -364,42 +402,65 @@
     half, parts, quads = nz // 2, 4, ny * nx // 4
     tall = parts * quads * rows
     shape = jax.ShapeDtypeStruct
-    resid, st, g_local, rates, still_open = pl.pallas_call(
+    resid, st, g_local, rates, still_open, coef, features, mask, held, later_head = pl.pallas_call(
         local_kernel,
         in_specs=[HBM] * 6,
-        out_specs=[VMEM] * 5,
+        out_specs=[VMEM] * 10,
         out_shape=[
-            shape((steps, kf + F + tall + F), bf16),
+            shape((steps, kf // 2 + F + tall + F), bf16),
             shape((tall, steps), bf16),
-            shape((steps, kf), f32),
+            shape((steps, kf // 2), f32),
             shape((num_k + 8, F), f32),
             shape((steps, F), f32),
+            shape((2 * num_k, F), f32),
+            shape((steps, F), f32),
+            shape((steps, steps), bf16),
+            shape((steps, width), bf16),
+            shape((width, kf // 2), bf16),
         ],
         scratch_shapes=[
             pltpu.SMEM((num_k,), f32),
             pltpu.SMEM((num_k,), f32),
             pltpu.VMEM((1, steps), jnp.int32),
-            pltpu.VMEM((steps, width), bf16),
             pltpu.VMEM((width, F), bf16),
-            pltpu.VMEM((n, width, blk), bf16),
-            pltpu.SemaphoreType.DMA((5 + n,)),
+            pltpu.VMEM((n // 2, width, blk), bf16),
+            pltpu.SemaphoreType.DMA((6 + n // 2,)),
         ],
-        compiler_params=params(48),
+        compiler_params=params(40),
         name="local",
     )(*[
         pltpu.with_memory_space_constraint(array, pltpu.HBM)
         for array in (horizon_gap, trace_gap, episode_end, states[0], feature_head, successor_head)
     ])
     resid_other = lax.ppermute(resid, "c", swap)
+    resid_late, g_late = pl.pallas_call(
+        rest_kernel,
+        in_specs=[VMEM] * 6,
+        out_specs=[VMEM] * 2,
+        out_shape=[shape((steps, kf // 2 + F), bf16), shape((steps, kf // 2), f32)],
+        compiler_params=params(16),
+        cost_estimate=pl.CostEstimate(flops=2 * steps * width * kf, bytes_accessed=6 * MIB, transcendentals=0),
+        name="rest",
+    )(held, later_head, features, mask, rates, coef)
+    resid_late_other = lax.ppermute(resid_late, "c", swap)
     deep = half * quads * rows + 32
+    early, st_other, factors = pl.pallas_call(
+        functools.partial(early_kernel, num_k),
+        in_specs=[VMEM] * 3,
+        out_specs=[VMEM] * 3,
+        out_shape=[shape((nz // 2, tall, cols), bf16), shape((tall, steps), bf16), shape((F, tall), f32)],
+        compiler_params=params(12),
+        cost_estimate=pl.CostEstimate(flops=2 * tall * steps * kf, bytes_accessed=4 * MIB, transcendentals=0),
+        name="early",
+    )(st, resid, resid_other)
     grad = pl.pallas_call(
         functools.partial(grad_kernel, num_k),
-        in_specs=[VMEM] * 3,
+        in_specs=[VMEM] * 8,
         out_specs=VMEM,
         out_shape=shape((2 * parts, deep, cols), bf16),
         compiler_params=params(12),
         name="grad",
-    )(st, resid, resid_other)
+    )(st, st_other, resid, resid_other, resid_late, resid_late_other, early, factors)
     grad = lax.all_to_all(grad, AXES, 0, 0, axis_index_groups=cubes())
     grad, partner = pl.pallas_call(
         functools.partial(cube_kernel, half, quads, rows, steps),
@@ -410,25 +471,20 @@
         name="sum_cube",
     )(rates, grad)
     grad = lax.all_to_all(grad, AXES, 0, 0, axis_index_groups=alike())
-    returns = pl.pallas_call(
-        functools.partial(returns_kernel, rows),
-        grid=(n,),
-        in_specs=[VMEM] * 2 + [pl.BlockSpec((steps, blk), lambda i: (0, i))] + [VMEM] * 2,
-        out_specs=pl.BlockSpec((steps, blk), lambda i: (0, i)),
-        out_shape=shape((steps, kf), bf16),
-        scratch_shapes=[pltpu.VMEM((num_k, F), f32)],
+    norm = float(steps * nz * ny * nx * nc) ** -0.5
+    returns, head_grad = pl.pallas_call(
+        functools.partial(final_kernel, norm),
+        in_specs=[VMEM] * 6,
+        out_specs=[HBM] * 2,
+        out_shape=[shape((steps, kf), bf16), shape((rows, cols), f32)],
+        scratch_shapes=[
+            pltpu.VMEM((steps, kf), bf16),
+            pltpu.VMEM((rows, cols), f32),
+            pltpu.SemaphoreType.DMA((kf // cols + 1,)),
+        ],
         compiler_params=params(12),
-        name="returns",
-    )(rates, still_open, g_local, partner, grad)
-    norm = float(steps * nz * ny * nx * nc) ** -0.5
-    head_grad = pl.pallas_call(
-        functools.partial(final_kernel, norm, steps),
-        in_specs=[VMEM] * 2,
-        out_specs=VMEM,
-        out_shape=shape((rows, cols), f32),
-        compiler_params=params(8),
-        name="sum_rest",
-    )(rates, grad)
+        name="final",
+    )(rates, still_open, g_local, g_late, partner, grad)
     return returns[None], head_grad
 
 

time: 63.9 us -> 61.7 us (0.966)
  waiting for transfers between devices: 2.85 us -> 1.13 us
    ppermute x1, waiting for transfers between devices: 2.85 us -> 0.4 us  [body(): resid_other = lax.ppermute(resid, 'c', swap)]
    ppermute x0 -> x1, waiting for transfers between devices: none -> 0.74 us  [body(): resid_late_other = lax.ppermute(resid_late, 'c', swap)]
    pallas_call x4 -> x5, Pallas kernels: 8.97 us -> 8.43 us  [the longest x1 3.18 us: body(): pl.pallas_call(local_kernel, in_specs=[HBM] * 6, out_specs=[VMEM] * 10, o...]
  transfers between devices with their start and end apart: 1 -> 2, of which waited for: 1 -> 2; matrix products, arithmetic and copies ran while one was open for 0% -> 0% of each run, Pallas kernels for 0% -> 4%
where the time goes in v6:
time: 61.7 us; the launch traced here: 61.4 us
  blocking collectives  47.3 us (77%)
  Pallas kernels  8.87 us (14%)
  starting transfers between devices  3.44 us (6%)
  waiting for transfers between devices  1.13 us (2%)
  between operations  0.67 us (1%)
    all_to_all x1, blocking collectives, body(): grad = lax.all_to_all(grad, AXES, 0, 0, axis_index_groups=cubes())  29.4 us
    all_to_all x1, blocking collectives, body(): grad = lax.all_to_all(grad, AXES, 0, 0, axis_index_groups=alike())  17.9 us
    ppermute x1, starting transfers between devices, body(): resid_other = lax.ppermute(resid, 'c', swap)  3.33 us
    pallas_call x1, Pallas kernels, body(): pl.pallas_call(local_kernel, in_specs=[HBM] * 6, out_specs=[VMEM] * 10, o...  3.18 us
    pallas_call x1, Pallas kernels, body(): pl.pallas_call(functools.partial(final_kernel, norm), in_specs=[VMEM] * 6...  2.01 us
    pallas_call x1, Pallas kernels, body(): pl.pallas_call(rest_kernel, in_specs=[VMEM] * 6, out_specs=[VMEM] * 2, ou...  1.59 us
  transfers between devices with their start and end apart: 2, of which 2 were waited for; matrix products, arithmetic and copies ran while one was open for 0% of the time, Pallas kernels for 4%

profile of v6, /device:TPU:1, one launch (start us, length us, event | category | flops | bytes accessed | tf_op | source)
XLA Modules:
  0.0 61.4 jit_solution(10342640409010503822)
XLA Ops:
  0.6 3.2 %local.1 = (bf16[256,1792]{1,0:T(8,128)(2,1)S(1)}, bf16[512,256]{1,0:T(8,128)(2,1)S(1)}, f32[256,1024]{1,0:T(8,128)S(1)}, f32[24,128]{1,0:T(8,128)S(1)}, f32[256...) custom-call(f32[16]{0:T(128)} %hg_hbm.1, ...), custom_call_target="tpu_custom_call" | custom-call | tf_op jit(solution)/shard_map/local/pallas_call | solution.py:405
  3.8 3.3 %collective-permute-start = (bf16[256,1792]{1,0:T(8,128)(2,1)S(1)}, bf16[256,1792]{1,0:T(8,128)(2,1)S(1)}, u32[]{:S(2)}, u32[]{:S(2)}) collective-permute-start(bf16[256,1792]{1,0:T(8,128)(2,1)S(1)} %get-tuple-element.31.r_ref), channel_id=1, source_target_pairs={{0,1},{1,0},{2,3},{3,2},{4,5},{5,4},{6,7},{7,6},{8,9},{9,8},{10,11... | collective-permute-start | bytes 2752520 | tf_op jit(solution)/shard_map/ppermute | solution.py:435
  7.1 1.6 %rest.1 = (bf16[256,1152]{1,0:T(8,128)(2,1)S(1)}, f32[256,1024]{1,0:T(8,128)S(1)}) custom-call(bf16[256,1024]{1,0:T(8,128)(2,1)S(1)} %get-tuple-element.24.s_ref, bf16[1024,1024]{1,0:T(8,128)(2,1)S(1)} %get-tuple-element.25.w_ref, f32[256,128]{1,0:T(8,128)S(1)} %get-tuple-element.26.f_ref, bf16[256,256]{1,0:T(8,128)(2,1)S(1)} %get-tuple-element.27.mask_ref, ...), custom_call_target="tpu_custom_call" | custom-call | flops 1073741824 | bytes 6291456 | tf_op jit(solution)/shard_map/rest/pallas_call | solution.py:436
  8.7 0.1 collective-permute-start.1
  8.9 0.4 collective-permute-done.ro_ref
  9.2 0.8 %early.1 = (bf16[4,512,256]{2,1,0:T(8,128)(2,1)S(1)}, bf16[512,256]{1,0:T(8,128)(2,1)S(1)}, f32[128,512]{1,0:T(8,128)S(1)}) custom-call(bf16[512,256]{1,0:T(8,128)(2,1)S(1)} %get-tuple-element.30.st_ref, bf16[256,1792]{1,0:T(8,128)(2,1)S(1)} %get-tuple-element.31.r_ref, bf16[256,1792]{1,0:T(8,128)(2,1)S(1)} %collective-permute-done.ro_ref), custom_call_target="tpu_custom_call" | custom-call | flops 536870912 | bytes 4194304 | tf_op jit(solution)/shard_map/early/pallas_call | solution.py:447
  10.1 0.7 %collective-permute-done.1.rlo_ref = bf16[256,1152]{1,0:T(8,128)(2,1)S(1)} collective-permute-done((bf16[256,1152]{1,0:T(8,128)(2,1)S(1)}, bf16[256,1152]{1,0:T(8,128)(2,1)S(1)}, u32[]{:S(2)}, u32[]{:S(2)}) %collective-permute-start.1) | collective-permute-done | bytes 589856 | tf_op jit(solution)/shard_map/ppermute | solution.py:445
  10.8 0.8 %grad.1 = bf16[8,544,256]{2,1,0:T(8,128)(2,1)S(1)} custom-call(bf16[512,256]{1,0:T(8,128)(2,1)S(1)} %get-tuple-element.30.st_ref, bf16[512,256]{1,0:T(8,128)(2,1)S(1)} %get-tuple-element.32.sto_ref, bf16[256,1792]{1,0:T(8,128)(2,1)S(1)} %get-tuple-element.31.r_ref, bf16[256,1792]{1,0:T(8,128)(2,1)S(1)} %collective-permute-done.ro_ref, ...), custom_call_target="tpu_custom_call" | custom-call | tf_op jit(solution)/shard_map/grad/pallas_call | solution.py:456
  11.7 29.4 %all_to_all.10.in_ref = bf16[8,544,256]{2,1,0:T(8,128)(2,1)S(1)} all-to-all(bf16[8,544,256]{2,1,0:T(8,128)(2,1)S(1)} %grad.1), channel_id=1, replica_groups={{0,2,8,10,32,34,40,42},{6,4,14,12,38,36,46,44},{24,26,16,18,56,58,48,50..., dimensions={0} | all-to-all | bytes 4456448 | tf_op jit(solution)/shard_map/all_to_all | solution.py:464
  41.0 0.4 sum_cube.1
  41.5 17.9 %all_to_all.11.x_ref = bf16[16,64,256]{2,1,0:T(8,128)(2,1)S(1)} all-to-all(bf16[16,64,256]{2,1,0:T(8,128)(2,1)S(1)} %get-tuple-element.37), channel_id=1, replica_groups={{0,6,24,30,64,70,88,94,128,134,152,158,192,198,216,222},{2,4,26,28,66,6..., dimensions={0} | all-to-all | bytes 1048576 | tf_op jit(solution)/shard_map/all_to_all | solution.py:473
  59.4 2.0 %final.1 = (bf16[256,2048]{1,0:T(8,128)(2,1)}, f32[32,256]{1,0:T(8,128)}) custom-call(f32[24,128]{1,0:T(8,128)S(1)} %get-tuple-element.21.rate_ref, f32[256,128]{1,0:T(8,128)S(1)} %get-tuple-element.22.open_ref, f32[256,1024]{1,0:T(8,128)S(1)} %get-tuple-element.23.g_ref, f32[256,1024]{1,0:T(8,128)S(1)} %get-tuple-element.29.gl_ref, ...), custom_call_target="tpu_custom_call" | custom-call | tf_op jit(solution)/shard_map/final/pallas_call | solution.py:475
Async XLA Ops:
  3.8 5.4 %collective-permute-start = (bf16[256,1792]{1,0:T(8,128)(2,1)S(1)}, bf16[256,1792]{1,0:T(8,128)(2,1)S(1)}, u32[]{:S(2)}, u32[]{:S(2)}) collective-permute-start(bf16[256,1792]{1,0:T(8,128)(2,1)S(1)} %get-tuple-element.31.r_ref), channel_id=1, source_target_pairs={{0,1},{1,0},{2,3},{3,2},{4,5},{5,4},{6,7},{7,6},{8,9},{9,8},{10,11... | collective-permute-start | bytes 2752520 | tf_op jit(solution)/shard_map/ppermute | solution.py:435
  8.7 2.1 %collective-permute-start.1 = (bf16[256,1152]{1,0:T(8,128)(2,1)S(1)}, bf16[256,1152]{1,0:T(8,128)(2,1)S(1)}, u32[]{:S(2)}, u32[]{:S(2)}) collective-permute-start(bf16[256,1152]{1,0:T(8,128)(2,1)S(1)} %get-tuple-element.33.rl_ref), channel_id=1, source_target_pairs={{0,1},{1,0},{2,3},{3,2},{4,5},{5,4},{6,7},{7,6},{8,9},{9,8},{10,11... | collective-permute-start | bytes 1769480 | tf_op jit(solution)/shard_map/ppermute | solution.py:445

commit v7 on v6

--- a/solution.py
+++ b/solution.py
@@ -271,16 +271,40 @@
     both = jnp.broadcast_to(my_free * other_free, (num_k, F))
 
     free = all_of(4 * halves)
+    count = free.shape[0] // 2
+
+    def in_time(x):
+        return jnp.where(core == 0, x[:count], x[count:]), jnp.where(core == 0, x[count:], x[:count])
+
+    free_early, free_late = in_time(free)
+    per = in_ref.shape[2] // F
     for half in range(halves):
-        total = jnp.sum(in_ref[:, half * part : (half + 1) * part, :].astype(f32), axis=0).astype(bf16)
-        carries, at = all_of(2 * half).astype(bf16), all_of(2 * halves + 2 * half)
+        k = [rate_ref[pl.ds((2 * half + z % 2) * per + j, 1), :] for j in range(per)]
+        through_k = jnp.exp(steps * jnp.concatenate(k, axis=1))
+        (early, late), (at_early, at_late) = in_time(all_of(2 * half)), in_time(all_of(2 * halves + 2 * half))
+        inside = jnp.where(apart, 0.0, late).astype(bf16)
+        carries = jnp.where(apart, early, early + through_k * free_early * late)
+        at = jnp.where(apart, at_late, at_late + through_k * free_late * at_early)
+        at_early = at_early.astype(bf16)
+        of_k = [
+            lax.dot_general(
+                at_early[:, j * F : (j + 1) * F],
+                inside[:, j * F : (j + 1) * F],
+                (((0,), (0,)), ((), ())),
+                preferred_element_type=f32,
+            )
+            for j in range(per)
+        ]
+        total = jnp.sum(in_ref[:, half * part : (half + 1) * part, :].astype(f32), axis=0)
+        total = (total - jnp.concatenate(of_k, axis=1)).astype(bf16)
         for quad in range(quads):
             here = slice(quad * rows, (quad + 1) * rows)
-            beside = [at[:, j * F + quad * rows : j * F + (quad + 1) * rows] for j in range(at.shape[1] // F)]
-            beside += [free[:, :rows], both[:, :rows], joined]
+            beside = [at[:, j * F + quad * rows : j * F + (quad + 1) * rows] for j in range(per)]
+            beside += [(free_early * free_late)[:, :rows], both[:count, :rows], joined[:count]]
+            rest = [joined[count:], jnp.zeros((num_k - count, F), f32)]
+            beside = [carries, jnp.concatenate(beside, axis=1), jnp.concatenate(rest, axis=1)]
             out_ref[half * quads + quad, :rows, :] = total[here]
-            out_ref[half * quads + quad, rows : rows + 16, :] = carries
-            out_ref[half * quads + quad, rows + 16 :, :] = jnp.concatenate(beside, axis=1).astype(bf16)
+            out_ref[half * quads + quad, rows:, :] = jnp.concatenate(beside, axis=0).astype(bf16)
 
 
 def final_kernel(norm, rate_ref, open_ref, g_ref, gl_ref, partner_ref, x_ref, out_hbm, y_hbm, out_ref, y_ref, sems):
@@ -294,8 +318,8 @@
     (_, iy), (_, ix) = own_place("y"), own_place("x")
 
     def pair(n):
-        block = x_ref[n * places + iy * 2 + ix, rows + 16 :, :].astype(f32)
-        return block[:, F:], block[:, F - 32 : F - 31]
+        block = x_ref[n * places + iy * 2 + ix, rows:, :].astype(f32)
+        return jnp.concatenate([block[8:16, F:], block[16:, :F]], axis=0), block[8:9, F - 32 : F - 31]
 
     through = jnp.exp(steps * rate_ref[:num_k, :])
     later = jnp.where((core == 1) & (pz == 0), pair(0)[0], 0.0)
@@ -316,26 +340,21 @@
             copies.append(pltpu.make_async_copy(out_ref.at[:, at], out_hbm.at[:, at], sems.at[len(copies)]))
             copies[-1].start()
 
-    def cube_of(z):
-        if z % 2:
-            other = jnp.where(pz == 1, (z - 1) // 2, (z + 1) // 2)
-        else:
-            other = jnp.where(pz == 1, (z // 2 + nz // 2 - 1) % (nz // 2), z // 2)
-        return jnp.where(core == 0, z // 2, other) % (nz // 2)
-
-    def units(z, first):
-        n, top = cube_of(z), first + z % 2 * 8
-        return jnp.concatenate([x_ref[n * places + p, top : top + 8, :].astype(f32) for p in range(places)], axis=0)
+    def units(n):
+        blocks = [x_ref[n * places + p, rows:, :].astype(f32) for p in range(places)]
+        return [jnp.concatenate([block[top : top + 8] for block in blocks], axis=0) for top in (0, 8)]
 
     k = [rate_ref[pl.ds(z_here * per + j, 1), :] for j in range(per)]
-    through = jnp.exp(steps * jnp.concatenate(k, axis=1))
-    later = jnp.zeros((8 * places, cols), f32)
+    through = jnp.exp(2 * steps * jnp.concatenate(k, axis=1))
+    order = [(2, 1, 0, 3)[i] for i in range(nz // 2)]
+    order = [jnp.where(core == 0, 3 - i, (n + 1 - pz) % (nz // 2)) for i, n in enumerate(order)]
+    later = jnp.where(core == 0, 0.0, units(order[-1])[0])
     h, at = [], []
-    for z in range(nz - 1, -1, -1):
-        beside = units(z, rows + 16)
+    for n in order:
+        carry, beside = units(n)
         h.append(later)
         at.append(beside[:, :F])
-        later = units(z, rows) + through * beside[:, per * rows : per * rows + 1] * later
+        later = carry + through * beside[:, per * rows : per * rows + 1] * later
     h = jnp.concatenate(h, axis=0).astype(bf16)
     at = jnp.concatenate(at, axis=0).astype(bf16)
     part = lax.dot_general(at, h, (((0,), (0,)), ((), ())), preferred_element_type=f32)
@@ -466,7 +485,7 @@
         functools.partial(cube_kernel, half, quads, rows, steps),
         in_specs=[VMEM] * 2,
         out_specs=[VMEM] * 2,
-        out_shape=[shape((half * quads, rows + 32, cols), bf16), shape((num_k + 8, F), f32)],
+        out_shape=[shape((half * quads, rows + 24, cols), bf16), shape((num_k + 8, F), f32)],
         compiler_params=params(12),
         name="sum_cube",
     )(rates, grad)

time: 61.7 us -> 60.3 us (0.977)
  blocking collectives: 47.3 us -> 45.9 us
    all_to_all x1, blocking collectives: 17.9 us -> 16.5 us  [body(): grad = lax.all_to_all(grad, AXES, 0, 0, axis_index_groups=alike())]
where the time goes in v7:
time: 60.3 us; the launch traced here: 60 us
  blocking collectives  45.9 us (76%)
  Pallas kernels  8.91 us (15%)
  starting transfers between devices  3.44 us (6%)
  waiting for transfers between devices  1.13 us (2%)
  between operations  0.67 us (1%)
    all_to_all x1, blocking collectives, body(): grad = lax.all_to_all(grad, AXES, 0, 0, axis_index_groups=cubes())  29.4 us
    all_to_all x1, blocking collectives, body(): grad = lax.all_to_all(grad, AXES, 0, 0, axis_index_groups=alike())  16.5 us
    ppermute x1, starting transfers between devices, body(): resid_other = lax.ppermute(resid, 'c', swap)  3.33 us
    pallas_call x1, Pallas kernels, body(): pl.pallas_call(local_kernel, in_specs=[HBM] * 6, out_specs=[VMEM] * 10, o...  3.18 us
    pallas_call x1, Pallas kernels, body(): pl.pallas_call(functools.partial(final_kernel, norm), in_specs=[VMEM] * 6...  2.04 us
    pallas_call x1, Pallas kernels, body(): pl.pallas_call(rest_kernel, in_specs=[VMEM] * 6, out_specs=[VMEM] * 2, ou...  1.59 us
  transfers between devices with their start and end apart: 2, of which 2 were waited for; matrix products, arithmetic and copies ran while one was open for 0% of the time, Pallas kernels for 4%

profile of v7, /device:TPU:1, one launch (start us, length us, event | category | flops | bytes accessed | tf_op | source)
XLA Modules:
  0.0 60.0 jit_solution(18288283315443640152)
XLA Ops:
  0.6 3.2 %local.1 = (bf16[256,1792]{1,0:T(8,128)(2,1)S(1)}, bf16[512,256]{1,0:T(8,128)(2,1)S(1)}, f32[256,1024]{1,0:T(8,128)S(1)}, f32[24,128]{1,0:T(8,128)S(1)}, f32[256...) custom-call(f32[16]{0:T(128)} %hg_hbm.1, ...), custom_call_target="tpu_custom_call" | custom-call | tf_op jit(solution)/shard_map/local/pallas_call | solution.py:424
  3.8 3.3 %collective-permute-start = (bf16[256,1792]{1,0:T(8,128)(2,1)S(1)}, bf16[256,1792]{1,0:T(8,128)(2,1)S(1)}, u32[]{:S(2)}, u32[]{:S(2)}) collective-permute-start(bf16[256,1792]{1,0:T(8,128)(2,1)S(1)} %get-tuple-element.31.r_ref), channel_id=1, source_target_pairs={{0,1},{1,0},{2,3},{3,2},{4,5},{5,4},{6,7},{7,6},{8,9},{9,8},{10,11... | collective-permute-start | bytes 2752520 | tf_op jit(solution)/shard_map/ppermute | solution.py:454
  7.1 1.6 %rest.1 = (bf16[256,1152]{1,0:T(8,128)(2,1)S(1)}, f32[256,1024]{1,0:T(8,128)S(1)}) custom-call(bf16[256,1024]{1,0:T(8,128)(2,1)S(1)} %get-tuple-element.24.s_ref, bf16[1024,1024]{1,0:T(8,128)(2,1)S(1)} %get-tuple-element.25.w_ref, f32[256,128]{1,0:T(8,128)S(1)} %get-tuple-element.26.f_ref, bf16[256,256]{1,0:T(8,128)(2,1)S(1)} %get-tuple-element.27.mask_ref, ...), custom_call_target="tpu_custom_call" | custom-call | flops 1073741824 | bytes 6291456 | tf_op jit(solution)/shard_map/rest/pallas_call | solution.py:455
  8.7 0.1 collective-permute-start.1
  8.9 0.4 collective-permute-done.ro_ref
  9.2 0.8 %early.1 = (bf16[4,512,256]{2,1,0:T(8,128)(2,1)S(1)}, bf16[512,256]{1,0:T(8,128)(2,1)S(1)}, f32[128,512]{1,0:T(8,128)S(1)}) custom-call(bf16[512,256]{1,0:T(8,128)(2,1)S(1)} %get-tuple-element.30.st_ref, bf16[256,1792]{1,0:T(8,128)(2,1)S(1)} %get-tuple-element.31.r_ref, bf16[256,1792]{1,0:T(8,128)(2,1)S(1)} %collective-permute-done.ro_ref), custom_call_target="tpu_custom_call" | custom-call | flops 536870912 | bytes 4194304 | tf_op jit(solution)/shard_map/early/pallas_call | solution.py:466
  10.1 0.7 %collective-permute-done.1.rlo_ref = bf16[256,1152]{1,0:T(8,128)(2,1)S(1)} collective-permute-done((bf16[256,1152]{1,0:T(8,128)(2,1)S(1)}, bf16[256,1152]{1,0:T(8,128)(2,1)S(1)}, u32[]{:S(2)}, u32[]{:S(2)}) %collective-permute-start.1) | collective-permute-done | bytes 589856 | tf_op jit(solution)/shard_map/ppermute | solution.py:464
  10.8 0.8 %grad.1 = bf16[8,544,256]{2,1,0:T(8,128)(2,1)S(1)} custom-call(bf16[512,256]{1,0:T(8,128)(2,1)S(1)} %get-tuple-element.30.st_ref, bf16[512,256]{1,0:T(8,128)(2,1)S(1)} %get-tuple-element.32.sto_ref, bf16[256,1792]{1,0:T(8,128)(2,1)S(1)} %get-tuple-element.31.r_ref, bf16[256,1792]{1,0:T(8,128)(2,1)S(1)} %collective-permute-done.ro_ref, ...), custom_call_target="tpu_custom_call" | custom-call | tf_op jit(solution)/shard_map/grad/pallas_call | solution.py:475
  11.7 29.4 %all_to_all.10.in_ref = bf16[8,544,256]{2,1,0:T(8,128)(2,1)S(1)} all-to-all(bf16[8,544,256]{2,1,0:T(8,128)(2,1)S(1)} %grad.1), channel_id=1, replica_groups={{0,2,8,10,32,34,40,42},{6,4,14,12,38,36,46,44},{24,26,16,18,56,58,48,50..., dimensions={0} | all-to-all | bytes 4456448 | tf_op jit(solution)/shard_map/all_to_all | solution.py:483
  41.0 0.4 sum_cube.1
  41.5 16.5 %all_to_all.11.x_ref = bf16[16,56,256]{2,1,0:T(8,128)(2,1)S(1)} all-to-all(bf16[16,56,256]{2,1,0:T(8,128)(2,1)S(1)} %get-tuple-element.37), channel_id=1, replica_groups={{0,6,24,30,64,70,88,94,128,134,152,158,192,198,216,222},{2,4,26,28,66,6..., dimensions={0} | all-to-all | bytes 917504 | tf_op jit(solution)/shard_map/all_to_all | solution.py:492
  58.0 2.0 %final.1 = (bf16[256,2048]{1,0:T(8,128)(2,1)}, f32[32,256]{1,0:T(8,128)}) custom-call(f32[24,128]{1,0:T(8,128)S(1)} %get-tuple-element.21.rate_ref, f32[256,128]{1,0:T(8,128)S(1)} %get-tuple-element.22.open_ref, f32[256,1024]{1,0:T(8,128)S(1)} %get-tuple-element.23.g_ref, f32[256,1024]{1,0:T(8,128)S(1)} %get-tuple-element.29.gl_ref, ...), custom_call_target="tpu_custom_call" | custom-call | tf_op jit(solution)/shard_map/final/pallas_call | solution.py:494
Async XLA Ops:
  3.8 5.4 %collective-permute-start = (bf16[256,1792]{1,0:T(8,128)(2,1)S(1)}, bf16[256,1792]{1,0:T(8,128)(2,1)S(1)}, u32[]{:S(2)}, u32[]{:S(2)}) collective-permute-start(bf16[256,1792]{1,0:T(8,128)(2,1)S(1)} %get-tuple-element.31.r_ref), channel_id=1, source_target_pairs={{0,1},{1,0},{2,3},{3,2},{4,5},{5,4},{6,7},{7,6},{8,9},{9,8},{10,11... | collective-permute-start | bytes 2752520 | tf_op jit(solution)/shard_map/ppermute | solution.py:454
  8.7 2.1 %collective-permute-start.1 = (bf16[256,1152]{1,0:T(8,128)(2,1)S(1)}, bf16[256,1152]{1,0:T(8,128)(2,1)S(1)}, u32[]{:S(2)}, u32[]{:S(2)}) collective-permute-start(bf16[256,1152]{1,0:T(8,128)(2,1)S(1)} %get-tuple-element.33.rl_ref), channel_id=1, source_target_pairs={{0,1},{1,0},{2,3},{3,2},{4,5},{5,4},{6,7},{7,6},{8,9},{9,8},{10,11... | collective-permute-start | bytes 1769480 | tf_op jit(solution)/shard_map/ppermute | solution.py:464
